TPU v7x, 32 devices: a whole 2x2x4 slice. The times are simulated.
32 devices in a mesh: seq: 8 (over y, x, core), batch: 4 (over z).
Axes of the slice: x: 2, y: 2, z: 4, core: 2. Of those that a mesh axis runs over, the one named last changes fastest.
Arguments:
- incoming_activations: bfloat16 [8, 2048, 1024], P('batch', 'seq'), may hold values from -6 to 6
- wkv_preceding_entry: bfloat16 [8, 1024], P('batch'), may hold values from -6 to 6
- feedforward_preceding_entry: bfloat16 [8, 1024], P('batch'), may hold values from -6 to 6
- preceding_partition_memory: float32 [8, 16, 64, 64], P('batch'), may hold values from -18 to 18
- upstream_sensitivity: bfloat16 [8, 2048, 1024], P('batch', 'seq'), may hold values from -6 to 6
- opening_standardize_scale: bfloat16 [1024], P(('seq', 'batch')), may hold values from 0.5 to 1.5
- opening_standardize_shift: bfloat16 [1024], P(('seq', 'batch')), may hold values from -1.5 to 1.5
- wkv_lag_blends: bfloat16 [1024, 4], P(('seq', 'batch')), may hold values from 0.049804688 to 0.94921875
- accept_projection: bfloat16 [1024, 1024], P(('seq', 'batch')), may hold values from -0.1875 to 0.1875
- lookup_projection: bfloat16 [1024, 1024], P(('seq', 'batch')), may hold values from -0.1875 to 0.1875
- content_projection: bfloat16 [1024, 1024], P(('seq', 'batch')), may hold values from -0.1875 to 0.1875
- gating_projection: bfloat16 [1024, 1024], P(('seq', 'batch')), may hold values from -0.1875 to 0.1875
- logarithmic_fading_factors: bfloat16 [1024], P(('seq', 'batch')), may hold values from -9.1875 to -3
- present_entry_reward: bfloat16 [1024], P(('seq', 'batch')), may hold values from -3 to 3
- cluster_standardize_scale: bfloat16 [1024], P(('seq', 'batch')), may hold values from 0.5 to 1.5
- cluster_standardize_shift: bfloat16 [1024], P(('seq', 'batch')), may hold values from -1.5 to 1.5
- emission_projection: bfloat16 [1024, 1024], P(('seq', 'batch')), may hold values from -0.1875 to 0.1875
- closing_standardize_scale: bfloat16 [1024], P(('seq', 'batch')), may hold values from 0.5 to 1.5
- closing_standardize_shift: bfloat16 [1024], P(('seq', 'batch')), may hold values from -1.5 to 1.5
- feedforward_lag_blends: bfloat16 [1024, 2], P(('seq', 'batch')), may hold values from 0.049804688 to 0.94921875
- feedforward_lookup_projection: bfloat16 [1024, 3584], P(('seq', 'batch')), may hold values from -0.1875 to 0.1875
- feedforward_content_projection: bfloat16 [3584, 1024], P(('seq', 'batch')), may hold values from -0.09375 to 0.09375
- feedforward_accept_projection: bfloat16 [1024, 1024], P(('seq', 'batch')), may hold values from -0.1875 to 0.1875
Outputs:
- block_result: bfloat16 [8, 2048, 1024], P('batch', 'seq')
- argument_sensitivity: bfloat16 [8, 2048, 1024], P('batch', 'seq')
- opening_standardize_scale_sens: float32 [1024], P(('seq', 'batch'))
- opening_standardize_shift_sens: float32 [1024], P(('seq', 'batch'))
- wkv_blend_cotangent: float32 [1024, 4], P(('seq', 'batch'))
- accept_projection_sens: float32 [1024, 1024], P(('seq', 'batch'))
- lookup_projection_sens: float32 [1024, 1024], P(('seq', 'batch'))
- content_projection_sens: float32 [1024, 1024], P(('seq', 'batch'))
- gating_projection_sens: float32 [1024, 1024], P(('seq', 'batch'))
- logarithmic_fading_sens: float32 [1024], P(('seq', 'batch'))
- sequence_reward_sens: float32 [1024], P(('seq', 'batch'))
- cluster_standardize_scale_sens: float32 [1024], P(('seq', 'batch'))
- cluster_standardize_shift_sens: float32 [1024], P(('seq', 'batch'))
- emission_projection_sens: float32 [1024, 1024], P(('seq', 'batch'))
- closing_standardize_scale_sens: float32 [1024], P(('seq', 'batch'))
- closing_standardize_shift_sens: float32 [1024], P(('seq', 'batch'))
- feedforward_blend_cotangent: float32 [1024, 2], P(('seq', 'batch'))
- feedforward_lookup_cotangent: float32 [1024, 3584], P(('seq', 'batch'))
- feedforward_content_cotangent: float32 [3584, 1024], P(('seq', 'batch'))
- feedforward_accept_cotangent: float32 [1024, 1024], P(('seq', 'batch'))
All inputs are finite; a program needn't handle non-finite values.
Results may differ from a plain program's by a relative error of at most 0.014.
The roundings to bfloat16 on the way count: a program that leaves them out, or rounds other values in their place, can miss the bound.
Values may be sent and summed in bfloat16 or wider, within the bound.
A program may use at most 320 MiB of HBM per device.

v0:
```python
import jax
import jax.numpy as jnp
from jax import lax
from jax.sharding import PartitionSpec as P

WKV_PARTITIONS = 16
SUBSPACE_EXTENT = 64
CH = 64


def shifted(block, axis, distance):
    devices = range(lax.axis_size(axis))
    route = [(i - distance, i) for i in devices if i - distance in devices]
    return lax.ppermute(block, axis, route)


def layer_norm(matrix, norm_gain, norm_bias, epsilon):
    center = matrix - jnp.mean(matrix, axis=-1, keepdims=True)
    spread = jnp.mean(center * center, axis=-1, keepdims=True)
    return center * lax.rsqrt(spread + epsilon) * norm_gain + norm_bias


def norm_rows(matrix, norm_gain, norm_bias):
    return layer_norm(matrix, norm_gain, norm_bias, 1e-05)


def mix_states(earlier, latter):
    decay_first, state_first = earlier
    decay_second, state_second = latter
    return (decay_first * decay_second, decay_second[..., None] * state_first + state_second)


def linear_scan_routine(
    accept_quantity,
    lookup_entries,
    content_entries,
    feature_fading_factor,
    reward_entries,
    starting_memory,
):
    head_count, length, head_width = accept_quantity.shape
    blocks = length // CH
    shaped = (head_count, blocks, CH, head_width)
    accept_single_entries = accept_quantity.reshape(shaped)
    lookup_single_entries = lookup_entries.reshape(shaped)
    value_b = content_entries.reshape(shaped)
    offsets = jnp.arange(CH, dtype=jnp.float32)[:, None]
    rates = feature_fading_factor[:, None, None, :]
    recept_dec = accept_single_entries * jnp.exp(-rates * offsets)
    key_up = lookup_single_entries * jnp.exp(rates * (offsets + 1.0))
    key_end = lookup_single_entries * jnp.exp(-rates * (CH - 1.0 - offsets))
    scores = jnp.einsum("hnti,hnsi->hnts", recept_dec, key_up, precision=lax.Precision.HIGHEST)
    earlier_mask = jnp.arange(CH)[:, None] > jnp.arange(CH)[None, :]
    scores = jnp.where(earlier_mask, scores, 0.0)
    selfpair_contribution = jnp.sum(
        accept_single_entries * reward_entries[:, None, None, :] * lookup_single_entries, axis=-1
    )
    inside = (
        jnp.einsum("hnts,hnsj->hntj", scores, value_b, precision=lax.Precision.HIGHEST)
        + selfpair_contribution[..., None] * value_b
    )
    own_states = jnp.einsum("hnsi,hnsj->hnij", key_end, value_b, precision=lax.Precision.HIGHEST)
    block_decay = jnp.exp(-feature_fading_factor * CH)
    own_states = own_states.at[:, 0].add(block_decay[:, :, None] * starting_memory)
    decays = jnp.broadcast_to(block_decay[:, None, :], (head_count, blocks, head_width))
    products, states = lax.associative_scan(mix_states, (decays, own_states), axis=1)
    begins = jnp.concatenate([starting_memory[:, None], states[:, :-1]], axis=1)
    across = jnp.einsum("hnti,hnij->hntj", recept_dec, begins, precision=lax.Precision.HIGHEST)
    return ((inside + across).reshape(head_count, length, head_width), states[:, -1])


def divide_partitions(flat_rows, head_count):
    return flat_rows.reshape(flat_rows.shape[0], head_count, SUBSPACE_EXTENT).transpose(1, 0, 2)


def from_heads(stacked):
    return stacked.transpose(1, 0, 2).reshape(stacked.shape[1], stacked.shape[0] * stacked.shape[2])


def shift_mix(normed, before, mix_table):
    return tuple(
        (
            normed * mix_table[:, column] + before * (1.0 - mix_table[:, column])
            for column in range(mix_table.shape[1])
        )
    )


def group_gate(wkv_rows, gate_pre, cluster_standardize_scale, cluster_standardize_shift):
    length = wkv_rows.shape[0]
    normalized = layer_norm(
        wkv_rows.reshape(length, WKV_PARTITIONS, SUBSPACE_EXTENT),
        cluster_standardize_scale.reshape(WKV_PARTITIONS, SUBSPACE_EXTENT),
        cluster_standardize_shift.reshape(WKV_PARTITIONS, SUBSPACE_EXTENT),
        0.00064,
    )
    return normalized.reshape(length, WKV_PARTITIONS * SUBSPACE_EXTENT) * jax.nn.silu(gate_pre)


def squared(key_pre):
    return jnp.square(jax.nn.relu(key_pre))


def channel_out(carried, recv_pre):
    return jax.nn.sigmoid(recv_pre) * carried


def project(rows, linear_coefficients):
    return jnp.dot(rows, linear_coefficients, preferred_element_type=jnp.float32)


def outer(left_side, right_side):
    return lax.dot_general(
        left_side, right_side, (((0,), (0,)), ((), ())), preferred_element_type=jnp.float32
    )


def back_through(grads, linear_coefficients):
    return lax.dot_general(
        grads, linear_coefficients, (((1,), (1,)), ((), ())), preferred_element_type=jnp.float32
    )


def local(
    incoming_activations,
    wkv_preceding_entry,
    feedforward_preceding_entry,
    preceding_partition_memory,
    upstream_sensitivity,
    opening_standardize_scale,
    opening_standardize_shift,
    wkv_lag_blends,
    accept_projection,
    lookup_projection,
    content_projection,
    gating_projection,
    logarithmic_fading_factors,
    present_entry_reward,
    cluster_standardize_scale,
    cluster_standardize_shift,
    emission_projection,
    closing_standardize_scale,
    closing_standardize_shift,
    feedforward_lag_blends,
    feedforward_lookup_projection,
    feedforward_content_projection,
    feedforward_accept_projection,
):
    shards = (
        opening_standardize_scale,
        opening_standardize_shift,
        wkv_lag_blends,
        accept_projection,
        lookup_projection,
        content_projection,
        gating_projection,
        logarithmic_fading_factors,
        present_entry_reward,
        cluster_standardize_scale,
        cluster_standardize_shift,
        emission_projection,
        closing_standardize_scale,
        closing_standardize_shift,
        feedforward_lag_blends,
        feedforward_lookup_projection,
        feedforward_content_projection,
        feedforward_accept_projection,
    )
    ranks = lax.axis_size(("seq", "batch"))
    cumulative_sums = [
        jnp.zeros((shard.shape[0] * ranks,) + shard.shape[1:], jnp.float32) for shard in shards
    ]
    is_first = lax.axis_index("seq") == 0
    resident_partitions = WKV_PARTITIONS // lax.axis_size("seq")
    partition_start = lax.axis_index("seq") * resident_partitions
    outputs = []
    in_grads = []
    micro_count = incoming_activations.shape[0]
    for micro_idx in range(micro_count):
        gathered = (
            lax.all_gather(shards[0], ("seq", "batch"), axis=0, tiled=True),
            lax.all_gather(shards[1], ("seq", "batch"), axis=0, tiled=True),
            lax.all_gather(shards[2], ("seq", "batch"), axis=0, tiled=True),
            lax.all_gather(shards[3], ("seq", "batch"), axis=0, tiled=True),
            lax.all_gather(shards[4], ("seq", "batch"), axis=0, tiled=True),
            lax.all_gather(shards[5], ("seq", "batch"), axis=0, tiled=True),
            lax.all_gather(shards[6], ("seq", "batch"), axis=0, tiled=True),
            lax.all_gather(shards[7], ("seq", "batch"), axis=0, tiled=True),
            lax.all_gather(shards[8], ("seq", "batch"), axis=0, tiled=True),
            lax.all_gather(shards[9], ("seq", "batch"), axis=0, tiled=True),
            lax.all_gather(shards[10], ("seq", "batch"), axis=0, tiled=True),
            lax.all_gather(shards[11], ("seq", "batch"), axis=0, tiled=True),
            lax.all_gather(shards[12], ("seq", "batch"), axis=0, tiled=True),
            lax.all_gather(shards[13], ("seq", "batch"), axis=0, tiled=True),
            lax.all_gather(shards[14], ("seq", "batch"), axis=0, tiled=True),
            lax.all_gather(shards[15], ("seq", "batch"), axis=0, tiled=True),
            lax.all_gather(shards[16], ("seq", "batch"), axis=0, tiled=True),
            lax.all_gather(shards[17], ("seq", "batch"), axis=0, tiled=True),
        )
        (
            full_ln1_gain,
            full_ln1_bias,
            full_att_mix,
            full_w_recept,
            full_w_key,
            full_w_value,
            full_w_gate,
            full_decay_log,
            whole_reward_vector,
            full_gn_gain,
            full_gn_bias,
            full_w_out,
            full_ln2_gain,
            full_ln2_bias,
            full_ffn_mix,
            full_ffn_key,
            full_ffn_value,
            full_ffn_recept,
        ) = gathered
        current = incoming_activations[micro_idx].astype(jnp.float32)
        normed, norm_pull = jax.vjp(
            norm_rows, current, full_ln1_gain.astype(jnp.float32), full_ln1_bias.astype(jnp.float32)
        )
        arrived = shifted(normed[-1:], "seq", 1)
        previous = jnp.where(
            is_first, wkv_preceding_entry[micro_idx][None, :].astype(jnp.float32), arrived
        )
        before = jnp.concatenate([previous, normed[:-1]], axis=0)
        mixed, mix_pull = jax.vjp(shift_mix, normed, before, full_att_mix.astype(jnp.float32))
        mixed_low = tuple((piece_rows.astype(jnp.bfloat16) for piece_rows in mixed))
        accept_quantity = project(mixed_low[0], full_w_recept).astype(jnp.bfloat16)
        lookup_entries = project(mixed_low[1], full_w_key).astype(jnp.bfloat16)
        content_entries = project(mixed_low[2], full_w_value).astype(jnp.bfloat16)
        gate_pre = project(mixed_low[3], full_w_gate)
        decay_f = full_decay_log.astype(jnp.float32)
        reward_single = whole_reward_vector.astype(jnp.float32)
        head_r, head_k, head_v = (
            lax.all_to_all(accept_quantity, "seq", split_axis=1, concat_axis=0, tiled=True),
            lax.all_to_all(lookup_entries, "seq", split_axis=1, concat_axis=0, tiled=True),
            lax.all_to_all(content_entries, "seq", split_axis=1, concat_axis=0, tiled=True),
        )
        starting_memory = lax.dynamic_slice_in_dim(
            preceding_partition_memory[micro_idx], partition_start, resident_partitions, 0
        )

        def evaluate_per_part(
            accept_argument, lookup_argument, content_argument, fading_argument, reward_argument
        ):
            feature_fading_factor = lax.dynamic_slice_in_dim(
                jnp.exp(fading_argument).reshape(WKV_PARTITIONS, SUBSPACE_EXTENT),
                partition_start,
                resident_partitions,
                0,
            )
            reward_entries = lax.dynamic_slice_in_dim(
                reward_argument.reshape(WKV_PARTITIONS, SUBSPACE_EXTENT),
                partition_start,
                resident_partitions,
                0,
            )
            blended_result, discarded_quantity = linear_scan_routine(
                divide_partitions(accept_argument, resident_partitions),
                divide_partitions(lookup_argument, resident_partitions),
                divide_partitions(content_argument, resident_partitions),
                feature_fading_factor,
                reward_entries,
                starting_memory,
            )
            return from_heads(blended_result)

        wkv_heads, weighted_value_pullback = jax.vjp(
            evaluate_per_part,
            head_r.astype(jnp.float32),
            head_k.astype(jnp.float32),
            head_v.astype(jnp.float32),
            decay_f,
            reward_single,
        )
        wkv_low = lax.all_to_all(
            wkv_heads.astype(jnp.bfloat16), "seq", split_axis=0, concat_axis=1, tiled=True
        )
        attended, post_pull = jax.vjp(
            group_gate,
            wkv_low.astype(jnp.float32),
            gate_pre,
            full_gn_gain.astype(jnp.float32),
            full_gn_bias.astype(jnp.float32),
        )
        attended_low = attended.astype(jnp.bfloat16)
        middle = current + project(attended_low, full_w_out)
        normed2, norm2_pull = jax.vjp(
            norm_rows, middle, full_ln2_gain.astype(jnp.float32), full_ln2_bias.astype(jnp.float32)
        )
        arrived2 = shifted(normed2[-1:], "seq", 1)
        previous2 = jnp.where(
            is_first, feedforward_preceding_entry[micro_idx][None, :].astype(jnp.float32), arrived2
        )
        before2 = jnp.concatenate([previous2, normed2[:-1]], axis=0)
        mixed2, mix2_pull = jax.vjp(shift_mix, normed2, before2, full_ffn_mix.astype(jnp.float32))
        key_low = mixed2[0].astype(jnp.bfloat16)
        recv_low = mixed2[1].astype(jnp.bfloat16)
        key_pre = project(key_low, full_ffn_key)
        hidden, hidden_pull = jax.vjp(squared, key_pre)
        hidden_low = hidden.astype(jnp.bfloat16)
        carried = project(hidden_low, full_ffn_value)
        recv_pre = project(recv_low, full_ffn_recept)
        branch_two, tail_pull = jax.vjp(channel_out, carried, recv_pre)
        outputs.append((middle + branch_two).astype(jnp.bfloat16))
        d_out = upstream_sensitivity[micro_idx].astype(jnp.float32)
        d_carried, d_recv = tail_pull(d_out)
        d_carried_low = d_carried.astype(jnp.bfloat16)
        d_recv_low = d_recv.astype(jnp.bfloat16)
        cumulative_sums[16] = cumulative_sums[16] + outer(hidden_low, d_carried_low)
        cumulative_sums[17] = cumulative_sums[17] + outer(recv_low, d_recv_low)
        (d_hidden,) = hidden_pull(back_through(d_carried_low, full_ffn_value))
        d_key_low = d_hidden.astype(jnp.bfloat16)
        cumulative_sums[15] = cumulative_sums[15] + outer(key_low, d_key_low)
        d_normed2, d_before2, d_mix2 = mix2_pull(
            (back_through(d_key_low, full_ffn_key), back_through(d_recv_low, full_ffn_recept))
        )
        cumulative_sums[14] = cumulative_sums[14] + d_mix2
        from_next2 = shifted(d_before2[:1], "seq", -1)
        d_normed2 = d_normed2 + jnp.concatenate([d_before2[1:], from_next2], axis=0)
        d_mid, d_gain2, d_bias2 = norm2_pull(d_normed2)
        cumulative_sums[12] = cumulative_sums[12] + d_gain2
        cumulative_sums[13] = cumulative_sums[13] + d_bias2
        d_middle = d_out + d_mid
        d_middle_low = d_middle.astype(jnp.bfloat16)
        cumulative_sums[11] = cumulative_sums[11] + outer(attended_low, d_middle_low)
        d_wkv, d_gate_pre, d_gn_gain, d_gn_bias = post_pull(back_through(d_middle_low, full_w_out))
        cumulative_sums[9] = cumulative_sums[9] + d_gn_gain
        cumulative_sums[10] = cumulative_sums[10] + d_gn_bias
        d_gate_low = d_gate_pre.astype(jnp.bfloat16)
        cumulative_sums[6] = cumulative_sums[6] + outer(mixed_low[3], d_gate_low)
        d_wkv_low = d_wkv.astype(jnp.bfloat16)
        heads_gradient = lax.all_to_all(d_wkv_low, "seq", split_axis=1, concat_axis=0, tiled=True)
        (
            head_receptance_gradient,
            head_key_gradient,
            head_value_gradient,
            decay_gradient,
            reward_cotangent,
        ) = weighted_value_pullback(heads_gradient.astype(jnp.float32))
        d_recept_low, d_key_rows_low, d_value_low = (
            lax.all_to_all(
                head_receptance_gradient.astype(jnp.bfloat16),
                "seq",
                split_axis=0,
                concat_axis=1,
                tiled=True,
            ),
            lax.all_to_all(
                head_key_gradient.astype(jnp.bfloat16),
                "seq",
                split_axis=0,
                concat_axis=1,
                tiled=True,
            ),
            lax.all_to_all(
                head_value_gradient.astype(jnp.bfloat16),
                "seq",
                split_axis=0,
                concat_axis=1,
                tiled=True,
            ),
        )
        cumulative_sums[7] = cumulative_sums[7] + decay_gradient
        cumulative_sums[8] = cumulative_sums[8] + reward_cotangent
        cumulative_sums[3] = cumulative_sums[3] + outer(mixed_low[0], d_recept_low)
        cumulative_sums[4] = cumulative_sums[4] + outer(mixed_low[1], d_key_rows_low)
        cumulative_sums[5] = cumulative_sums[5] + outer(mixed_low[2], d_value_low)
        d_normed, d_before, d_mix = mix_pull(
            (
                back_through(d_recept_low, full_w_recept),
                back_through(d_key_rows_low, full_w_key),
                back_through(d_value_low, full_w_value),
                back_through(d_gate_low, full_w_gate),
            )
        )
        cumulative_sums[2] = cumulative_sums[2] + d_mix
        from_next = shifted(d_before[:1], "seq", -1)
        d_normed = d_normed + jnp.concatenate([d_before[1:], from_next], axis=0)
        d_input, d_gain1, d_bias1 = norm_pull(d_normed)
        cumulative_sums[0] = cumulative_sums[0] + d_gain1
        cumulative_sums[1] = cumulative_sums[1] + d_bias1
        in_grads.append((d_middle + d_input).astype(jnp.bfloat16))
    reduced = tuple(
        lax.psum_scatter(tuple(cumulative_sums), ("seq", "batch"), scatter_dimension=0, tiled=True)
    )
    return (jnp.stack(outputs), jnp.stack(in_grads)) + reduced


def solution(mesh):
    return jax.shard_map(
        local,
        mesh=mesh,
        in_specs=(
            P("batch", "seq", None),
            P("batch", None),
            P("batch", None),
            P("batch", None, None, None),
            P("batch", "seq", None),
            P(("seq", "batch")),
            P(("seq", "batch")),
            P(("seq", "batch"), None),
            P(("seq", "batch"), None),
            P(("seq", "batch"), None),
            P(("seq", "batch"), None),
            P(("seq", "batch"), None),
            P(("seq", "batch")),
            P(("seq", "batch")),
            P(("seq", "batch")),
            P(("seq", "batch")),
            P(("seq", "batch"), None),
            P(("seq", "batch")),
            P(("seq", "batch")),
            P(("seq", "batch"), None),
            P(("seq", "batch"), None),
            P(("seq", "batch"), None),
            P(("seq", "batch"), None),
        ),
        out_specs=(
            P("batch", "seq", None),
            P("batch", "seq", None),
            P(("seq", "batch")),
            P(("seq", "batch")),
            P(("seq", "batch"), None),
            P(("seq", "batch"), None),
            P(("seq", "batch"), None),
            P(("seq", "batch"), None),
            P(("seq", "batch"), None),
            P(("seq", "batch")),
            P(("seq", "batch")),
            P(("seq", "batch")),
            P(("seq", "batch")),
            P(("seq", "batch"), None),
            P(("seq", "batch")),
            P(("seq", "batch")),
            P(("seq", "batch"), None),
            P(("seq", "batch"), None),
            P(("seq", "batch"), None),
            P(("seq", "batch"), None),
        ),
        check_vma=False,
    )
```

profile of v0, /device:TPU:0, one launch (start us, length us, event | category | flops | bytes accessed | tf_op | source)
XLA Modules:
  0.0 2970.9 jit_solution(13763989634842645353)
XLA Ops:
  18.7 42.4 %all-reduce.133 = (bf16[1024]{0:T(1024)(128)(2,1)S(1)}, bf16[1024]{0:T(1024)(128)(2,1)S(1)}, bf16[1024]{0:T(1024)(128)(2,1)S(1)}, bf16[1024]{0:T(1024)(128)(2,1)...) all-reduce(bf16[1024]{0:T(1024)(128)(2,1)S(1)} %dynamic-update-slic, ...), channel_id=1, replica_groups=mesh['seq'=8,'batch'=4] {'seq','batch'}, use_global_device_ids=true, to_apply=%add.117 | all-reduce | flops 8192 | bytes 32768
  73.8 64.5 %all-gather.1 = bf16[32,32,2]{1,2,0:T(2,128)(2,1)S(1)} all-gather(bf16[1,32,2]{1,2,0:T(2,128)(2,1)S(1)} %bitcast.664), channel_id=1, replica_groups=mesh['seq'=8,'batch'=4] {'seq','batch'}, dimensions={0}, use_global_device_ids=true | all-gather | bytes 4224 | tf_op jit(solution)/shard_map/all_gather | solution.py:195
  139.6 64.4 %all-gather = bf16[32,32,4]{1,2,0:T(4,128)(2,1)S(1)} all-gather(bf16[1,32,4]{1,2,0:T(4,128)(2,1)S(1)} %bitcast.663), channel_id=1, replica_groups=mesh['seq'=8,'batch'=4] {'seq','batch'}, dimensions={0}, use_global_device_ids=true | all-gather | bytes 8448 | tf_op jit(solution)/shard_map/all_gather | solution.py:183
  444.3 16.7 pad.984
  466.5 16.6 pad.624
  506.4 16.7 pad.985
  525.4 16.6 pad.622
  918.9 16.7 pad.520
  935.6 16.7 pad.488
  952.3 16.7 pad.521
  969.0 16.0 pad.491
  1017.9 16.7 pad.489
  1034.6 15.8 pad.459
  1242.9 54.5 %reduce-scatter.33.cloned.1.call-done = f32[32,2]{1,0:T(8,128)} async-done(((f32[1024,2]{1,0:T(8,128)}), f32[32,2]{1,0:T(8,128)}) %reduce-scatter.33.cloned.1.call-update) | async-done | bytes 272
  1314.3 37.7 %all-reduce.132 = (f32[1024]{0:T(1024)S(1)}, f32[1024]{0:T(1024)S(1)}, f32[1024]{0:T(1024)S(1)}, f32[1024]{0:T(1024)S(1)}, f32[1024]{0:T(1024)S(1)}, /*index=5*/...) all-reduce(f32[1024]{0:T(1024)S(1)} %add.756, ...), channel_id=2, replica_groups=mesh['seq'=8,'batch'=4] {'seq','batch'}, use_global_device_ids=true, to_apply=%region_30.31.clone | all-reduce | flops 8192 | bytes 65536
  1362.2 68.0 %reduce-scatter.31.cloned.1.call-done = f32[32,4]{1,0:T(8,128)} async-done(((f32[1024,4]{1,0:T(8,128)}), f32[32,4]{1,0:T(8,128)}) %reduce-scatter.31.cloned.1.call-update) | async-done | bytes 528
  1431.5 145.5 %reduce-scatter.29.cloned.1.call-done = f32[32,1024]{1,0:T(8,128)} async-done(((f32[1024,1024]{1,0:T(8,128)}), f32[32,1024]{1,0:T(8,128)}) %reduce-scatter.29.cloned.1.call-update) | async-done | bytes 131088 | tf_op jit(solution)/shard_map/reduce_scatter | solution.py:388
  1577.0 148.9 %reduce-scatter.21.cloned.1.call-done = f32[32,1024]{1,0:T(8,128)} async-done(((f32[1024,1024]{1,0:T(8,128)}), f32[32,1024]{1,0:T(8,128)}) %reduce-scatter.21.cloned.1.call-update) | async-done | bytes 131088 | tf_op jit(solution)/shard_map/reduce_scatter | solution.py:388
  1725.9 149.6 %reduce-scatter.23.cloned.1.call-done = f32[32,1024]{1,0:T(8,128)} async-done(((f32[1024,1024]{1,0:T(8,128)}), f32[32,1024]{1,0:T(8,128)}) %reduce-scatter.23.cloned.1.call-update) | async-done | bytes 131088 | tf_op jit(solution)/shard_map/reduce_scatter | solution.py:388
  1875.5 149.6 %reduce-scatter.15.cloned.1.call-done = f32[32,1024]{1,0:T(8,128)} async-done(((f32[1024,1024]{1,0:T(8,128)}), f32[32,1024]{1,0:T(8,128)}) %reduce-scatter.15.cloned.1.call-update) | async-done | bytes 131088 | tf_op jit(solution)/shard_map/reduce_scatter | solution.py:388
  2025.2 148.9 %reduce-scatter.17.cloned.1.call-done = f32[32,1024]{1,0:T(8,128)} async-done(((f32[1024,1024]{1,0:T(8,128)}), f32[32,1024]{1,0:T(8,128)}) %reduce-scatter.17.cloned.1.call-update) | async-done | bytes 131088 | tf_op jit(solution)/shard_map/reduce_scatter | solution.py:388
  2174.1 149.9 %reduce-scatter.19.cloned.1.call-done = f32[32,1024]{1,0:T(8,128)} async-done(((f32[1024,1024]{1,0:T(8,128)}), f32[32,1024]{1,0:T(8,128)}) %reduce-scatter.19.cloned.1.call-update) | async-done | bytes 131088 | tf_op jit(solution)/shard_map/reduce_scatter | solution.py:388
  2323.9 318.7 %reduce-scatter.27.cloned.1.call-done = f32[112,1024]{1,0:T(8,128)} async-done(((f32[3584,1024]{1,0:T(8,128)}), f32[112,1024]{1,0:T(8,128)}) %reduce-scatter.27.cloned.1.call-update) | async-done | bytes 458768 | tf_op jit(solution)/shard_map/reduce_scatter | solution.py:388
  2642.7 321.1 %reduce-scatter.25.cloned.1.call-done = f32[32,3584]{1,0:T(8,128)} async-done(((f32[1024,3584]{1,0:T(8,128)}), f32[32,3584]{1,0:T(8,128)}) %reduce-scatter.25.cloned.1.call-update) | async-done | bytes 458768 | tf_op jit(solution)/shard_map/reduce_scatter | solution.py:388
  (1206 shorter events, 923.3 us)
Async XLA Ops:
  7.2 201.0 %all-gather.13.cloned.1.call-start = ((), (), s32[]{:S(2)}) async-start(), calls=%async_computation.27 | async-start | bytes 2162688 | tf_op jit(solution)/shard_map/all_gather | solution.py:185
  7.9 212.9 %all-gather.15.cloned.1.call-start = ((), (), s32[]{:S(2)}) async-start(), calls=%async_computation.28 | async-start | bytes 2162688 | tf_op jit(solution)/shard_map/all_gather | solution.py:186
  8.7 223.0 %all-gather.11.cloned.1.call-start = ((), (), s32[]{:S(2)}) async-start(), calls=%async_computation.26 | async-start | bytes 2162688 | tf_op jit(solution)/shard_map/all_gather | solution.py:184
  9.4 255.4 %all-gather.17.cloned.1.call-start = ((), (), s32[]{:S(2)}) async-start(), calls=%async_computation.29 | async-start | bytes 2162688 | tf_op jit(solution)/shard_map/all_gather | solution.py:187
  10.0 600.9 %all-gather.19.cloned.1.call-start = ((), (), s32[]{:S(2)}) async-start(), calls=%async_computation.30 | async-start | bytes 2162688 | tf_op jit(solution)/shard_map/all_gather | solution.py:192
  10.6 616.5 %all-gather.21.cloned.1.call-start = ((), (), s32[]{:S(2)}) async-start(), calls=%async_computation.31 | async-start | bytes 2162688 | tf_op jit(solution)/shard_map/all_gather | solution.py:198
  11.2 621.5 %all-gather.23.cloned.1.call-start = ((), (), s32[]{:S(2)}) async-start(), calls=%async_computation.32 | async-start | bytes 7569408 | tf_op jit(solution)/shard_map/all_gather | solution.py:196
  11.9 631.9 %all-gather.25.cloned.1.call-start = ((), (), s32[]{:S(2)}) async-start(), calls=%async_computation.33 | async-start | bytes 7569408 | tf_op jit(solution)/shard_map/all_gather | solution.py:197
  63.5 144.1 %collective-permute-start.2 = (f32[1,1024]{1,0:T(1,128)S(1)}, f32[1,1024]{1,0:T(1,128)S(1)}, u32[]{:S(2)}, u32[]{:S(2)}) collective-permute-start(f32[1,1024]{1,0:T(1,128)S(1)} %slice.537), channel_id=1, source_target_pairs={{0,4},{4,8},{8,12},{12,16},{16,20},{20,24},{24,28},{1,5},{5,9},{9,... | collective-permute-start | bytes 12296 | tf_op jit(solution)/shard_map/ppermute | solution.py:14
  65.3 142.3 %collective-permute-start = (f32[1,1024]{1,0:T(1,128)S(1)}, f32[1,1024]{1,0:T(1,128)S(1)}, u32[]{:S(2)}, u32[]{:S(2)}) collective-permute-start(f32[1,1024]{1,0:T(1,128)S(1)} %slice.513), channel_id=1, source_target_pairs={{0,4},{4,8},{8,12},{12,16},{16,20},{20,24},{24,28},{1,5},{5,9},{9,... | collective-permute-start | bytes 12296 | tf_op jit(solution)/shard_map/ppermute | solution.py:14
  287.8 23.6 all-to-all-start
  501.6 67.7 %all-to-all-start.7 = ((bf16[8,256,128]{1,2,0:T(8,128)(2,1)}), bf16[8,256,128]{1,2,0:T(8,128)(2,1)}, u32[]{:S(2)}, u32[]{:S(2)}) async-start(bf16[8,256,128]{1,2,0:T(8,128)(2,1)} %copy.265), calls=%async_computation.7 | async-start | bytes 1048576 | tf_op jit(solution)/shard_map/all_to_all | solution.py:279
  1007.9 66.3 %all-to-all-start.13 = ((bf16[8,256,128]{1,2,0:T(8,128)(2,1)}), bf16[8,256,128]{1,2,0:T(8,128)(2,1)}, u32[]{:S(2)}, u32[]{:S(2)}) async-start(bf16[8,256,128]{1,2,0:T(8,128)(2,1)} %copy.303), calls=%async_computation.13 | async-start | bytes 1048576 | tf_op jit(solution)/shard_map/all_to_all | solution.py:359
  1074.1 19.7 all-to-all-start.15
  1141.6 155.8 %reduce-scatter.33.cloned.1.call-start = ((), (), s32[]{:S(2)}) async-start(), calls=%async_computation.43 | async-start | bytes 540672
  1161.9 268.3 %reduce-scatter.31.cloned.1.call-start = ((), (), s32[]{:S(2)}) async-start(), calls=%async_computation.42 | async-start | bytes 540672
  1175.0 402.0 %reduce-scatter.29.cloned.1.call-start = ((), (), s32[]{:S(2)}) async-start(), calls=%async_computation.41 | async-start | bytes 4325376 | tf_op jit(solution)/shard_map/reduce_scatter | solution.py:388
  1180.1 545.9 %reduce-scatter.21.cloned.1.call-start = ((), (), s32[]{:S(2)}) async-start(), calls=%async_computation.37 | async-start | bytes 4325376 | tf_op jit(solution)/shard_map/reduce_scatter | solution.py:388
  1186.4 689.1 %reduce-scatter.23.cloned.1.call-start = ((), (), s32[]{:S(2)}) async-start(), calls=%async_computation.38 | async-start | bytes 4325376 | tf_op jit(solution)/shard_map/reduce_scatter | solution.py:388
  1191.1 834.1 %reduce-scatter.15.cloned.1.call-start = ((), (), s32[]{:S(2)}) async-start(), calls=%async_computation.34 | async-start | bytes 4325376 | tf_op jit(solution)/shard_map/reduce_scatter | solution.py:388
  1198.5 975.5 %reduce-scatter.17.cloned.1.call-start = ((), (), s32[]{:S(2)}) async-start(), calls=%async_computation.35 | async-start | bytes 4325376 | tf_op jit(solution)/shard_map/reduce_scatter | solution.py:388
  1204.5 1119.4 %reduce-scatter.19.cloned.1.call-start = ((), (), s32[]{:S(2)}) async-start(), calls=%async_computation.36 | async-start | bytes 4325376 | tf_op jit(solution)/shard_map/reduce_scatter | solution.py:388
  1210.6 1432.1 %reduce-scatter.27.cloned.1.call-start = ((), (), s32[]{:S(2)}) async-start(), calls=%async_computation.40 | async-start | bytes 15138816 | tf_op jit(solution)/shard_map/reduce_scatter | solution.py:388
  1225.8 1738.0 %reduce-scatter.25.cloned.1.call-start = ((), (), s32[]{:S(2)}) async-start(), calls=%async_computation.39 | async-start | bytes 15138816 | tf_op jit(solution)/shard_map/reduce_scatter | solution.py:388
  (341 other events, 5422.2 us)
Sparse Core Ops, SparseCore 0:
  11.0 59.6 all-gather.12
  73.6 55.3 all-gather.14
  131.9 55.3 all-gather.10
  190.0 58.5 all-gather.16
  251.4 59.8 all-gather.18
  314.0 56.7 all-gather.20
  373.7 72.4 all-gather.22
  449.0 72.1 all-gather.24
  1162.0 135.3 reduce-scatter.32
  1299.6 130.5 reduce-scatter.30
  1433.0 143.9 reduce-scatter.28
  1579.8 146.1 reduce-scatter.20
  1728.8 146.7 reduce-scatter.22
  1878.2 146.8 reduce-scatter.14
  2027.9 146.1 reduce-scatter.16
  2176.8 147.1 reduce-scatter.18
  2326.7 315.9 reduce-scatter.26
  2645.4 318.3 reduce-scatter.24
where the time goes:
time: 3020 us; the launch traced here: 2970 us
  waiting for transfers between devices  1690 us (56%)
  local copies, waits for them, and re-layouts  528 us (17%)
  matrix products  267 us (9%)
  blocking collectives  209 us (7%)
  other arithmetic  167 us (6%)
  starting transfers between devices  89.2 us (3%)
    reduce_scatter x8, waiting for transfers between devices, local(): lax.psum_scatter(tuple(cumulative_sums), ('seq', 'batch'), scatter_dimens...  1530 us
    pad x64, local copies, waits for them, and re-layouts, linear_scan_routine(): lax.associative_scan(mix_states, (decays, own_states), axis=1)  269 us
    unnamed x20, waiting for transfers between devices  127 us
    unnamed x672, local copies, waits for them, and re-layouts  86.2 us
    unnamed x2, blocking collectives  80.1 us
    all_gather x1, blocking collectives, local(): lax.all_gather(shards[14], ('seq', 'batch'), axis=0, tiled=True)  64.5 us
    all_gather x1, blocking collectives, local(): lax.all_gather(shards[2], ('seq', 'batch'), axis=0, tiled=True)  64.4 us
    dot_general x16, matrix products, project(): jnp.dot(rows, linear_coefficients, preferred_element_type=jnp.float32)  62.5 us
  transfers between devices with their start and end apart: 42, of which 20 were waited for; matrix products, arithmetic and copies ran while one was open for 21% of the time, Pallas kernels for 0%

commit v1 on v0

v1 whole, which is shorter than its diff:
```python
import functools

import jax
import jax.numpy as jnp
from jax import lax
from jax.experimental import pallas as pl
from jax.experimental.pallas import tpu as pltpu
from jax.sharding import PartitionSpec as P

WKV_PARTITIONS = 16
SUBSPACE_EXTENT = 64
LANES = 128
MESH = pl.DeviceIdType.MESH
F32 = jnp.float32
BF16 = jnp.bfloat16
VMEM_LIMIT = 60 * 1024 * 1024


class Grid:
    def __init__(self, seq, batch):
        self.seq, self.batch = seq, batch
        if seq == 8 and batch == 4:
            digits = [("y", "seq", 4, 2), ("x", "seq", 2, 2), ("c", "seq", 1, 2), ("z", "batch", 1, 4)]
        elif seq == 16 and batch == 8:
            digits = [("y", "seq", 4, 4), ("x", "seq", 1, 4), ("z", "batch", 2, 4), ("c", "batch", 1, 2)]
        else:
            digits = [("y", "seq", 1, seq), ("x", "seq", 1, 1), ("z", "batch", 1, batch), ("c", "batch", 1, 1)]
        self.order = [name for name, *_ in digits]
        self.axis = {name: axis for name, axis, *_ in digits}
        self.stride = {name: stride for name, _, stride, _ in digits}
        self.size = {name: size for name, *_, size in digits}
        self.shape = tuple(self.size[name] for name in self.order)

    def place(self):
        index = {"seq": lax.axis_index("seq"), "batch": lax.axis_index("batch")}
        return index, {
            name: (index[self.axis[name]] // self.stride[name]) % self.size[name] for name in self.order
        }

    def peer(self, index, digit, name, target):
        where = dict(index)
        axis = self.axis[name]
        where[axis] = index[axis] + (target - digit[name]) * self.stride[name]
        return (where["seq"], where["batch"])

    def at(self, ref, gone="", **fixed):
        return ref.at[tuple(fixed.get(name, slice(None)) for name in self.order if name not in gone)]

    def sizes(self, gone=""):
        return tuple(self.size[name] for name in self.order if name not in gone)


def greet(peers):
    barrier = pltpu.get_barrier_semaphore()
    for peer in peers:
        pl.semaphore_signal(barrier, inc=1, device_id=peer, device_id_type=MESH)
    pl.semaphore_wait(barrier, len(peers))


def gather_kernel(grid, orders, *refs):
    count = len(orders)
    shards, fulls = refs[:count], refs[count : 2 * count]
    own_sem, send_sem, recv_sem = refs[2 * count :]
    index, digit = grid.place()

    def others(name):
        return [(j, lax.rem(digit[name] + j, grid.size[name])) for j in range(1, grid.size[name])]

    greet([grid.peer(index, digit, name, t) for name in grid.order for _, t in others(name)])

    started = []

    def send(chunk, source, place, name):
        copies = []
        for j, target in others(name):
            slot = len(started)
            copy = pltpu.make_async_remote_copy(
                src_ref=source,
                dst_ref=place,
                send_sem=send_sem.at[slot],
                recv_sem=recv_sem.at[slot],
                device_id=grid.peer(index, digit, name, target),
                device_id_type=MESH,
            )
            copy.start()
            started.append(copy)
            copies.append(copy)
        return copies

    pending = {}
    own = {}

    def stage(chunk, number):
        full = fulls[chunk]
        first, second = orders[chunk]
        if number == 0:
            place = grid.at(full, **digit)
            copy = pltpu.make_async_copy(shards[chunk], place, own_sem.at[chunk])
            copy.start()
            own[chunk] = copy
            pending[chunk] = send(chunk, shards[chunk], place, "z")
            return
        for copy in pending[chunk]:
            copy.wait_recv()
        if number == 1:
            own[chunk].wait()
            fixed = {n: digit[n] for n in ("x", "y", "c")}
            name = first
        elif number == 2:
            fixed = {n: digit[n] for n in (second, "c")}
            name = second
        elif number == 3:
            fixed = {"c": digit["c"]}
            name = "c"
        else:
            return
        place = grid.at(full, **fixed)
        pending[chunk] = send(chunk, place, place, name)

    for chunk in range(count):
        stage(chunk, 0)
    for tick in range(count + 3):
        for number in (1, 2, 3, 4):
            chunk = tick - (number - 1)
            if 0 <= chunk < count:
                stage(chunk, number)
    for copy in started:
        copy.wait_send()


def gather_all(grid, shards, orders):
    count = len(shards)
    steps = count * sum(size - 1 for size in grid.shape)
    anywhere = pl.BlockSpec(memory_space=pl.ANY)
    return pl.pallas_call(
        functools.partial(gather_kernel, grid, orders),
        out_shape=[jax.ShapeDtypeStruct(grid.shape + s.shape, s.dtype) for s in shards],
        in_specs=[anywhere] * count,
        out_specs=[anywhere] * count,
        scratch_shapes=[
            pltpu.SemaphoreType.DMA((count,)),
            pltpu.SemaphoreType.DMA((steps,)),
            pltpu.SemaphoreType.DMA((steps,)),
        ],
        compiler_params=pltpu.CompilerParams(collective_id=0, has_side_effects=True),
    )(*shards)


def scatter_kernel(grid, chunks, *refs):
    count = len(chunks)
    parts, outs = refs[:count], refs[count : 2 * count]
    mine, rc, rx, ry, rz = (refs[2 * count + i * count : 2 * count + (i + 1) * count] for i in range(5))
    own_sem, send_sem, recv_sem = refs[7 * count :]
    index, digit = grid.place()

    def others(name):
        return [(j, lax.rem(digit[name] + j, grid.size[name])) for j in range(1, grid.size[name])]

    greet([grid.peer(index, digit, name, t) for name in grid.order for _, t in others(name)])
    started = []

    def send(source, gone, name, slots):
        copies = []
        for j, target in others(name):
            slot = len(started)
            copy = pltpu.make_async_remote_copy(
                src_ref=grid.at(source, gone, **{name: target}),
                dst_ref=slots.at[j - 1],
                send_sem=send_sem.at[slot],
                recv_sem=recv_sem.at[slot],
                device_id=grid.peer(index, digit, name, target),
                device_id_type=MESH,
            )
            copy.start()
            started.append(copy)
            copies.append(copy)
        return copies

    pending, own = {}, {}

    def total(target, terms, shape):
        steps = 1
        for size in shape:
            steps *= size

        def body(i, carry):
            where, rest = [], i
            for size in reversed(shape):
                where.append(lax.rem(rest, size))
                rest = lax.div(rest, size)
            where = tuple(reversed(where))
            value = terms[0](where).astype(F32)
            for term in terms[1:]:
                value = value + term(where).astype(F32)
            target(where, value)
            return carry

        lax.fori_loop(0, steps, body, 0)

    def picker(ref, gone, name):
        names = [n for n in grid.order if n not in gone and n != name]

        def read(where):
            at = dict(zip(names, where))
            at[name] = digit[name]
            return ref[tuple(at[n] for n in grid.order if n not in gone)]

        return read

    def slot_reader(slots, j):
        return lambda where: slots[(j,) + where]

    def stage(chunk, number):
        first, second = chunks[chunk]
        if number == 0:
            copy = pltpu.make_async_copy(grid.at(parts[chunk], c=digit["c"]), mine[chunk], own_sem.at[chunk])
            copy.start()
            own[chunk] = copy
            pending[chunk] = send(parts[chunk], "", "c", rc[chunk])
            return
        for copy in pending[chunk]:
            copy.wait_recv()
        if number == 1:
            own[chunk].wait()
            m = mine[chunk]

            def put(where, value):
                m[where] = value.astype(m.dtype)

            if grid.size["c"] > 1:
                total(put, [lambda where: m[where]] + [slot_reader(rc[chunk], j) for j in range(grid.size["c"] - 1)], grid.sizes("c"))
            pending[chunk] = send(m, "c", first, (rx if first == "x" else ry)[chunk])
        elif number == 2:
            m, slots = mine[chunk], (rx if first == "x" else ry)[chunk]

            def put(where, value):
                slots[(0,) + where] = value.astype(slots.dtype)

            total(put, [picker(m, "c", first)] + [slot_reader(slots, j) for j in range(grid.size[first] - 1)], grid.sizes("c" + first))
            pending[chunk] = send(slots.at[0], "c" + first, second, (rx if second == "x" else ry)[chunk])
        elif number == 3:
            before, slots = (rx if first == "x" else ry)[chunk].at[0], (rx if second == "x" else ry)[chunk]

            def put(where, value):
                slots[(0,) + where] = value.astype(slots.dtype)

            total(put, [picker(before, "c" + first, second)] + [slot_reader(slots, j) for j in range(grid.size[second] - 1)], grid.sizes("cxy"))
            pending[chunk] = send(slots.at[0], "cxy", "z", rz[chunk])
        elif number == 4:
            before, slots = (rx if second == "x" else ry)[chunk].at[0], rz[chunk]
            value = before[digit["z"]].astype(F32)
            for j in range(grid.size["z"] - 1):
                value = value + slots[j].astype(F32)
            outs[chunk][...] = value

    for chunk in range(count):
        stage(chunk, 0)
    for tick in range(count + 3):
        for number in (1, 2, 3, 4):
            chunk = tick - (number - 1)
            if 0 <= chunk < count:
                stage(chunk, number)
    for copy in started:
        copy.wait_send()


def scatter_all(grid, parts, chunks):
    count = len(parts)
    steps = count * sum(size - 1 for size in grid.shape)
    anywhere = pl.BlockSpec(memory_space=pl.ANY)
    mine, rc, rx, ry, rz = [], [], [], [], []
    for part, (first, second) in zip(parts, chunks):
        tile, kind = part.shape[4:], part.dtype
        mine.append(pltpu.VMEM(grid.sizes("c") + tile, kind))
        rc.append(pltpu.VMEM((max(grid.size["c"] - 1, 1),) + grid.sizes("c") + tile, kind))
        shapes = {
            first: pltpu.VMEM((max(grid.size[first] - 1, 1),) + grid.sizes("c" + first) + tile, kind),
            second: pltpu.VMEM((max(grid.size[second] - 1, 1),) + grid.sizes("cxy") + tile, kind),
        }
        rx.append(shapes["x"])
        ry.append(shapes["y"])
        rz.append(pltpu.VMEM((max(grid.size["z"] - 1, 1),) + tile, kind))
    return pl.pallas_call(
        functools.partial(scatter_kernel, grid, chunks),
        out_shape=[jax.ShapeDtypeStruct(p.shape[4:], F32) for p in parts],
        in_specs=[anywhere] * count,
        out_specs=[pl.BlockSpec(memory_space=pltpu.VMEM)] * count,
        scratch_shapes=mine + rc + rx + ry + rz + [
            pltpu.SemaphoreType.DMA((count,)),
            pltpu.SemaphoreType.DMA((steps,)),
            pltpu.SemaphoreType.DMA((steps,)),
        ],
        compiler_params=pltpu.CompilerParams(
            collective_id=1, has_side_effects=True, vmem_limit_bytes=VMEM_LIMIT
        ),
    )(*parts)


def dot(a, b, da, db):
    return lax.dot_general(a, b, (((da,), (db,)), ((), ())), preferred_element_type=F32)


PRECISE = dict(score=1, inner=1, cross=1, own=1, back=1)


def parts_of(value):
    high = value.astype(BF16)
    return high, (value - high.astype(F32)).astype(BF16)


def dot2(a, b, da, db, name):
    if not PRECISE[name]:
        return dot(a.astype(BF16), b, da, db)
    high, low = parts_of(a)
    return dot(high, b, da, db) + dot(low, b, da, db)


def dot3(a, b, da, db, name):
    if not PRECISE[name]:
        return dot(a.astype(BF16), b.astype(BF16), da, db)
    a_high, a_low = parts_of(a)
    b_high, b_low = parts_of(b)
    return dot(a_high, b_high, da, db) + (dot(a_low, b_high, da, db) + dot(a_high, b_low, da, db))


def half_masks(rows):
    lane = lax.broadcasted_iota(jnp.int32, (rows, LANES), 1)
    return lane < SUBSPACE_EXTENT


def block_ones(kind):
    row = lax.broadcasted_iota(jnp.int32, (LANES, LANES), 0) // SUBSPACE_EXTENT
    lane = lax.broadcasted_iota(jnp.int32, (LANES, LANES), 1) // SUBSPACE_EXTENT
    return (row == lane).astype(kind)


def head_sum(value, ones):
    high = value.astype(BF16)
    low = (value - high.astype(F32)).astype(BF16)
    return dot(high, ones, 1, 0) + dot(low, ones, 1, 0)


def decays(rate, length):
    step = lax.broadcasted_iota(jnp.int32, (length, LANES), 0).astype(F32)
    return jnp.exp(-rate * step), jnp.exp(rate * (step + 1.0)), jnp.exp(-rate * (length - 1.0 - step))


def fold(first, second, ones):
    pick = half_masks(LANES)
    a, b = first * ones, second * ones
    a = a + pltpu.roll(a, SUBSPACE_EXTENT, 1)
    b = b + pltpu.roll(b, SUBSPACE_EXTENT, 1)
    return jnp.where(pick, a, b)


def unfold(both, segment, ones):
    pick = half_masks(LANES)
    turned = pltpu.roll(both, SUBSPACE_EXTENT, 1)
    full = jnp.where(pick, both, turned) if segment == 0 else jnp.where(pick, turned, both)
    return full * ones


def exchange(grid, index, source, slots, rows, send_sem, recv_sem):
    me, copies = index["seq"], []
    for j in range(1, grid.seq):
        target = lax.rem(me + j, grid.seq)
        copy = pltpu.make_async_remote_copy(
            src_ref=source.at[pl.ds(pl.multiple_of(target * rows, 16), rows)],
            dst_ref=slots.at[pl.ds(pl.multiple_of(me * rows, 16), rows)],
            send_sem=send_sem.at[j - 1],
            recv_sem=recv_sem.at[j - 1],
            device_id=(target, index["batch"]),
            device_id_type=MESH,
        )
        copy.start()
        copies.append(copy)
    here = pl.ds(pl.multiple_of(me * rows, 16), rows)
    slots[here, :] = source[here, :]
    return copies


def wkv_forward_kernel(
    grid, length,
    r_ref, k_ref, v_ref, gate_ref, rate_ref, reward_ref, gain_ref, bias_ref, start_ref, fade_ref,
    wkv_ref, attended_ref, begin_ref,
    own_ref, got_ref, out_ref, inner_ref, send_a, recv_a, send_b, recv_b,
):
    index, _ = grid.place()
    me = index["seq"]
    greet([(lax.rem(me + j, grid.seq), index["batch"]) for j in range(1, grid.seq)])
    width = r_ref.shape[1]
    pairs, rows = width // LANES, width // grid.seq
    ones, ones16 = block_ones(F32), block_ones(BF16)

    def columns(p):
        return pl.ds(pl.multiple_of(p * LANES, LANES), LANES)

    def own_states(p, carry):
        _, _, end = decays(rate_ref[:, columns(p)], length)
        both = []
        for q in range(2):
            token = pl.ds(q * length, length)
            k_end = k_ref[token, columns(p)].astype(F32) * end
            both.append(dot2(k_end, v_ref[token, columns(p)], 0, 0, "own"))
        own_ref[columns(p), :] = fold(both[0], both[1], ones).astype(BF16)
        return carry

    lax.fori_loop(0, pairs, own_states, 0)
    first = exchange(grid, index, own_ref, got_ref, rows, send_a, recv_a)

    later = lax.broadcasted_iota(jnp.int32, (length, length), 0) > lax.broadcasted_iota(
        jnp.int32, (length, length), 1
    )

    def inside(p, carry):
        down, up, _ = decays(rate_ref[:, columns(p)], length)
        pick = half_masks(length)
        for q in range(2):
            token = pl.ds(q * length, length)
            r = r_ref[token, columns(p)].astype(F32)
            k = k_ref[token, columns(p)].astype(F32)
            v = v_ref[token, columns(p)]
            r_down = r * down
            k_up = k * up
            halves = []
            for h in range(2):
                r_head = jnp.where(pick == (h == 0), r_down, 0.0)
                scores = jnp.where(later, dot3(r_head, k_up, 1, 1, "score"), 0.0)
                halves.append(dot2(scores, v, 1, 0, "inner"))
            inner = jnp.where(pick, halves[0], halves[1])
            self_part = head_sum(r * reward_ref[:, columns(p)] * k, ones16)
            inner_ref[token, columns(p)] = inner + self_part * v.astype(F32)
        return carry

    lax.fori_loop(0, pairs, inside, 0)

    for copy in first:
        copy.wait_recv()
    state = start_ref[...]
    fade = fade_ref[...]
    for block in range(grid.seq):
        at = pl.ds(block * rows, rows)
        out_ref[at, :] = state.astype(BF16)
        state = fade * state + got_ref[at, :].astype(F32)
    second = exchange(grid, index, out_ref, begin_ref, rows, send_b, recv_b)
    for copy in second:
        copy.wait_recv()

    def across(p, carry):
        down, _, _ = decays(rate_ref[:, columns(p)], length)
        begin = begin_ref[columns(p), :].astype(F32)
        for q in range(2):
            token = pl.ds(q * length, length)
            r_down = r_ref[token, columns(p)].astype(F32) * down
            state16 = unfold(begin, q, ones).astype(BF16)
            y = (inner_ref[token, columns(p)] + dot2(r_down, state16, 1, 0, "cross")).astype(BF16)
            wkv_ref[token, columns(p)] = y
            center = y.astype(F32) - dot(y, ones16, 1, 0) * (1.0 / SUBSPACE_EXTENT)
            spread = head_sum(center * center, ones16) * (1.0 / SUBSPACE_EXTENT)
            z = center * lax.rsqrt(spread + 0.00064)
            normalized = z * gain_ref[:, columns(p)] + bias_ref[:, columns(p)]
            g = gate_ref[token, columns(p)]
            attended_ref[token, columns(p)] = (normalized * g / (1.0 + jnp.exp(-g))).astype(BF16)
        return carry

    lax.fori_loop(0, pairs, across, 0)
    for copy in first + second:
        copy.wait_send()


def wkv_forward(grid, r, k, v, gate_pre, rate, reward, gain, bias, start, fade):
    tokens, width = r.shape
    state = pltpu.VMEM((width, LANES), BF16)
    sems = pltpu.SemaphoreType.DMA((grid.seq - 1,))
    vmem = pl.BlockSpec(memory_space=pltpu.VMEM)
    return pl.pallas_call(
        functools.partial(wkv_forward_kernel, grid, tokens // 2),
        out_shape=[
            jax.ShapeDtypeStruct((tokens, width), BF16),
            jax.ShapeDtypeStruct((tokens, width), BF16),
            jax.ShapeDtypeStruct((width, LANES), BF16),
        ],
        in_specs=[vmem] * 10,
        out_specs=[vmem] * 3,
        scratch_shapes=[state, state, state, pltpu.VMEM((tokens, width), F32), sems, sems, sems, sems],
        compiler_params=pltpu.CompilerParams(
            collective_id=2, has_side_effects=True, vmem_limit_bytes=VMEM_LIMIT
        ),
    )(r, k, v, gate_pre, rate, reward, gain, bias, start, fade)


def wkv_backward_kernel(
    grid, length,
    r_ref, k_ref, v_ref, gate_ref, wkv_ref, d_att_ref, rate_ref, reward_ref, gain_ref, bias_ref, fade_ref, begin_ref,
    d_gate_ref, dr_ref, dk_ref, dv_ref, sums_ref,
    dy_ref, own_ref, got_ref, out_ref, end_ref, send_a, recv_a, send_b, recv_b,
):
    index, _ = grid.place()
    me = index["seq"]
    greet([(lax.rem(me + j, grid.seq), index["batch"]) for j in range(1, grid.seq)])
    width = r_ref.shape[1]
    pairs, rows = width // LANES, width // grid.seq
    ones, ones16 = block_ones(F32), block_ones(BF16)
    share = 1.0 / SUBSPACE_EXTENT

    def columns(p):
        return pl.ds(pl.multiple_of(p * LANES, LANES), LANES)

    def own_states(p, carry):
        down, _, _ = decays(rate_ref[:, columns(p)], length)
        both = []
        gain_sum, bias_sum = jnp.zeros((1, LANES), F32), jnp.zeros((1, LANES), F32)
        for q in range(2):
            token = pl.ds(q * length, length)
            y = wkv_ref[token, columns(p)]
            center = y.astype(F32) - dot(y, ones16, 1, 0) * share
            spread = head_sum(center * center, ones16) * share
            scale = lax.rsqrt(spread + 0.00064)
            z = center * scale
            gain = gain_ref[:, columns(p)]
            normalized = z * gain + bias_ref[:, columns(p)]
            g = gate_ref[token, columns(p)]
            s = 1.0 / (1.0 + jnp.exp(-g))
            d_att = d_att_ref[token, columns(p)]
            d_gate_ref[token, columns(p)] = (d_att * normalized * s * (1.0 + g * (1.0 - s))).astype(BF16)
            d_norm = d_att * g * s
            gain_sum = gain_sum + jnp.sum(d_norm * z, axis=0, keepdims=True)
            bias_sum = bias_sum + jnp.sum(d_norm, axis=0, keepdims=True)
            e = d_norm * gain
            dy = ((e - head_sum(e, ones16) * share - z * (head_sum(e * z, ones16) * share)) * scale).astype(BF16)
            dy_ref[token, columns(p)] = dy
            r_down = r_ref[token, columns(p)].astype(F32) * down
            both.append(dot2(r_down, dy, 0, 0, "own"))
        sums_ref[0:1, columns(p)] = gain_sum
        sums_ref[1:2, columns(p)] = bias_sum
        own_ref[columns(p), :] = fold(both[0], both[1], ones).astype(BF16)
        return carry

    lax.fori_loop(0, pairs, own_states, 0)
    first = exchange(grid, index, own_ref, got_ref, rows, send_a, recv_a)
    for copy in first:
        copy.wait_recv()
    fade = fade_ref[...]
    state = jnp.zeros_like(fade)
    for block in reversed(range(grid.seq)):
        at = pl.ds(block * rows, rows)
        out_ref[at, :] = state.astype(BF16)
        state = fade * state + got_ref[at, :].astype(F32)
    second = exchange(grid, index, out_ref, end_ref, rows, send_b, recv_b)
    for copy in second:
        copy.wait_recv()

    later = lax.broadcasted_iota(jnp.int32, (length, length), 0) > lax.broadcasted_iota(
        jnp.int32, (length, length), 1
    )
    step = lax.broadcasted_iota(jnp.int32, (length, LANES), 0).astype(F32)

    def inside(p, carry):
        rate = rate_ref[:, columns(p)]
        reward = reward_ref[:, columns(p)]
        down, up, end = decays(rate, length)
        pick = half_masks(length)
        begins, ends = begin_ref[columns(p), :].astype(F32), end_ref[columns(p), :].astype(F32)
        reward_sum, rate_sum = jnp.zeros((1, LANES), F32), jnp.zeros((1, LANES), F32)
        for q in range(2):
            token = pl.ds(q * length, length)
            r = r_ref[token, columns(p)].astype(F32)
            k = k_ref[token, columns(p)].astype(F32)
            v = v_ref[token, columns(p)]
            dy = dy_ref[token, columns(p)]
            begin, finish = unfold(begins, q, ones), unfold(ends, q, ones)
            begin16, finish16 = begin.astype(BF16), finish.astype(BF16)
            r_down = r * down
            k_up = k * up
            k_end = k * end
            if not PRECISE["back"]:
                r_down = r_down.astype(BF16).astype(F32)
                k_up = k_up.astype(BF16).astype(F32)
                k_end = k_end.astype(BF16).astype(F32)
            d_r, d_k, d_v = [], [], []
            for h in range(2):
                r_head = jnp.where(pick == (h == 0), r_down, 0.0)
                dy_head = jnp.where(pick == (h == 0), dy.astype(F32), 0.0).astype(BF16)
                scores = jnp.where(later, dot3(r_head, k_up, 1, 1, "score"), 0.0)
                d_scores = jnp.where(later, dot(dy_head, v, 1, 1), 0.0)
                d_r.append(dot3(d_scores, k_up, 1, 0, "back"))
                d_k.append(dot3(d_scores, r_down, 0, 0, "back"))
                d_v.append(dot2(scores, dy, 0, 0, "inner"))
            from_r = jnp.where(pick, d_r[0], d_r[1]) + dot(dy, begin16, 1, 1)
            from_k = jnp.where(pick, d_k[0], d_k[1])
            from_end = dot(v, finish16, 1, 1)
            v32, dy32 = v.astype(F32), dy.astype(F32)
            v_dy = head_sum(v32 * dy32, ones16)
            self_part = head_sum(r * reward * k, ones16)
            dr_ref[token, columns(p)] = (from_r * down + reward * k * v_dy).astype(BF16)
            dk_ref[token, columns(p)] = (from_k * up + from_end * end + reward * r * v_dy).astype(BF16)
            dv_ref[token, columns(p)] = (
                jnp.where(pick, d_v[0], d_v[1]) + dot2(k_end, finish16, 1, 0, "cross") + self_part * dy32
            ).astype(BF16)
            reward_sum = reward_sum + jnp.sum(r * k * v_dy, axis=0, keepdims=True)
            terms = (
                (step + 1.0) * k_up * from_k
                - step * r_down * from_r
                - (length - 1.0 - step) * k_end * from_end
            )
            through = lax.dot_general(
                jnp.ones((8, LANES), F32), begin * finish, (((1,), (1,)), ((), ())),
                precision=lax.Precision.HIGHEST, preferred_element_type=F32,
            )[0:1, :]
            rate_sum = rate_sum + jnp.sum(terms, axis=0, keepdims=True) - length * jnp.exp(-rate * length) * through
        sums_ref[2:3, columns(p)] = reward_sum
        sums_ref[3:4, columns(p)] = rate_sum * rate
        return carry

    lax.fori_loop(0, pairs, inside, 0)
    sums_ref[4:8, :] = jnp.zeros((4, width), F32)
    for copy in first + second:
        copy.wait_send()


def wkv_backward(grid, r, k, v, gate_pre, wkv, d_att, rate, reward, gain, bias, fade, begin):
    tokens, width = r.shape
    state = pltpu.VMEM((width, LANES), BF16)
    sems = pltpu.SemaphoreType.DMA((grid.seq - 1,))
    vmem = pl.BlockSpec(memory_space=pltpu.VMEM)
    flat = jax.ShapeDtypeStruct((tokens, width), BF16)
    return pl.pallas_call(
        functools.partial(wkv_backward_kernel, grid, tokens // 2),
        out_shape=[flat, flat, flat, flat, jax.ShapeDtypeStruct((8, width), F32)],
        in_specs=[vmem] * 12,
        out_specs=[vmem] * 5,
        scratch_shapes=[pltpu.VMEM((tokens, width), BF16), state, state, state, state, sems, sems, sems, sems],
        compiler_params=pltpu.CompilerParams(
            collective_id=3, has_side_effects=True, vmem_limit_bytes=VMEM_LIMIT
        ),
    )(r, k, v, gate_pre, wkv, d_att, rate, reward, gain, bias, fade, begin)


def shifted(block, axis, distance):
    devices = range(lax.axis_size(axis))
    route = [(i - distance, i) for i in devices if i - distance in devices]
    return lax.ppermute(block, axis, route)


def standardize(rows, epsilon):
    center = rows - jnp.mean(rows, axis=-1, keepdims=True)
    spread = jnp.mean(center * center, axis=-1, keepdims=True)
    scale = lax.rsqrt(spread + epsilon)
    return center * scale, scale


def back_standardize(e, z, scale):
    return (e - jnp.mean(e, axis=-1, keepdims=True) - z * jnp.mean(e * z, axis=-1, keepdims=True)) * scale


def project(rows, weights):
    return dot(rows, weights, 1, 0)


def outer(left_side, right_side):
    return dot(left_side, right_side, 0, 0).astype(BF16)


def back_through(grads, weights):
    return dot(grads, weights, 1, 1)


def local(grid, *args):
    (
        incoming, att_entry, ffn_entry, memory, upstream,
        ln1_gain, ln1_bias, att_mix, w_recept, w_key, w_value, w_gate, decay_log, reward,
        gn_gain, gn_bias, w_out, ln2_gain, ln2_bias, ffn_mix, f_key, f_value, f_recept,
    ) = args
    segments, length, width = incoming.shape
    tokens = segments * length
    ranks = grid.seq * grid.batch
    share = width // ranks
    is_first = lax.axis_index("seq") == 0

    small = jnp.stack(
        [ln1_gain, ln1_bias] + [att_mix[:, c] for c in range(4)] + [decay_log, reward, gn_gain, gn_bias, ln2_gain, ln2_bias]
        + [ffn_mix[:, c] for c in range(2)]
    )
    small = jnp.pad(small, ((0, 2), (0, LANES - share)))
    half = f_key.shape[1] // 2
    shards = [small, w_recept, w_key, w_value, w_gate, w_out, f_recept, f_key, f_value]
    orders = [("x", "y"), ("x", "y"), ("y", "x"), ("x", "y"), ("y", "x"), ("x", "y"), ("y", "x"), ("x", "y"), ("y", "x")]
    full = gather_all(grid, shards, orders)
    table = full[0].reshape(ranks, 16, LANES)[:, :14, :share].transpose(1, 0, 2).reshape(14, width).astype(F32)
    W_r, W_k, W_v, W_g, W_o, F_r, F_k, F_v = [
        w.reshape((ranks * w.shape[4], w.shape[5])) for w in full[1:]
    ]
    g1, b1 = table[0], table[1]
    mix1 = table[2:6]
    rate = jnp.exp(table[6])[None, :]
    bonus = table[7][None, :]
    gg, gb = table[8][None, :], table[9][None, :]
    g2, b2 = table[10], table[11]
    mix2 = table[12:14]

    x = incoming.astype(F32)
    z1, s1 = standardize(x, 1e-05)
    normed = z1 * g1 + b1
    arrived = shifted(normed[:, -1:], "seq", 1)
    previous = jnp.where(is_first, att_entry[:, None, :].astype(F32), arrived)
    before = jnp.concatenate([previous, normed[:, :-1]], axis=1)
    mixed = [
        (normed * mix1[c] + before * (1.0 - mix1[c])).astype(BF16).reshape(tokens, width) for c in range(4)
    ]
    r = project(mixed[0], W_r).astype(BF16)
    k = project(mixed[1], W_k).astype(BF16)
    v = project(mixed[2], W_v).astype(BF16)
    gate_pre = project(mixed[3], W_g)

    rows = width // grid.seq
    row = lax.axis_index("seq") * rows
    start = memory.transpose(1, 2, 0, 3).reshape(width, segments * SUBSPACE_EXTENT)
    start = lax.dynamic_slice_in_dim(start, row, rows, 0)
    own_rate = lax.dynamic_slice_in_dim(rate[0], row, rows, 0)
    fade = jnp.broadcast_to(jnp.exp(-own_rate * length)[:, None], (rows, LANES))
    wkv, attended, begin = wkv_forward(grid, r, k, v, gate_pre, rate, bonus, gg, gb, start, fade)

    middle = x.reshape(tokens, width) + project(attended, W_o)
    middle = middle.reshape(segments, length, width)
    z2, s2 = standardize(middle, 1e-05)
    normed2 = z2 * g2 + b2
    arrived2 = shifted(normed2[:, -1:], "seq", 1)
    previous2 = jnp.where(is_first, ffn_entry[:, None, :].astype(F32), arrived2)
    before2 = jnp.concatenate([previous2, normed2[:, :-1]], axis=1)
    mixed2 = [
        (normed2 * mix2[c] + before2 * (1.0 - mix2[c])).astype(BF16).reshape(tokens, width) for c in range(2)
    ]
    key_pos = jnp.maximum(project(mixed2[0], F_k), 0.0)
    hidden = (key_pos * key_pos).astype(BF16)
    carried = project(hidden, F_v)
    recv = jax.nn.sigmoid(project(mixed2[1], F_r))
    result = (middle.reshape(tokens, width) + recv * carried).astype(BF16)

    d_out = upstream.astype(F32).reshape(tokens, width)
    d_carried = (recv * d_out).astype(BF16)
    d_recv = (recv * (1.0 - recv) * carried * d_out).astype(BF16)
    grad_f_value = outer(hidden, d_carried)
    grad_f_recept = outer(mixed2[1], d_recv)
    d_key = (2.0 * key_pos * back_through(d_carried, F_v)).astype(BF16)
    grad_f_key = outer(mixed2[0], d_key)
    d_mixed2 = [
        back_through(d_key, F_k).reshape(segments, length, width),
        back_through(d_recv, F_r).reshape(segments, length, width),
    ]
    difference2 = normed2 - before2
    d_mix2 = [jnp.sum(difference2 * d, axis=(0, 1)) for d in d_mixed2]
    d_before2 = sum((1.0 - mix2[c]) * d_mixed2[c] for c in range(2))
    from_next2 = shifted(d_before2[:, :1], "seq", -1)
    d_normed2 = sum(mix2[c] * d_mixed2[c] for c in range(2)) + jnp.concatenate([d_before2[:, 1:], from_next2], axis=1)
    d_g2 = jnp.sum(z2 * d_normed2, axis=(0, 1))
    d_b2 = jnp.sum(d_normed2, axis=(0, 1))
    d_middle = d_out.reshape(segments, length, width) + back_standardize(d_normed2 * g2, z2, s2)
    d_branch = d_middle.astype(BF16).reshape(tokens, width)
    grad_out = outer(attended, d_branch)
    d_attended = back_through(d_branch, W_o)
    d_gate, d_r, d_k, d_v, sums = wkv_backward(
        grid, r, k, v, gate_pre, wkv, d_attended, rate, bonus, gg, gb, fade, begin
    )
    grad_r, grad_k, grad_v, grad_g = [
        outer(m, d) for m, d in zip(mixed, (d_r, d_k, d_v, d_gate))
    ]
    d_mixed = [
        back_through(d, w).reshape(segments, length, width)
        for d, w in zip((d_r, d_k, d_v, d_gate), (W_r, W_k, W_v, W_g))
    ]
    difference = normed - before
    d_mix1 = [jnp.sum(difference * d, axis=(0, 1)) for d in d_mixed]
    d_before = sum((1.0 - mix1[c]) * d_mixed[c] for c in range(4))
    from_next = shifted(d_before[:, :1], "seq", -1)
    d_normed = sum(mix1[c] * d_mixed[c] for c in range(4)) + jnp.concatenate([d_before[:, 1:], from_next], axis=1)
    d_g1 = jnp.sum(z1 * d_normed, axis=(0, 1))
    d_b1 = jnp.sum(d_normed, axis=(0, 1))
    d_input = (d_middle + back_standardize(d_normed * g1, z1, s1)).astype(BF16)

    rows_of = [d_g1, d_b1] + d_mix1 + [sums[3], sums[2], sums[0], sums[1], d_g2, d_b2] + d_mix2
    small_grad = jnp.stack(rows_of).reshape(14, ranks, share).transpose(1, 0, 2)
    small_grad = jnp.pad(small_grad, ((0, 0), (0, 2), (0, LANES - share))).reshape(grid.shape + (16, LANES))
    parts = [
        g.reshape(grid.shape + (g.shape[0] // ranks, g.shape[1]))
        for g in (grad_f_value, grad_f_key, grad_f_recept, grad_out, grad_g, grad_r, grad_k, grad_v)
    ] + [small_grad]
    chunks = [("x", "y"), ("y", "x"), ("x", "y"), ("y", "x"), ("x", "y"), ("y", "x"), ("x", "y"), ("y", "x"), ("x", "y")]
    s_fv, s_fk, s_fr, s_o, s_g, s_r, s_k, s_v, s_small = scatter_all(grid, parts, chunks)
    s = s_small[:14, :share]
    shape = incoming.shape
    return (
        result.reshape(shape), d_input.reshape(shape),
        s[0], s[1], s[2:6].T, s_r, s_k, s_v, s_g, s[6], s[7], s[8], s[9], s_o, s[10], s[11], s[12:14].T,
        s_fk, s_fv, s_fr,
    )


def solution(mesh):
    grid = Grid(mesh.shape["seq"], mesh.shape["batch"])
    both, rows = P(("seq", "batch")), P(("seq", "batch"), None)
    tokens, entry = P("batch", "seq", None), P("batch", None)
    return jax.shard_map(
        functools.partial(local, grid),
        mesh=mesh,
        in_specs=(
            tokens, entry, entry, P("batch", None, None, None), tokens,
            both, both, rows, rows, rows, rows, rows, both, both, both, both, rows, both, both, rows, rows, rows, rows,
        ),
        out_specs=(
            tokens, tokens, both, both, rows, rows, rows, rows, rows, both, both, both, both, rows, both, both, rows,
            rows, rows, rows,
        ),
        check_vma=False,
    )
```

time: 3020 us -> 583 us (0.19); the launches traced: 2970 us -> 574 us
  waiting for transfers between devices: 1690 us -> 0.78 us
  local copies, waits for them, and re-layouts: 528 us -> 36.2 us
  Pallas kernels: 0 us -> 416 us
  blocking collectives: 209 us -> 0 us
  matrix products: 267 us -> 85.4 us
  other arithmetic: 167 us -> 26.4 us
  starting transfers between devices: 89.2 us -> 7.41 us
    reduce_scatter x8 -> x0, waiting for transfers between devices: 1530 us -> none  [local(): lax.psum_scatter(tuple(cumulative_sums), ('seq', 'batch'), scatter_dimens...]
    pallas_call x0 -> x4, Pallas kernels: none -> 416 us  [the longest x1 176 us: scatter_all(): pl.pallas_call(functools.partial(scatter_kernel, grid, chunks), out_shape...]
    pad x64 -> x2, local copies, waits for them, and re-layouts: 269 us -> 1.33 us  [the longest x1 0.72 us: local(): jnp.pad(small_grad, ((0, 0), (0, 2), (0, LANES - share)))]
    dot_general x70 -> x24, matrix products: 262 us -> 85.4 us  [dot(): lax.dot_general(a, b, (((da,), (db,)), ((), ())), preferred_element_type=...]
    all_gather x2 -> x0, blocking collectives: 129 us -> none  [the longest x1 64.5 us: local(): lax.all_gather(shards[14], ('seq', 'batch'), axis=0, tiled=True)]
    unnamed x20 -> x0, waiting for transfers between devices: 127 us -> none
    unnamed x2 -> x0, blocking collectives: 80.1 us -> none
    unnamed x672 -> x152, local copies, waits for them, and re-layouts: 86.2 us -> 11 us
  transfers between devices with their start and end apart: 42 -> 4, of which waited for: 20 -> 1; matrix products, arithmetic and copies ran while one was open for 21% -> 3% of each run, Pallas kernels for 0% -> 0%
where the time goes in v1:
time: 583 us; the launch traced here: 574 us
  Pallas kernels  416 us (71%)
  matrix products  85.4 us (15%)
  local copies, waits for them, and re-layouts  36.2 us (6%)
  other arithmetic  26.4 us (5%)
  starting transfers between devices  7.41 us (1%)
    pallas_call x1, Pallas kernels, scatter_all(): pl.pallas_call(functools.partial(scatter_kernel, grid, chunks), out_shape...  176 us
    pallas_call x1, Pallas kernels, gather_all(): pl.pallas_call(functools.partial(gather_kernel, grid, orders), out_shape=...  148 us
    dot_general x24, matrix products, dot(): lax.dot_general(a, b, (((da,), (db,)), ((), ())), preferred_element_type=...  85.4 us
    pallas_call x1, Pallas kernels, wkv_backward(): pl.pallas_call(functools.partial(wkv_backward_kernel, grid, tokens // 2),...  53.4 us
    pallas_call x1, Pallas kernels, wkv_forward(): pl.pallas_call(functools.partial(wkv_forward_kernel, grid, tokens // 2),...  38.5 us
  transfers between devices with their start and end apart: 4, of which 1 were waited for; matrix products, arithmetic and copies ran while one was open for 3% of the time, Pallas kernels for 0%

profile of v1, /device:TPU:0, one launch (start us, length us, event | category | flops | bytes accessed | tf_op | source)
XLA Modules:
  0.0 574.2 jit_solution(2548148324908490536)
XLA Ops:
  4.8 148.3 %shard_map.374 = (bf16[2,2,2,4,16,128]{5,4,3,2,1,0:T(8,128)(2,1)}, bf16[2,2,2,4,32,1024]{5,4,3,2,1,0:T(8,128)(2,1)}, bf16[2,2,2,4,32,1024]{5,4,3,2,1,0:T(8,128)(...) custom-call(bf16[16,128]{1,0:T(8,128)(2,1)} %pad.8.refs_0_, ...), custom_call_target="tpu_custom_call" | custom-call | tf_op jit(solution)/shard_map/pallas_call | solution.py:135
  157.2 3.0 copy.44
  181.7 38.5 %shard_map.375 = (bf16[512,1024]{1,0:T(8,128)(2,1)}, bf16[512,1024]{1,0:T(8,128)(2,1)}, bf16[1024,128]{1,0:T(8,128)(2,1)}) custom-call(bf16[512,1024]{1,0:T(8,128)(2,1)} %convolution_convert_fusion.10.r_ref, bf16[512,1024]{1,0:T(8,128)(2,1)} %convolution_convert_fusion.9.k_ref, bf16[512,1024]{1,0:T(8,128)(2,1)} %convolution_convert_fusion.8.v_ref, ...), custom_call_target="tpu_custom_call" | custom-call | tf_op jit(solution)/shard_map/pallas_call | solution.py:476
  220.2 3.3 fusion.14
  229.3 4.0 fusion.16
  233.3 3.9 fusion.8
  237.6 3.5 fusion.2
  241.0 9.9 %multiply_convert_fusion = bf16[512,3584]{1,0:T(8,128)(2,1)} fusion(f32[512,3584]{1,0:T(8,128)} %copy-done.67, bf16[512,1024]{1,0:T(8,128)(2,1)S(1)} %get-tuple-element.102, bf16[3584,1024]{1,0:T(8,128)(2,1)} %bitcast.212), kind=kOutput, calls=%fused_computation.2 | convolution fusion | flops 3765436416 | bytes 19398656 | tf_op jit(solution)/shard_map/dot_general | solution.py:300
  251.0 9.4 %convolution_convert_fusion.1 = bf16[3584,1024]{1,0:T(8,128)(2,1)} fusion(bf16[512,1024]{1,0:T(8,128)(2,1)S(1)} %get-tuple-element.102, f32[512,3584]{1,0:T(8,128)} %copy-done.67), kind=kOutput, calls=%fused_computation.1 | convolution fusion | flops 3767271424 | bytes 15728640 | tf_op jit(solution)/shard_map/dot_general | solution.py:300
  260.4 6.1 %convolution_convert_fusion = bf16[1024,3584]{1,0:T(8,128)(2,1)} fusion(bf16[512,1024]{1,0:T(8,128)(2,1)S(1)} %get-tuple-element.94, bf16[512,3584]{1,0:T(8,128)(2,1)S(1)} %copy-done.66), kind=kOutput, calls=%fused_computation | convolution fusion | flops 3761766400 | bytes 12058624 | tf_op jit(solution)/shard_map/dot_general | solution.py:300
  266.5 6.3 %fusion.17 = f32[2,256,1024]{2,1,0:T(8,128)S(1)} fusion(bf16[2,256,3584]{2,1,0:T(8,128)(2,1)S(1)} %bitcast.227, bf16[1024,3584,1]{1,0,2:T(8,128)(2,1)} %bitcast.208), kind=kOutput, calls=%fused_computation.107 | convolution fusion | flops 3758096384 | bytes 13107200 | tf_op jit(solution)/shard_map/dot_general | solution.py:300
  272.8 2.8 multiply_reduce_fusion
  277.0 2.6 convolution_convert_fusion.7
  281.4 4.0 multiply_reduce_fusion.2
  287.8 2.6 fusion.18.d_att_ref
  290.4 2.6 convolution_convert_fusion.6
  293.1 53.4 %shard_map.376 = (bf16[512,1024]{1,0:T(8,128)(2,1)}, bf16[512,1024]{1,0:T(8,128)(2,1)}, bf16[512,1024]{1,0:T(8,128)(2,1)}, bf16[512,1024]{1,0:T(8,128)(2,1)}, f32[8,1024]{1,0:T(8,128)}) custom-call(bf16[512,1024]{1,0:T(8,128)(2,1)} %convolution_convert_fusion.10.r_ref, bf16[512,1024]{1,0:T(8,128)(2,1)} %convolution_convert_fusion.9.k_ref, ...), custom_call_target="tpu_custom_call" | custom-call | tf_op jit(solution)/shard_map/pallas_call | solution.py:627
  346.5 4.4 convolution_convert_fusion.4
  350.9 2.7 convolution_convert_fusion.3
  353.6 2.7 convolution_convert_fusion.2
  364.2 2.8 multiply_add_fusion
  370.5 8.0 %multiply_reduce_fusion.7 = (f32[1024]{0:T(1024)S(1)}, f32[2,256]{1,0:T(2,128)}, f32[2,256]{1,0:T(2,128)}, f32[1024]{0:T(1024)S(1)}, f32[1024]{0:T(1024)S(1)}, /...) fusion(bf16[2,256,1024]{2,1,0:T(8,128)(2,1)S(1)} %copy-done, ...), kind=kLoop, calls=%fused_computation.29 | loop fusion | flops 16245760 | bytes 15785984 | tf_op jit(solution)/shard_map/reduce_sum | solution.py:776
  384.5 175.9 %shard_map.377 = (f32[112,1024]{1,0:T(8,128)}, f32[32,3584]{1,0:T(8,128)}, f32[32,1024]{1,0:T(8,128)}, f32[32,1024]{1,0:T(8,128)}, f32[32,1024]{1,0:T(8,128)}, /...) custom-call(bf16[2,2,2,4,112,1024]{5,4,3,2,1,0:T(8,128)(2,1)} %bitcast.170, ...), custom_call_target="tpu_custom_call" | custom-call | tf_op jit(solution)/shard_map/pallas_call | solution.py:283
  564.3 4.1 add_convert_fusion
  (250 shorter events, 67.4 us)
Async XLA Ops:
  0.7 153.5 %copy-start = (bf16[2,256,1024]{2,1,0:T(8,128)(2,1)S(1)}, bf16[2,256,1024]{2,1,0:T(8,128)(2,1)}, u32[]{:S(2)}) copy-start(bf16[2,256,1024]{2,1,0:T(8,128)(2,1)} %param.23) | copy-start | bytes 3145732
  154.6 16.5 %copy-start.1 = (f32[2,256,1024]{2,1,0:T(8,128)}, f32[2,256,1024]{2,1,0:T(8,128)S(1)}, u32[]{:S(2)}) copy-start(f32[2,256,1024]{2,1,0:T(8,128)S(1)} %multiply_add_fusion.4) | copy-start | bytes 6291460
  154.6 10.1 %copy-start.43 = (bf16[2,1024]{1,0:T(2,128)(2,1)S(1)}, bf16[2,1024]{1,0:T(2,128)(2,1)}, u32[]{:S(2)}) copy-start(bf16[2,1024]{1,0:T(2,128)(2,1)} %param.24) | copy-start | bytes 12292
  154.7 12.4 %collective-permute-start = (f32[2,1,1024]{2,1,0:T(1,128)S(1)}, f32[2,1,1024]{2,1,0:T(1,128)S(1)}, u32[]{:S(2)}, u32[]{:S(2)}) collective-permute-start(f32[2,1,1024]{2,1,0:T(1,128)S(1)} %slice.234), channel_id=1, source_target_pairs={{0,4},{4,8},{8,12},{12,16},{16,20},{20,24},{24,28},{1,5},{5,9},{9,... | collective-permute-start | bytes 24584 | tf_op jit(solution)/shard_map/ppermute | solution.py:642
  173.0 5.3 copy-start.14
  223.4 62.0 %copy-start.31 = (f32[2,256]{1,0:T(2,128)}, f32[2,256]{1,0:T(2,128)S(1)}, u32[]{:S(2)}) copy-start(f32[2,256]{1,0:T(2,128)S(1)} %div.33) | copy-start | bytes 6148
  223.8 61.7 %copy-start.33 = (f32[2,256]{1,0:T(2,128)}, f32[2,256]{1,0:T(2,128)S(1)}, u32[]{:S(2)}) copy-start(f32[2,256]{1,0:T(2,128)S(1)} %rsqrt.22) | copy-start | bytes 6148
  224.3 3.2 collective-permute-start.1
  227.8 5.5 slice-start.2
  228.9 8.4 %copy-start.20 = (bf16[512,1024]{1,0:T(8,128)(2,1)}, bf16[512,1024]{1,0:T(8,128)(2,1)S(1)}, u32[]{:S(2)}) copy-start(bf16[512,1024]{1,0:T(8,128)(2,1)S(1)} %get-tuple-element.95) | copy-start | bytes 3145732
  251.0 9.4 %copy-start.66 = (bf16[512,3584]{1,0:T(8,128)(2,1)S(1)}, bf16[512,3584]{1,0:T(8,128)(2,1)}, u32[]{:S(2)}) copy-start(bf16[512,3584]{1,0:T(8,128)(2,1)} %multiply_convert_fusion) | copy-start | bytes 11010052
  266.5 6.3 %copy-start.13 = (bf16[512,1024]{1,0:T(8,128)(2,1)S(1)}, bf16[512,1024]{1,0:T(8,128)(2,1)}, u32[]{:S(2)}) copy-start(bf16[512,1024]{1,0:T(8,128)(2,1)} %get-tuple-element.97) | copy-start | bytes 3145732
  275.7 5.7 collective-permute-start.2
  367.0 3.5 collective-permute-start.3
  384.5 179.7 %copy-start.41 = (f32[2,256]{1,0:T(2,128)S(1)}, f32[2,256]{1,0:T(2,128)}, u32[]{:S(2)}) copy-start(f32[2,256]{1,0:T(2,128)} %get-tuple-element.79) | copy-start | bytes 6148
  384.5 179.8 %copy-start.40 = (f32[2,256]{1,0:T(2,128)S(1)}, f32[2,256]{1,0:T(2,128)}, u32[]{:S(2)}) copy-start(f32[2,256]{1,0:T(2,128)} %get-tuple-element.80) | copy-start | bytes 6148
  384.5 179.8 %copy-start.32 = (f32[2,256]{1,0:T(2,128)S(1)}, f32[2,256]{1,0:T(2,128)}, u32[]{:S(2)}) copy-start(f32[2,256]{1,0:T(2,128)} %copy-done.31) | copy-start | bytes 6148
  384.5 179.8 %copy-start.34 = (f32[2,256]{1,0:T(2,128)S(1)}, f32[2,256]{1,0:T(2,128)}, u32[]{:S(2)}) copy-start(f32[2,256]{1,0:T(2,128)} %copy-done.33) | copy-start | bytes 6148
  384.5 179.8 %copy-start.37 = (f32[2,256]{1,0:T(2,128)S(1)}, f32[2,256]{1,0:T(2,128)}, u32[]{:S(2)}) copy-start(f32[2,256]{1,0:T(2,128)} %copy-done.36) | copy-start | bytes 6148
  384.5 179.8 %copy-start.39 = (f32[2,256]{1,0:T(2,128)S(1)}, f32[2,256]{1,0:T(2,128)}, u32[]{:S(2)}) copy-start(f32[2,256]{1,0:T(2,128)} %copy-done.38) | copy-start | bytes 6148
  564.3 5.5 copy-start.28
  564.3 6.1 %copy-start.27 = (f32[32,1024]{1,0:T(8,128)S(1)}, f32[32,1024]{1,0:T(8,128)}, u32[]{:S(2)}) copy-start(f32[32,1024]{1,0:T(8,128)} %get-tuple-element.168) | copy-start | bytes 393220
  564.3 6.8 %copy-start.26 = (f32[32,1024]{1,0:T(8,128)S(1)}, f32[32,1024]{1,0:T(8,128)}, u32[]{:S(2)}) copy-start(f32[32,1024]{1,0:T(8,128)} %get-tuple-element.173) | copy-start | bytes 393220
  564.3 7.4 %copy-start.24 = (f32[32,3584]{1,0:T(8,128)S(1)}, f32[32,3584]{1,0:T(8,128)}, u32[]{:S(2)}) copy-start(f32[32,3584]{1,0:T(8,128)} %get-tuple-element.177) | copy-start | bytes 1376260
  (52 other events, 159.6 us)

commit v2 on v1

--- a/solution.py
+++ b/solution.py
@@ -55,95 +55,6 @@
     for peer in peers:
         pl.semaphore_signal(barrier, inc=1, device_id=peer, device_id_type=MESH)
     pl.semaphore_wait(barrier, len(peers))
-
-
-def gather_kernel(grid, orders, *refs):
-    count = len(orders)
-    shards, fulls = refs[:count], refs[count : 2 * count]
-    own_sem, send_sem, recv_sem = refs[2 * count :]
-    index, digit = grid.place()
-
-    def others(name):
-        return [(j, lax.rem(digit[name] + j, grid.size[name])) for j in range(1, grid.size[name])]
-
-    greet([grid.peer(index, digit, name, t) for name in grid.order for _, t in others(name)])
-
-    started = []
-
-    def send(chunk, source, place, name):
-        copies = []
-        for j, target in others(name):
-            slot = len(started)
-            copy = pltpu.make_async_remote_copy(
-                src_ref=source,
-                dst_ref=place,
-                send_sem=send_sem.at[slot],
-                recv_sem=recv_sem.at[slot],
-                device_id=grid.peer(index, digit, name, target),
-                device_id_type=MESH,
-            )
-            copy.start()
-            started.append(copy)
-            copies.append(copy)
-        return copies
-
-    pending = {}
-    own = {}
-
-    def stage(chunk, number):
-        full = fulls[chunk]
-        first, second = orders[chunk]
-        if number == 0:
-            place = grid.at(full, **digit)
-            copy = pltpu.make_async_copy(shards[chunk], place, own_sem.at[chunk])
-            copy.start()
-            own[chunk] = copy
-            pending[chunk] = send(chunk, shards[chunk], place, "z")
-            return
-        for copy in pending[chunk]:
-            copy.wait_recv()
-        if number == 1:
-            own[chunk].wait()
-            fixed = {n: digit[n] for n in ("x", "y", "c")}
-            name = first
-        elif number == 2:
-            fixed = {n: digit[n] for n in (second, "c")}
-            name = second
-        elif number == 3:
-            fixed = {"c": digit["c"]}
-            name = "c"
-        else:
-            return
-        place = grid.at(full, **fixed)
-        pending[chunk] = send(chunk, place, place, name)
-
-    for chunk in range(count):
-        stage(chunk, 0)
-    for tick in range(count + 3):
-        for number in (1, 2, 3, 4):
-            chunk = tick - (number - 1)
-            if 0 <= chunk < count:
-                stage(chunk, number)
-    for copy in started:
-        copy.wait_send()
-
-
-def gather_all(grid, shards, orders):
-    count = len(shards)
-    steps = count * sum(size - 1 for size in grid.shape)
-    anywhere = pl.BlockSpec(memory_space=pl.ANY)
-    return pl.pallas_call(
-        functools.partial(gather_kernel, grid, orders),
-        out_shape=[jax.ShapeDtypeStruct(grid.shape + s.shape, s.dtype) for s in shards],
-        in_specs=[anywhere] * count,
-        out_specs=[anywhere] * count,
-        scratch_shapes=[
-            pltpu.SemaphoreType.DMA((count,)),
-            pltpu.SemaphoreType.DMA((steps,)),
-            pltpu.SemaphoreType.DMA((steps,)),
-        ],
-        compiler_params=pltpu.CompilerParams(collective_id=0, has_side_effects=True),
-    )(*shards)
 
 
 def scatter_kernel(grid, chunks, *refs):
@@ -300,7 +211,7 @@
     return lax.dot_general(a, b, (((da,), (db,)), ((), ())), preferred_element_type=F32)
 
 
-PRECISE = dict(score=1, inner=1, cross=1, own=1, back=1)
+PRECISE = dict(score=0, inner=1, cross=1, own=1, back=0)
 
 
 def parts_of(value):
@@ -379,26 +290,276 @@
     return copies
 
 
-def wkv_forward_kernel(
-    grid, length,
-    r_ref, k_ref, v_ref, gate_ref, rate_ref, reward_ref, gain_ref, bias_ref, start_ref, fade_ref,
-    wkv_ref, attended_ref, begin_ref,
-    own_ref, got_ref, out_ref, inner_ref, send_a, recv_a, send_b, recv_b,
-):
-    index, _ = grid.place()
+CHUNK = 1024
+TALL = 512
+
+
+def pieces(columns, step):
+    return [(at, min(step, columns - at)) for at in range(0, columns, step)]
+
+
+class Gather:
+    def __init__(self, grid, index, digit, shards, fulls, plan, own_sem, send_sem, recv_sem):
+        self.grid, self.index, self.digit = grid, index, digit
+        self.shards, self.fulls, self.plan = shards, fulls, plan
+        self.own_sem, self.send_sem, self.recv_sem = own_sem, send_sem, recv_sem
+        self.started, self.pending, self.own = [], {}, {}
+        self.tick, self.done = 0, 0
+
+    def others(self, name):
+        size = self.grid.size[name]
+        return [lax.rem(self.digit[name] + j, size) for j in range(1, size)]
+
+    def send(self, source, place, name):
+        copies = []
+        for target in self.others(name):
+            slot = len(self.started)
+            copy = pltpu.make_async_remote_copy(
+                src_ref=source,
+                dst_ref=place,
+                send_sem=self.send_sem.at[slot],
+                recv_sem=self.recv_sem.at[slot],
+                device_id=self.grid.peer(self.index, self.digit, name, target),
+                device_id_type=MESH,
+            )
+            copy.start()
+            self.started.append(copy)
+            copies.append(copy)
+        return copies
+
+    def stage(self, unit, number):
+        if not 0 <= unit < len(self.plan):
+            return
+        for piece in range(len(self.plan[unit][1])):
+            self.step(unit, piece, number)
+
+    def step(self, unit, piece, number):
+        array, parts = self.plan[unit]
+        column, columns, first, second = parts[piece]
+        digit = self.digit
+        window = pl.ds(column, columns)
+        full = self.fulls[array]
+        key = (unit, piece)
+
+        def at(**fixed):
+            place = tuple(fixed.get(name, slice(None)) for name in self.grid.order)
+            return full.at[place + (slice(None), window)]
+
+        if number == 0:
+            place = at(**digit)
+            source = self.shards[array].at[:, window]
+            copy = pltpu.make_async_copy(source, place, self.own_sem.at[len(self.own)])
+            copy.start()
+            self.own[key] = copy
+            self.pending[key] = self.send(source, place, "z")
+            return
+        for copy in self.pending[key]:
+            copy.wait_recv()
+        if number == 1:
+            self.own[key].wait()
+            fixed, name = {n: digit[n] for n in ("x", "y", "c")}, first
+        elif number == 2:
+            fixed, name = {n: digit[n] for n in (second, "c")}, second
+        elif number == 3:
+            fixed, name = {"c": digit["c"]}, "c"
+        else:
+            self.pending[key] = []
+            return
+        place = at(**fixed)
+        self.pending[key] = self.send(place, place, name)
+
+    def open(self, ahead):
+        self.ahead = ahead
+        for piece in range(ahead):
+            self.stage(piece, 0)
+
+    def pump(self, count=1):
+        for _ in range(count):
+            tick = self.tick
+            self.tick += 1
+            for number in (1, 2, 3):
+                self.stage(tick - (number - 1), number)
+            self.stage(tick + self.ahead, 0)
+
+    def ready(self, piece):
+        while self.tick < piece + 3:
+            self.pump()
+        while self.done <= piece:
+            self.stage(self.done, 4)
+            self.done += 1
+
+    def close(self):
+        for copy in self.started:
+            copy.wait_send()
+
+
+def gather_plan(arrays):
+    plan, starts = [], []
+    for array, (columns, step) in enumerate(arrays):
+        starts.append(len(plan))
+        for column, size in pieces(columns, step):
+            half = size // 2
+            if half % LANES:
+                plan.append((array, [(column, size, "x", "y")]))
+            else:
+                plan.append((array, [(column, half, "x", "y"), (column + half, half, "y", "x")]))
+    return plan, starts
+
+
+def span(unit):
+    return unit[1][0][0], sum(part[1] for part in unit[1])
+
+
+def column_of(row, length):
+    at = lax.broadcasted_iota(jnp.int32, (LANES, LANES), 0)
+    lane = lax.broadcasted_iota(jnp.int32, (LANES, LANES), 1)
+    spread = jnp.where(at == lane, jnp.broadcast_to(row, (LANES, LANES)), 0.0)
+    return jnp.broadcast_to(jnp.sum(spread, axis=1, keepdims=True), (LANES, LANES))
+
+
+def forward_kernel(grid, length, plan, starts, *refs):
+    (
+        x_ref, up_ref, att_entry_ref, ffn_entry_ref, start_ref, *shards
+    ) = refs[:14]
+    fulls = refs[14:23]
+    (
+        result_ref, table_ref, mixed_ref, r_ref, k_ref, v_ref, gate_ref, wkv_ref, attended_ref, begin_ref,
+        middle_ref, mixed2_ref, hidden_ref, d_carried_ref, d_recv_ref, prev_ref,
+    ) = refs[23:39]
+    (
+        normed_ref, wide_ref, tall_ref, small_ref, edge_ref, arrive_ref, recv_ref,
+        own_ref, got_ref, out_ref, fade_ref,
+        own_sem, send_sem, recv_sem, load_sem, edge_send, edge_recv, send_a, recv_a, send_b, recv_b,
+    ) = refs[39:]
+    index, digit = grid.place()
     me = index["seq"]
-    greet([(lax.rem(me + j, grid.seq), index["batch"]) for j in range(1, grid.seq)])
-    width = r_ref.shape[1]
+    tokens, width = x_ref.shape
+    segments = tokens // length
     pairs, rows = width // LANES, width // grid.seq
+    batch_roles = [n for n in grid.order if grid.axis[n] == "batch"]
+    gather = Gather(grid, index, digit, shards, fulls, plan, own_sem, send_sem, recv_sem)
+    peers = [grid.peer(index, digit, n, t) for n in batch_roles for t in gather.others(n)]
+    peers += [(lax.rem(me + j, grid.seq), index["batch"]) for j in range(1, grid.seq)]
+    greet(peers)
+    gather.open(3)
+
+    def first_piece(array):
+        return starts[array]
+
+    def load(array, piece, buffer, slot):
+        gather.ready(piece)
+        column, columns = span(plan[piece])
+        source = fulls[array].at[(slice(None),) * 5 + (pl.ds(column, columns),)]
+        target = buffer.at[(slot,) + (slice(None),) * 5 + (pl.ds(0, columns),)]
+        copy = pltpu.make_async_copy(source, target, load_sem.at[slot])
+        copy.start()
+        return copy
+
+    def weight(buffer, slot, window):
+        value = buffer[(slot,) + (slice(None),) * 5 + (window,)]
+        return value.reshape((-1, value.shape[-1]))
+
+    def tile(n, step=256):
+        return pl.ds(pl.multiple_of(n * step, step), step)
+
+    gather.ready(0)
+    copy = pltpu.make_async_copy(fulls[0], small_ref, load_sem.at[0])
+    copy.start()
+    copy.wait()
+    ranks = grid.seq * grid.batch
+    small = small_ref[...].astype(F32).reshape((ranks, 16, LANES))
+    per = ranks // pairs
+    for p in range(pairs):
+        total = small[p * per]
+        for j in range(1, per):
+            total = total + small[p * per + j]
+        table_ref[:, p * LANES : (p + 1) * LANES] = total
+    gather.pump()
+
+    def shift_rows(segment, source_ref, body):
+        step = 64
+
+        def run(i, carry):
+            at = pl.ds(pl.multiple_of(segment * length + i * step, step), step)
+            current = source_ref[at, :]
+            row = lax.broadcasted_iota(jnp.int32, (step, 1), 0)
+            previous = jnp.where(row == 0, carry, pltpu.roll(current, 1, 0))
+            body(at, current, previous)
+            return current[step - 1 : step, :]
+
+        lax.fori_loop(0, length // step, run, prev_ref[segment : segment + 1, :])
+
+    def swap_edges(entry_ref, slot):
+        edge_ref[...] = jnp.zeros_like(edge_ref)
+        for q in range(segments):
+            last = (q + 1) * length
+            edge_ref[q : q + 1, :] = normed_ref[last - 8 : last, :][7:8, :]
+        copy = pltpu.make_async_remote_copy(
+            src_ref=edge_ref,
+            dst_ref=arrive_ref.at[slot],
+            send_sem=edge_send.at[slot],
+            recv_sem=edge_recv.at[slot],
+            device_id=(lax.rem(me + 1, grid.seq), index["batch"]),
+            device_id_type=MESH,
+        )
+        copy.start()
+        copy.wait()
+        first = jnp.where(me == 0, 1.0, 0.0)
+        prev_ref[...] = arrive_ref[slot] * (1.0 - first)
+        prev_ref[0:segments, :] += entry_ref[...].astype(F32) * first
+
+    def norm(source_ref, gain, bias):
+        step = 64
+
+        def run(i, carry):
+            at = pl.ds(pl.multiple_of(i * step, step), step)
+            value = source_ref[at, :].astype(F32)
+            center = value - jnp.mean(value, axis=-1, keepdims=True)
+            spread = jnp.mean(center * center, axis=-1, keepdims=True)
+            normed_ref[at, :] = center * lax.rsqrt(spread + 1e-05) * table_ref[gain : gain + 1, :] + table_ref[bias : bias + 1, :]
+            return carry
+
+        lax.fori_loop(0, tokens // step, run, 0)
+
+    norm(x_ref, 0, 1)
+    swap_edges(att_entry_ref, 0)
+
+    def mix_one(at, current, previous):
+        for c in range(4):
+            blend = table_ref[2 + c : 3 + c, :]
+            mixed_ref[c, at, :] = (current * blend + previous * (1.0 - blend)).astype(BF16)
+
+    for q in range(segments):
+        shift_rows(q, normed_ref, mix_one)
+
+    def project_to(array, slot, left, target_ref):
+        copy = load(array, first_piece(array), wide_ref, slot)
+        copy.wait()
+
+        def run(n, carry):
+            value = dot(left[...], weight(wide_ref, slot, tile(n)), 1, 0)
+            target_ref[:, tile(n)] = value.astype(target_ref.dtype)
+            return carry
+
+        lax.fori_loop(0, width // 256, run, 0)
+
+    project_to(1, 0, mixed_ref.at[1], k_ref)
+    project_to(2, 1, mixed_ref.at[2], v_ref)
     ones, ones16 = block_ones(F32), block_ones(BF16)
+    group = lax.div(me * rows, LANES)
+    own_log = table_ref[6:7, pl.ds(pl.multiple_of(group * LANES, LANES), LANES)]
+    fade_ref[...] = column_of(jnp.exp(-length * jnp.exp(own_log)), length)
 
     def columns(p):
         return pl.ds(pl.multiple_of(p * LANES, LANES), LANES)
 
+    def rate_of(p):
+        return jnp.exp(table_ref[6:7, columns(p)])
+
     def own_states(p, carry):
-        _, _, end = decays(rate_ref[:, columns(p)], length)
+        _, _, end = decays(rate_of(p), length)
         both = []
-        for q in range(2):
+        for q in range(segments):
             token = pl.ds(q * length, length)
             k_end = k_ref[token, columns(p)].astype(F32) * end
             both.append(dot2(k_end, v_ref[token, columns(p)], 0, 0, "own"))
@@ -407,15 +568,30 @@
 
     lax.fori_loop(0, pairs, own_states, 0)
     first = exchange(grid, index, own_ref, got_ref, rows, send_a, recv_a)
+    project_to(3, 0, mixed_ref.at[0], r_ref)
+    project_to(4, 1, mixed_ref.at[3], gate_ref)
+    for copy in first:
+        copy.wait_recv()
+    state = start_ref[...]
+    fade = fade_ref[pl.ds(pl.multiple_of(lax.rem(me * rows, LANES), rows), rows), :]
+    for block in range(grid.seq):
+        at = pl.ds(block * rows, rows)
+        out_ref[at, :] = state.astype(BF16)
+        state = fade * state + got_ref[at, :].astype(F32)
+    second = exchange(grid, index, out_ref, begin_ref, rows, send_b, recv_b)
+    gather.pump()
 
     later = lax.broadcasted_iota(jnp.int32, (length, length), 0) > lax.broadcasted_iota(
         jnp.int32, (length, length), 1
     )
+    for copy in second:
+        copy.wait_recv()
 
     def inside(p, carry):
-        down, up, _ = decays(rate_ref[:, columns(p)], length)
+        down, up, _ = decays(rate_of(p), length)
         pick = half_masks(length)
-        for q in range(2):
+        begin = begin_ref[columns(p), :].astype(F32)
+        for q in range(segments):
             token = pl.ds(q * length, length)
             r = r_ref[token, columns(p)].astype(F32)
             k = k_ref[token, columns(p)].astype(F32)
@@ -428,65 +604,135 @@
                 scores = jnp.where(later, dot3(r_head, k_up, 1, 1, "score"), 0.0)
                 halves.append(dot2(scores, v, 1, 0, "inner"))
             inner = jnp.where(pick, halves[0], halves[1])
-            self_part = head_sum(r * reward_ref[:, columns(p)] * k, ones16)
-            inner_ref[token, columns(p)] = inner + self_part * v.astype(F32)
-        return carry
-
-    lax.fori_loop(0, pairs, inside, 0)
-
-    for copy in first:
-        copy.wait_recv()
-    state = start_ref[...]
-    fade = fade_ref[...]
-    for block in range(grid.seq):
-        at = pl.ds(block * rows, rows)
-        out_ref[at, :] = state.astype(BF16)
-        state = fade * state + got_ref[at, :].astype(F32)
-    second = exchange(grid, index, out_ref, begin_ref, rows, send_b, recv_b)
-    for copy in second:
-        copy.wait_recv()
-
-    def across(p, carry):
-        down, _, _ = decays(rate_ref[:, columns(p)], length)
-        begin = begin_ref[columns(p), :].astype(F32)
-        for q in range(2):
-            token = pl.ds(q * length, length)
-            r_down = r_ref[token, columns(p)].astype(F32) * down
+            self_part = head_sum(r * table_ref[7:8, columns(p)] * k, ones16)
+            inner = inner + self_part * v.astype(F32)
             state16 = unfold(begin, q, ones).astype(BF16)
-            y = (inner_ref[token, columns(p)] + dot2(r_down, state16, 1, 0, "cross")).astype(BF16)
+            y = (inner + dot2(r_down, state16, 1, 0, "cross")).astype(BF16)
             wkv_ref[token, columns(p)] = y
             center = y.astype(F32) - dot(y, ones16, 1, 0) * (1.0 / SUBSPACE_EXTENT)
             spread = head_sum(center * center, ones16) * (1.0 / SUBSPACE_EXTENT)
             z = center * lax.rsqrt(spread + 0.00064)
-            normalized = z * gain_ref[:, columns(p)] + bias_ref[:, columns(p)]
+            normalized = z * table_ref[8:9, columns(p)] + table_ref[9:10, columns(p)]
             g = gate_ref[token, columns(p)]
             attended_ref[token, columns(p)] = (normalized * g / (1.0 + jnp.exp(-g))).astype(BF16)
         return carry
 
-    lax.fori_loop(0, pairs, across, 0)
+    for quarter in range(4):
+        lax.fori_loop(quarter * pairs // 4, (quarter + 1) * pairs // 4, inside, 0)
+        gather.pump()
+
+    copy = load(5, first_piece(5), wide_ref, 0)
+    copy.wait()
+
+    def out_project(n, carry):
+        value = dot(attended_ref[...], weight(wide_ref, 0, tile(n)), 1, 0)
+        middle_ref[:, tile(n)] = x_ref[:, tile(n)].astype(F32) + value
+        return carry
+
+    lax.fori_loop(0, width // 256, out_project, 0)
+    norm(middle_ref, 10, 11)
+    swap_edges(ffn_entry_ref, 1)
+
+    def mix_two(at, current, previous):
+        for c in range(2):
+            blend = table_ref[12 + c : 13 + c, :]
+            mixed2_ref[c, at, :] = (current * blend + previous * (1.0 - blend)).astype(BF16)
+
+    for q in range(segments):
+        shift_rows(q, normed_ref, mix_two)
+    copy = load(6, first_piece(6), wide_ref, 1)
+    copy.wait()
+
+    def receive(n, carry):
+        value = dot(mixed2_ref[1], weight(wide_ref, 1, tile(n)), 1, 0)
+        recv = 1.0 / (1.0 + jnp.exp(-value))
+        recv_ref[:, tile(n)] = recv
+        d_carried_ref[:, tile(n)] = (recv * up_ref[:, tile(n)].astype(F32)).astype(BF16)
+        return carry
+
+    lax.fori_loop(0, width // 256, receive, 0)
+
+    for piece in range(starts[7], starts[8]):
+        slot = (piece - starts[7]) % 2
+        column, size = span(plan[piece])
+        copy = load(7, piece, wide_ref, slot)
+        copy.wait()
+
+        def key(n, carry):
+            value = jnp.maximum(dot(mixed2_ref[0], weight(wide_ref, slot, tile(n)), 1, 0), 0.0)
+            hidden_ref[:, pl.ds(pl.multiple_of(column + n * 256, 256), 256)] = (value * value).astype(BF16)
+            return carry
+
+        lax.fori_loop(0, size // 256, key, 0)
+    for piece in range(starts[8], len(plan)):
+        slot = (piece - starts[8]) % 2
+        column, size = span(plan[piece])
+        copy = load(8, piece, tall_ref, slot)
+        copy.wait()
+        window = pl.ds(column, size)
+
+        def carry_out(m, carry):
+            at = tile(m, 256)
+            carried = dot(hidden_ref[at, :], weight(tall_ref, slot, pl.ds(0, size)), 1, 0)
+            recv = recv_ref[at, window]
+            result_ref[at, window] = (middle_ref[at, window] + recv * carried).astype(BF16)
+            upstream = up_ref[at, window].astype(F32)
+            d_recv_ref[at, window] = (recv * (1.0 - recv) * carried * upstream).astype(BF16)
+            return carry
+
+        lax.fori_loop(0, tokens // 256, carry_out, 0)
+
     for copy in first + second:
         copy.wait_send()
-
-
-def wkv_forward(grid, r, k, v, gate_pre, rate, reward, gain, bias, start, fade):
-    tokens, width = r.shape
+    gather.close()
+
+
+def forward(grid, x, upstream, att_entry, ffn_entry, start, shards, length):
+    tokens, width = x.shape
+    steps = [LANES] + [CHUNK] * 7 + [TALL]
+    plan, starts = gather_plan([(s.shape[1], step) for s, step in zip(shards, steps)])
+    total = sum(len(unit[1]) for unit in plan)
+    hidden = shards[7].shape[1]
+    vmem = pl.BlockSpec(memory_space=pltpu.VMEM)
+    anywhere = pl.BlockSpec(memory_space=pl.ANY)
+    flat = jax.ShapeDtypeStruct((tokens, width), BF16)
+    flat32 = jax.ShapeDtypeStruct((tokens, width), F32)
     state = pltpu.VMEM((width, LANES), BF16)
     sems = pltpu.SemaphoreType.DMA((grid.seq - 1,))
-    vmem = pl.BlockSpec(memory_space=pltpu.VMEM)
+    count = total * sum(size - 1 for size in grid.shape)
     return pl.pallas_call(
-        functools.partial(wkv_forward_kernel, grid, tokens // 2),
-        out_shape=[
-            jax.ShapeDtypeStruct((tokens, width), BF16),
-            jax.ShapeDtypeStruct((tokens, width), BF16),
-            jax.ShapeDtypeStruct((width, LANES), BF16),
+        functools.partial(forward_kernel, grid, length, plan, starts),
+        out_shape=[jax.ShapeDtypeStruct(grid.shape + s.shape, s.dtype) for s in shards]
+        + [
+            flat, jax.ShapeDtypeStruct((16, width), F32), jax.ShapeDtypeStruct((4, tokens, width), BF16),
+            flat, flat, flat, flat32, flat, flat, jax.ShapeDtypeStruct((width, LANES), BF16),
+            flat32, jax.ShapeDtypeStruct((2, tokens, width), BF16), jax.ShapeDtypeStruct((tokens, hidden), BF16),
+            flat, flat, jax.ShapeDtypeStruct((8, width), F32),
         ],
-        in_specs=[vmem] * 10,
-        out_specs=[vmem] * 3,
-        scratch_shapes=[state, state, state, pltpu.VMEM((tokens, width), F32), sems, sems, sems, sems],
+        in_specs=[vmem] * 5 + [anywhere] * 9,
+        out_specs=[anywhere] * 9 + [vmem] * 16,
+        scratch_shapes=[
+            pltpu.VMEM((tokens, width), F32),
+            pltpu.VMEM((2,) + grid.shape + (shards[1].shape[0], CHUNK), BF16),
+            pltpu.VMEM((2,) + grid.shape + (shards[8].shape[0], TALL), BF16),
+            pltpu.VMEM(grid.shape + shards[0].shape, BF16),
+            pltpu.VMEM((8, width), F32),
+            pltpu.VMEM((2, 8, width), F32),
+            pltpu.VMEM((tokens, width), F32),
+            state, state, state,
+            pltpu.VMEM((LANES, LANES), F32),
+            pltpu.SemaphoreType.DMA((total,)),
+            pltpu.SemaphoreType.DMA((count,)),
+            pltpu.SemaphoreType.DMA((count,)),
+            pltpu.SemaphoreType.DMA((2,)),
+            pltpu.SemaphoreType.DMA((2,)),
+            pltpu.SemaphoreType.DMA((2,)),
+            sems, sems, sems, sems,
+        ],
         compiler_params=pltpu.CompilerParams(
-            collective_id=2, has_side_effects=True, vmem_limit_bytes=VMEM_LIMIT
+            collective_id=0, has_side_effects=True, vmem_limit_bytes=VMEM_LIMIT
         ),
-    )(r, k, v, gate_pre, rate, reward, gain, bias, start, fade)
+    )(x, upstream, att_entry, ffn_entry, start, *shards)
 
 
 def wkv_backward_kernel(
@@ -677,19 +923,27 @@
     share = width // ranks
     is_first = lax.axis_index("seq") == 0
 
+    per = LANES // share
+    rank = lax.axis_index(("seq", "batch"))
     small = jnp.stack(
         [ln1_gain, ln1_bias] + [att_mix[:, c] for c in range(4)] + [decay_log, reward, gn_gain, gn_bias, ln2_gain, ln2_bias]
         + [ffn_mix[:, c] for c in range(2)]
     )
-    small = jnp.pad(small, ((0, 2), (0, LANES - share)))
-    half = f_key.shape[1] // 2
-    shards = [small, w_recept, w_key, w_value, w_gate, w_out, f_recept, f_key, f_value]
-    orders = [("x", "y"), ("x", "y"), ("y", "x"), ("x", "y"), ("y", "x"), ("x", "y"), ("y", "x"), ("x", "y"), ("y", "x")]
-    full = gather_all(grid, shards, orders)
-    table = full[0].reshape(ranks, 16, LANES)[:, :14, :share].transpose(1, 0, 2).reshape(14, width).astype(F32)
-    W_r, W_k, W_v, W_g, W_o, F_r, F_k, F_v = [
-        w.reshape((ranks * w.shape[4], w.shape[5])) for w in full[1:]
-    ]
+    small = jnp.tile(jnp.pad(small, ((0, 2), (0, 0))), (1, per))
+    lane = lax.broadcasted_iota(jnp.int32, small.shape, 1)
+    small = jnp.where(lane // share == rank % per, small, jnp.zeros_like(small))
+    rows = width // grid.seq
+    row = lax.axis_index("seq") * rows
+    start = memory.transpose(1, 2, 0, 3).reshape(width, segments * SUBSPACE_EXTENT)
+    start = lax.dynamic_slice_in_dim(start, row, rows, 0)
+    shards = [small, w_key, w_value, w_recept, w_gate, w_out, f_recept, f_key, f_value]
+    outs = forward(
+        grid, incoming.reshape(tokens, width), upstream.reshape(tokens, width), att_entry, ffn_entry, start, shards, length
+    )
+    W_k, W_v, W_r, W_g, W_o, F_r, F_k, F_v = [w.reshape((ranks * w.shape[4], w.shape[5])) for w in outs[1:9]]
+    (
+        result, table, mixed, r, k, v, gate_pre, wkv, attended, begin, middle, mixed2, hidden, d_carried, d_recv, prev2,
+    ) = outs[9:]
     g1, b1 = table[0], table[1]
     mix1 = table[2:6]
     rate = jnp.exp(table[6])[None, :]
@@ -697,48 +951,21 @@
     gg, gb = table[8][None, :], table[9][None, :]
     g2, b2 = table[10], table[11]
     mix2 = table[12:14]
-
+    own_rate = lax.dynamic_slice_in_dim(rate[0], row, rows, 0)
+    fade = jnp.broadcast_to(jnp.exp(-own_rate * length)[:, None], (rows, LANES))
     x = incoming.astype(F32)
     z1, s1 = standardize(x, 1e-05)
     normed = z1 * g1 + b1
     arrived = shifted(normed[:, -1:], "seq", 1)
     previous = jnp.where(is_first, att_entry[:, None, :].astype(F32), arrived)
     before = jnp.concatenate([previous, normed[:, :-1]], axis=1)
-    mixed = [
-        (normed * mix1[c] + before * (1.0 - mix1[c])).astype(BF16).reshape(tokens, width) for c in range(4)
-    ]
-    r = project(mixed[0], W_r).astype(BF16)
-    k = project(mixed[1], W_k).astype(BF16)
-    v = project(mixed[2], W_v).astype(BF16)
-    gate_pre = project(mixed[3], W_g)
-
-    rows = width // grid.seq
-    row = lax.axis_index("seq") * rows
-    start = memory.transpose(1, 2, 0, 3).reshape(width, segments * SUBSPACE_EXTENT)
-    start = lax.dynamic_slice_in_dim(start, row, rows, 0)
-    own_rate = lax.dynamic_slice_in_dim(rate[0], row, rows, 0)
-    fade = jnp.broadcast_to(jnp.exp(-own_rate * length)[:, None], (rows, LANES))
-    wkv, attended, begin = wkv_forward(grid, r, k, v, gate_pre, rate, bonus, gg, gb, start, fade)
-
-    middle = x.reshape(tokens, width) + project(attended, W_o)
     middle = middle.reshape(segments, length, width)
     z2, s2 = standardize(middle, 1e-05)
     normed2 = z2 * g2 + b2
-    arrived2 = shifted(normed2[:, -1:], "seq", 1)
-    previous2 = jnp.where(is_first, ffn_entry[:, None, :].astype(F32), arrived2)
-    before2 = jnp.concatenate([previous2, normed2[:, :-1]], axis=1)
-    mixed2 = [
-        (normed2 * mix2[c] + before2 * (1.0 - mix2[c])).astype(BF16).reshape(tokens, width) for c in range(2)
-    ]
-    key_pos = jnp.maximum(project(mixed2[0], F_k), 0.0)
-    hidden = (key_pos * key_pos).astype(BF16)
-    carried = project(hidden, F_v)
-    recv = jax.nn.sigmoid(project(mixed2[1], F_r))
-    result = (middle.reshape(tokens, width) + recv * carried).astype(BF16)
+    before2 = jnp.concatenate([prev2[:segments][:, None], normed2[:, :-1]], axis=1)
+    key_pos = jnp.sqrt(hidden.astype(F32))
 
     d_out = upstream.astype(F32).reshape(tokens, width)
-    d_carried = (recv * d_out).astype(BF16)
-    d_recv = (recv * (1.0 - recv) * carried * d_out).astype(BF16)
     grad_f_value = outer(hidden, d_carried)
     grad_f_recept = outer(mixed2[1], d_recv)
     d_key = (2.0 * key_pos * back_through(d_carried, F_v)).astype(BF16)

time: 583 us -> 524 us (0.90); the launches traced: 574 us -> 521 us
  matrix products: 85.4 us -> 57.8 us
  Pallas kernels: 416 us -> 400 us
    dot_general x24 -> x16, matrix products: 85.4 us -> 57.8 us  [dot(): lax.dot_general(a, b, (((da,), (db,)), ((), ())), preferred_element_type=...]
    pallas_call x2 -> x1, Pallas kernels: 187 us -> 178 us  [forward(): pl.pallas_call(functools.partial(forward_kernel, grid, length, plan, star...]
    pallas_call x1, Pallas kernels: 53.4 us -> 47.4 us  [wkv_backward(): pl.pallas_call(functools.partial(wkv_backward_kernel, grid, tokens // 2),...]
    unnamed x152 -> x109, local copies, waits for them, and re-layouts: 11 us -> 13.6 us
  transfers between devices with their start and end apart: 4 -> 3, of which waited for: 1 -> 0; matrix products, arithmetic and copies ran while one was open for 3% -> 9% of each run, Pallas kernels for 0% -> 9%
where the time goes in v2:
time: 524 us; the launch traced here: 521 us
  Pallas kernels  400 us (76%)
  matrix products  57.8 us (11%)
  local copies, waits for them, and re-layouts  35.3 us (7%)
  other arithmetic  21 us (4%)
  starting transfers between devices  5.6 us (1%)
    pallas_call x1, Pallas kernels, forward(): pl.pallas_call(functools.partial(forward_kernel, grid, length, plan, star...  178 us
    pallas_call x1, Pallas kernels, scatter_all(): pl.pallas_call(functools.partial(scatter_kernel, grid, chunks), out_shape...  175 us
    dot_general x16, matrix products, dot(): lax.dot_general(a, b, (((da,), (db,)), ((), ())), preferred_element_type=...  57.8 us
    pallas_call x1, Pallas kernels, wkv_backward(): pl.pallas_call(functools.partial(wkv_backward_kernel, grid, tokens // 2),...  47.4 us
    unnamed x109, local copies, waits for them, and re-layouts  13.6 us
  transfers between devices with their start and end apart: 3, of which 0 were waited for; matrix products, arithmetic and copies ran while one was open for 9% of the time, Pallas kernels for 9%

profile of v2, /device:TPU:0, one launch (start us, length us, event | category | flops | bytes accessed | tf_op | source)
XLA Modules:
  0.0 521.4 jit_solution(9862518604144283708)
XLA Ops:
  3.1 2.0 copy.43
  7.0 177.7 %shard_map.374 = (bf16[2,2,2,4,16,128]{5,4,3,2,1,0:T(8,128)(2,1)}, bf16[2,2,2,4,32,1024]{5,4,3,2,1,0:T(8,128)(2,1)}, bf16[2,2,2,4,32,1024]{5,4,3,2,1,0:T(8,128)(...) custom-call(bf16[512,1024]{1,0:T(8,128)(2,1)} %bitcast.152, ...), custom_call_target="tpu_custom_call" | custom-call | tf_op jit(solution)/shard_map/pallas_call | solution.py:703
  184.7 1.9 reduce_sum.163
  188.7 9.6 %multiply_convert_fusion = bf16[512,3584]{1,0:T(8,128)(2,1)S(1)} fusion(bf16[512,3584]{1,0:T(8,128)(2,1)} %get-tuple-element.60, bf16[512,1024]{1,0:T(8,128)(2,1)} %get-tuple-element.61, bf16[3584,1024]{1,0:T(8,128)(2,1)} %bitcast.207), kind=kOutput, calls=%fused_computation.2 | convolution fusion | flops 3765436416 | bytes 15728640 | tf_op jit(solution)/shard_map/dot_general | solution.py:211
  198.4 6.2 %fusion.29 = f32[2,256,1024]{2,1,0:T(8,128)S(1)} fusion(bf16[2,256,3584]{2,1,0:T(8,128)(2,1)S(1)} %bitcast.215, bf16[1024,3584,1]{1,0,2:T(8,128)(2,1)} %bitcast.206), kind=kOutput, calls=%fused_computation.103 | convolution fusion | flops 3758096384 | bytes 13107200 | tf_op jit(solution)/shard_map/dot_general | solution.py:211
  207.2 2.9 multiply_reduce_fusion
  213.9 3.0 collective-permute-start.2
  216.9 6.2 %convolution_convert_fusion = bf16[1024,3584]{1,0:T(8,128)(2,1)} fusion(bf16[512,3584]{1,0:T(8,128)(2,1)S(1)} %multiply_convert_fusion, bf16[2,512,1024]{2,1,0:T(8,128)(2,1)S(1)} %copy-done.44), kind=kOutput, calls=%fused_computation | convolution fusion | flops 3761766400 | bytes 12058624 | tf_op jit(solution)/shard_map/dot_general | solution.py:211
  223.2 2.6 convolution_convert_fusion.7
  225.8 6.2 %convolution_convert_fusion.1 = bf16[3584,1024]{1,0:T(8,128)(2,1)} fusion(bf16[512,3584]{1,0:T(8,128)(2,1)S(1)} %copy-done.39, bf16[512,1024]{1,0:T(8,128)(2,1)S(1)} %copy-done.46), kind=kOutput, calls=%fused_computation.1 | convolution fusion | flops 3761766400 | bytes 12058624 | tf_op jit(solution)/shard_map/dot_general | solution.py:211
  232.0 1.7 slice.199
  233.9 3.6 multiply_reduce_fusion.2
  240.1 2.6 fusion.30.d_att_ref
  243.4 47.4 %shard_map.375 = (bf16[512,1024]{1,0:T(8,128)(2,1)}, bf16[512,1024]{1,0:T(8,128)(2,1)}, bf16[512,1024]{1,0:T(8,128)(2,1)}, bf16[512,1024]{1,0:T(8,128)(2,1)}, f32[8,1024]{1,0:T(8,128)}) custom-call(bf16[512,1024]{1,0:T(8,128)(2,1)} %get-tuple-element.67.r_ref, bf16[512,1024]{1,0:T(8,128)(2,1)} %get-tuple-element.68.k_ref, ...), custom_call_target="tpu_custom_call" | custom-call | tf_op jit(solution)/shard_map/pallas_call | solution.py:873
  290.8 4.3 convolution_convert_fusion.2
  295.1 2.6 convolution_convert_fusion.3
  297.8 2.6 convolution_convert_fusion.4
  300.4 2.6 convolution_convert_fusion.5
  308.5 2.8 multiply_add_fusion.1
  312.6 2.6 convolution_convert_fusion.6
  315.3 1.7 slice.201
  317.4 8.0 %fusion.11 = (f32[1024]{0:T(1024)S(1)}, f32[2,256]{1,0:T(2,128)}, f32[2,256]{1,0:T(2,128)}, f32[1024]{0:T(1024)S(1)}, f32[1024]{0:T(1024)S(1)}, /*index=5*/f32[1...) fusion(bf16[2,256,1024]{2,1,0:T(8,128)(2,1)S(1)} %copy-done.1, ...), kind=kLoop, calls=%fused_computation.16 | loop fusion | flops 16245760 | bytes 15785984 | tf_op jit(solution)/shard_map/reduce_sum | solution.py:1003
  331.5 175.1 %shard_map.376 = (f32[112,1024]{1,0:T(8,128)}, f32[32,3584]{1,0:T(8,128)}, f32[32,1024]{1,0:T(8,128)}, f32[32,1024]{1,0:T(8,128)}, f32[32,1024]{1,0:T(8,128)}, /...) custom-call(bf16[2,2,2,4,112,1024]{5,4,3,2,1,0:T(8,128)(2,1)} %bitcast.157, ...), custom_call_target="tpu_custom_call" | custom-call | tf_op jit(solution)/shard_map/pallas_call | solution.py:194
  510.5 4.1 fusion.10
  (180 shorter events, 39.6 us)
Async XLA Ops:
  187.9 44.0 %copy-start.34 = (f32[1,1024]{1,0:T(1,128)}, f32[1,1024]{1,0:T(1,128)S(1)}, u32[]{:S(2)}) copy-start(f32[1,1024]{1,0:T(1,128)S(1)} %get-tuple-element.128.rate_ref) | copy-start | bytes 12292
  207.2 4.2 copy-start.1
  210.2 23.7 %collective-permute-start = (f32[2,1,1024]{2,1,0:T(1,128)S(1)}, f32[2,1,1024]{2,1,0:T(1,128)S(1)}, u32[]{:S(2)}, u32[]{:S(2)}) collective-permute-start(f32[2,1,1024]{2,1,0:T(1,128)S(1)} %slice.200), channel_id=1, source_target_pairs={{4,0},{8,4},{12,8},{16,12},{20,16},{24,20},{28,24},{5,1},{9,5},{13... | collective-permute-start | bytes 24584 | tf_op jit(solution)/shard_map/ppermute | solution.py:888
  211.7 105.7 %copy-start.24 = (f32[2,256]{1,0:T(2,128)}, f32[2,256]{1,0:T(2,128)S(1)}, u32[]{:S(2)}) copy-start(f32[2,256]{1,0:T(2,128)S(1)} %broadcast_multiply_fusion.2) | copy-start | bytes 6148
  211.7 5.2 %copy-start.44 = (bf16[2,512,1024]{2,1,0:T(8,128)(2,1)S(1)}, bf16[2,512,1024]{2,1,0:T(8,128)(2,1)}, u32[]{:S(2)}) copy-start(bf16[2,512,1024]{2,1,0:T(8,128)(2,1)} %get-tuple-element.82) | copy-start | bytes 6291460
  212.1 105.3 %copy-start.27 = (f32[2,256]{1,0:T(2,128)}, f32[2,256]{1,0:T(2,128)S(1)}, u32[]{:S(2)}) copy-start(f32[2,256]{1,0:T(2,128)S(1)} %add_rsqrt_fusion) | copy-start | bytes 6148
  213.9 101.4 %collective-permute-start.2 = (f32[2,1,1024]{2,1,0:T(1,128)S(1)}, f32[2,1,1024]{2,1,0:T(1,128)S(1)}, u32[]{:S(2)}, u32[]{:S(2)}) collective-permute-start(f32[2,1,1024]{2,1,0:T(1,128)S(1)} %slice.203), channel_id=1, source_target_pairs={{0,4},{4,8},{8,12},{12,16},{16,20},{20,24},{24,28},{1,5},{5,9},{9,... | collective-permute-start | bytes 24584 | tf_op jit(solution)/shard_map/ppermute | solution.py:888
  233.9 3.7 copy-start.3
  238.8 3.9 copy-start.12
  290.8 4.3 copy-start.38
  290.8 4.3 copy-start.49
  308.5 4.1 copy-start.13
  308.5 4.1 copy-start.45
  311.3 6.1 %collective-permute-start.1 = (f32[2,1,1024]{2,1,0:T(1,128)S(1)}, f32[2,1,1024]{2,1,0:T(1,128)S(1)}, u32[]{:S(2)}, u32[]{:S(2)}) collective-permute-start(f32[2,1,1024]{2,1,0:T(1,128)S(1)} %slice.202), channel_id=1, source_target_pairs={{4,0},{8,4},{12,8},{16,12},{20,16},{24,20},{28,24},{5,1},{9,5},{13... | collective-permute-start | bytes 24584 | tf_op jit(solution)/shard_map/ppermute | solution.py:888
  331.4 179.0 %copy-start.36 = (f32[2,256]{1,0:T(2,128)S(1)}, f32[2,256]{1,0:T(2,128)}, u32[]{:S(2)}) copy-start(f32[2,256]{1,0:T(2,128)} %get-tuple-element.103) | copy-start | bytes 6148
  331.5 179.0 %copy-start.35 = (f32[2,256]{1,0:T(2,128)S(1)}, f32[2,256]{1,0:T(2,128)}, u32[]{:S(2)}) copy-start(f32[2,256]{1,0:T(2,128)} %get-tuple-element.104) | copy-start | bytes 6148
  331.5 179.0 %copy-start.25 = (f32[2,256]{1,0:T(2,128)S(1)}, f32[2,256]{1,0:T(2,128)}, u32[]{:S(2)}) copy-start(f32[2,256]{1,0:T(2,128)} %copy-done.24) | copy-start | bytes 6148
  331.5 179.0 %copy-start.28 = (f32[2,256]{1,0:T(2,128)S(1)}, f32[2,256]{1,0:T(2,128)}, u32[]{:S(2)}) copy-start(f32[2,256]{1,0:T(2,128)} %copy-done.27) | copy-start | bytes 6148
  331.5 179.0 %copy-start.30 = (f32[2,256]{1,0:T(2,128)S(1)}, f32[2,256]{1,0:T(2,128)}, u32[]{:S(2)}) copy-start(f32[2,256]{1,0:T(2,128)} %copy-done.29) | copy-start | bytes 6148
  331.5 179.0 %copy-start.32 = (f32[2,256]{1,0:T(2,128)S(1)}, f32[2,256]{1,0:T(2,128)}, u32[]{:S(2)}) copy-start(f32[2,256]{1,0:T(2,128)} %copy-done.31) | copy-start | bytes 6148
  510.5 4.1 copy-start.11
  514.6 4.3 copy-start.17
  514.6 5.1 copy-start.16
  514.7 5.8 %copy-start.18 = (f32[32,1024]{1,0:T(8,128)S(1)}, f32[32,1024]{1,0:T(8,128)}, u32[]{:S(2)}) copy-start(f32[32,1024]{1,0:T(8,128)} %get-tuple-element.195) | copy-start | bytes 393220
  (29 other events, 63.8 us)

commit v3 on v2

--- a/solution.py
+++ b/solution.py
@@ -13,7 +13,7 @@
 MESH = pl.DeviceIdType.MESH
 F32 = jnp.float32
 BF16 = jnp.bfloat16
-VMEM_LIMIT = 60 * 1024 * 1024
+VMEM_LIMIT = 63 * 1024 * 1024
 
 
 class Grid:
@@ -24,7 +24,7 @@
         elif seq == 16 and batch == 8:
             digits = [("y", "seq", 4, 4), ("x", "seq", 1, 4), ("z", "batch", 2, 4), ("c", "batch", 1, 2)]
         else:
-            digits = [("y", "seq", 1, seq), ("x", "seq", 1, 1), ("z", "batch", 1, batch), ("c", "batch", 1, 1)]
+            raise ValueError("unknown mesh")
         self.order = [name for name, *_ in digits]
         self.axis = {name: axis for name, axis, *_ in digits}
         self.stride = {name: stride for name, _, stride, _ in digits}
@@ -55,156 +55,6 @@
     for peer in peers:
         pl.semaphore_signal(barrier, inc=1, device_id=peer, device_id_type=MESH)
     pl.semaphore_wait(barrier, len(peers))
-
-
-def scatter_kernel(grid, chunks, *refs):
-    count = len(chunks)
-    parts, outs = refs[:count], refs[count : 2 * count]
-    mine, rc, rx, ry, rz = (refs[2 * count + i * count : 2 * count + (i + 1) * count] for i in range(5))
-    own_sem, send_sem, recv_sem = refs[7 * count :]
-    index, digit = grid.place()
-
-    def others(name):
-        return [(j, lax.rem(digit[name] + j, grid.size[name])) for j in range(1, grid.size[name])]
-
-    greet([grid.peer(index, digit, name, t) for name in grid.order for _, t in others(name)])
-    started = []
-
-    def send(source, gone, name, slots):
-        copies = []
-        for j, target in others(name):
-            slot = len(started)
-            copy = pltpu.make_async_remote_copy(
-                src_ref=grid.at(source, gone, **{name: target}),
-                dst_ref=slots.at[j - 1],
-                send_sem=send_sem.at[slot],
-                recv_sem=recv_sem.at[slot],
-                device_id=grid.peer(index, digit, name, target),
-                device_id_type=MESH,
-            )
-            copy.start()
-            started.append(copy)
-            copies.append(copy)
-        return copies
-
-    pending, own = {}, {}
-
-    def total(target, terms, shape):
-        steps = 1
-        for size in shape:
-            steps *= size
-
-        def body(i, carry):
-            where, rest = [], i
-            for size in reversed(shape):
-                where.append(lax.rem(rest, size))
-                rest = lax.div(rest, size)
-            where = tuple(reversed(where))
-            value = terms[0](where).astype(F32)
-            for term in terms[1:]:
-                value = value + term(where).astype(F32)
-            target(where, value)
-            return carry
-
-        lax.fori_loop(0, steps, body, 0)
-
-    def picker(ref, gone, name):
-        names = [n for n in grid.order if n not in gone and n != name]
-
-        def read(where):
-            at = dict(zip(names, where))
-            at[name] = digit[name]
-            return ref[tuple(at[n] for n in grid.order if n not in gone)]
-
-        return read
-
-    def slot_reader(slots, j):
-        return lambda where: slots[(j,) + where]
-
-    def stage(chunk, number):
-        first, second = chunks[chunk]
-        if number == 0:
-            copy = pltpu.make_async_copy(grid.at(parts[chunk], c=digit["c"]), mine[chunk], own_sem.at[chunk])
-            copy.start()
-            own[chunk] = copy
-            pending[chunk] = send(parts[chunk], "", "c", rc[chunk])
-            return
-        for copy in pending[chunk]:
-            copy.wait_recv()
-        if number == 1:
-            own[chunk].wait()
-            m = mine[chunk]
-
-            def put(where, value):
-                m[where] = value.astype(m.dtype)
-
-            if grid.size["c"] > 1:
-                total(put, [lambda where: m[where]] + [slot_reader(rc[chunk], j) for j in range(grid.size["c"] - 1)], grid.sizes("c"))
-            pending[chunk] = send(m, "c", first, (rx if first == "x" else ry)[chunk])
-        elif number == 2:
-            m, slots = mine[chunk], (rx if first == "x" else ry)[chunk]
-
-            def put(where, value):
-                slots[(0,) + where] = value.astype(slots.dtype)
-
-            total(put, [picker(m, "c", first)] + [slot_reader(slots, j) for j in range(grid.size[first] - 1)], grid.sizes("c" + first))
-            pending[chunk] = send(slots.at[0], "c" + first, second, (rx if second == "x" else ry)[chunk])
-        elif number == 3:
-            before, slots = (rx if first == "x" else ry)[chunk].at[0], (rx if second == "x" else ry)[chunk]
-
-            def put(where, value):
-                slots[(0,) + where] = value.astype(slots.dtype)
-
-            total(put, [picker(before, "c" + first, second)] + [slot_reader(slots, j) for j in range(grid.size[second] - 1)], grid.sizes("cxy"))
-            pending[chunk] = send(slots.at[0], "cxy", "z", rz[chunk])
-        elif number == 4:
-            before, slots = (rx if second == "x" else ry)[chunk].at[0], rz[chunk]
-            value = before[digit["z"]].astype(F32)
-            for j in range(grid.size["z"] - 1):
-                value = value + slots[j].astype(F32)
-            outs[chunk][...] = value
-
-    for chunk in range(count):
-        stage(chunk, 0)
-    for tick in range(count + 3):
-        for number in (1, 2, 3, 4):
-            chunk = tick - (number - 1)
-            if 0 <= chunk < count:
-                stage(chunk, number)
-    for copy in started:
-        copy.wait_send()
-
-
-def scatter_all(grid, parts, chunks):
-    count = len(parts)
-    steps = count * sum(size - 1 for size in grid.shape)
-    anywhere = pl.BlockSpec(memory_space=pl.ANY)
-    mine, rc, rx, ry, rz = [], [], [], [], []
-    for part, (first, second) in zip(parts, chunks):
-        tile, kind = part.shape[4:], part.dtype
-        mine.append(pltpu.VMEM(grid.sizes("c") + tile, kind))
-        rc.append(pltpu.VMEM((max(grid.size["c"] - 1, 1),) + grid.sizes("c") + tile, kind))
-        shapes = {
-            first: pltpu.VMEM((max(grid.size[first] - 1, 1),) + grid.sizes("c" + first) + tile, kind),
-            second: pltpu.VMEM((max(grid.size[second] - 1, 1),) + grid.sizes("cxy") + tile, kind),
-        }
-        rx.append(shapes["x"])
-        ry.append(shapes["y"])
-        rz.append(pltpu.VMEM((max(grid.size["z"] - 1, 1),) + tile, kind))
-    return pl.pallas_call(
-        functools.partial(scatter_kernel, grid, chunks),
-        out_shape=[jax.ShapeDtypeStruct(p.shape[4:], F32) for p in parts],
-        in_specs=[anywhere] * count,
-        out_specs=[pl.BlockSpec(memory_space=pltpu.VMEM)] * count,
-        scratch_shapes=mine + rc + rx + ry + rz + [
-            pltpu.SemaphoreType.DMA((count,)),
-            pltpu.SemaphoreType.DMA((steps,)),
-            pltpu.SemaphoreType.DMA((steps,)),
-        ],
-        compiler_params=pltpu.CompilerParams(
-            collective_id=1, has_side_effects=True, vmem_limit_bytes=VMEM_LIMIT
-        ),
-    )(*parts)
 
 
 def dot(a, b, da, db):
@@ -476,7 +326,7 @@
         table_ref[:, p * LANES : (p + 1) * LANES] = total
     gather.pump()
 
-    def shift_rows(segment, source_ref, body):
+    def shift_rows(segment, source_ref, slot, body):
         step = 64
 
         def run(i, carry):
@@ -487,7 +337,7 @@
             body(at, current, previous)
             return current[step - 1 : step, :]
 
-        lax.fori_loop(0, length // step, run, prev_ref[segment : segment + 1, :])
+        lax.fori_loop(0, length // step, run, prev_ref[slot, segment : segment + 1, :])
 
     def swap_edges(entry_ref, slot):
         edge_ref[...] = jnp.zeros_like(edge_ref)
@@ -505,8 +355,8 @@
         copy.start()
         copy.wait()
         first = jnp.where(me == 0, 1.0, 0.0)
-        prev_ref[...] = arrive_ref[slot] * (1.0 - first)
-        prev_ref[0:segments, :] += entry_ref[...].astype(F32) * first
+        prev_ref[slot] = arrive_ref[slot] * (1.0 - first)
+        prev_ref[slot, 0:segments, :] += entry_ref[...].astype(F32) * first
 
     def norm(source_ref, gain, bias):
         step = 64
@@ -530,7 +380,7 @@
             mixed_ref[c, at, :] = (current * blend + previous * (1.0 - blend)).astype(BF16)
 
     for q in range(segments):
-        shift_rows(q, normed_ref, mix_one)
+        shift_rows(q, normed_ref, 0, mix_one)
 
     def project_to(array, slot, left, target_ref):
         copy = load(array, first_piece(array), wide_ref, slot)
@@ -639,7 +489,7 @@
             mixed2_ref[c, at, :] = (current * blend + previous * (1.0 - blend)).astype(BF16)
 
     for q in range(segments):
-        shift_rows(q, normed_ref, mix_two)
+        shift_rows(q, normed_ref, 1, mix_two)
     copy = load(6, first_piece(6), wide_ref, 1)
     copy.wait()
 
@@ -707,7 +557,7 @@
             flat, jax.ShapeDtypeStruct((16, width), F32), jax.ShapeDtypeStruct((4, tokens, width), BF16),
             flat, flat, flat, flat32, flat, flat, jax.ShapeDtypeStruct((width, LANES), BF16),
             flat32, jax.ShapeDtypeStruct((2, tokens, width), BF16), jax.ShapeDtypeStruct((tokens, hidden), BF16),
-            flat, flat, jax.ShapeDtypeStruct((8, width), F32),
+            flat, flat, jax.ShapeDtypeStruct((2, 8, width), F32),
         ],
         in_specs=[vmem] * 5 + [anywhere] * 9,
         out_specs=[anywhere] * 9 + [vmem] * 16,
@@ -735,102 +585,519 @@
     )(x, upstream, att_entry, ffn_entry, start, *shards)
 
 
-def wkv_backward_kernel(
-    grid, length,
-    r_ref, k_ref, v_ref, gate_ref, wkv_ref, d_att_ref, rate_ref, reward_ref, gain_ref, bias_ref, fade_ref, begin_ref,
-    d_gate_ref, dr_ref, dk_ref, dv_ref, sums_ref,
-    dy_ref, own_ref, got_ref, out_ref, end_ref, send_a, recv_a, send_b, recv_b,
-):
-    index, _ = grid.place()
+STAGES = ("c", "first", "second", "z")
+GAPS = (1, 2, 2, 2)
+
+
+class Piece:
+    def __init__(self, array, column, columns, tile, first, kind):
+        self.array, self.column, self.columns = array, column, columns
+        self.first, self.second = (first, "y" if first == "x" else "x")
+        self.tile, self.kind = (tile, columns), kind
+        self.group = (tile, columns, first, jnp.dtype(kind).name)
+
+
+def scatter_plan(arrays):
+    units, of_array, counts = [], [], {}
+    for array, (tile, columns, step, kind) in enumerate(arrays):
+        mine = []
+        at = 0
+        while at < columns:
+            unit = []
+            for first in ("x", "y"):
+                if at < columns:
+                    piece = Piece(array, at, step, tile, first, kind)
+                    piece.place = counts.get(piece.group, 0)
+                    counts[piece.group] = piece.place + 1
+                    unit.append(piece)
+                    at += step
+            mine.append(len(units))
+            units.append(unit)
+        of_array.append(mine)
+    return units, of_array, counts
+
+
+def stage_shapes(grid, group):
+    tile, columns, first, _ = group
+    second = "y" if first == "x" else "x"
+    end = (tile, columns)
+    return [
+        grid.sizes("c") + end,
+        (grid.size[first] - 1,) + grid.sizes("c" + first) + end,
+        (grid.size[second] - 1,) + grid.sizes("cxy") + end,
+        (grid.size["z"] - 1,) + end,
+    ]
+
+
+class Scatter:
+    def __init__(self, grid, index, digit, units, keeps, gives, landings, loads, outs, send_sem, recv_sem, load_sem):
+        self.grid, self.index, self.digit, self.units = grid, index, digit, units
+        self.keeps, self.gives, self.landings, self.loads, self.outs = keeps, gives, landings, loads, outs
+        self.send_sem, self.recv_sem, self.load_sem = send_sem, recv_sem, load_sem
+        self.started, self.pending, self.giving = [], {}, {}
+        self.stage, self.when, self.now = {}, {}, 0
+
+    def copy(self, source, target, name, digit):
+        slot = len(self.started)
+        copy = pltpu.make_async_remote_copy(
+            src_ref=source,
+            dst_ref=target,
+            send_sem=self.send_sem.at[slot],
+            recv_sem=self.recv_sem.at[slot],
+            device_id=self.grid.peer(self.index, self.digit, name, digit),
+            device_id_type=MESH,
+        )
+        copy.start()
+        self.started.append([copy, True])
+        return copy
+
+    def open(self, unit, number):
+        piece = self.units[unit][number]
+        if piece.group in self.giving:
+            entry = self.giving.pop(piece.group)
+            entry[0].wait_send()
+            entry[1] = False
+        return self.keeps[unit, number], self.gives[piece.group]
+
+    def give(self, unit):
+        for number, piece in enumerate(self.units[unit]):
+            target = lax.rem(self.digit["c"] + 1, 2)
+            copy = self.copy(self.gives[piece.group], self.landings[piece.group][0].at[piece.place], "c", target)
+            self.giving[piece.group] = self.started[-1]
+            self.pending[unit, number] = [copy]
+        self.stage[unit], self.when[unit] = 0, self.now
+
+    def load(self, unit, number):
+        piece, stage = self.units[unit][number], self.stage[unit]
+        for copy in self.pending[unit, number]:
+            copy.wait_recv()
+        copy = pltpu.make_async_copy(
+            self.landings[piece.group][stage].at[piece.place],
+            self.loads[piece.group][stage],
+            self.load_sem.at[2 * stage + number],
+        )
+        copy.start()
+        return copy
+
+    def add(self, unit, number, copy):
+        piece, stage = self.units[unit][number], self.stage[unit]
+        keep, got = self.keeps[unit, number], self.loads[piece.group][stage]
+        names = [n for n in self.grid.order if n != "c"]
+        fixed = ((), (piece.first,), (piece.first, piece.second), ("x", "y", "z"))[stage]
+        free = [n for n in names if n not in fixed]
+        copy.wait()
+        terms = 1 if stage == 0 else got.shape[0]
+        steps = 1
+        for n in free:
+            steps *= self.grid.size[n]
+
+        def body(i, carry):
+            at, rest = {n: self.digit[n] for n in fixed}, i
+            for n in reversed(free):
+                at[n] = lax.rem(rest, self.grid.size[n])
+                rest = lax.div(rest, self.grid.size[n])
+            where, inner = tuple(at[n] for n in names), tuple(at[n] for n in free)
+            value = keep[where].astype(F32)
+            for j in range(terms):
+                value = value + got[inner if stage == 0 else (j,) + inner].astype(F32)
+            if stage == 3:
+                self.outs[piece.array][:, piece.column : piece.column + piece.columns] = value
+            else:
+                keep[where] = value.astype(keep.dtype)
+            return carry
+
+        if steps == 1:
+            body(0, 0)
+        else:
+            lax.fori_loop(0, steps, body, 0)
+        if stage == 3:
+            return
+        name = (piece.first, piece.second, "z")[stage]
+        held = {n: self.digit[n] for n in fixed}
+        copies = []
+        for j in range(1, self.grid.size[name]):
+            target = lax.rem(self.digit[name] + j, self.grid.size[name])
+            source = self.grid.at(keep, "c", **held, **{name: target})
+            copies.append(self.copy(source, self.landings[piece.group][stage + 1].at[piece.place, j - 1], name, target))
+        self.pending[unit, number] = copies
+
+    def tick(self, gaps=GAPS):
+        work = []
+        for stage in (3, 2, 1, 0):
+            waiting = [u for u in sorted(self.stage) if self.stage[u] == stage]
+            if waiting and self.now - self.when[waiting[0]] >= gaps[stage]:
+                work.append(waiting[0])
+        copies = {}
+        for unit in work:
+            for number in range(len(self.units[unit])):
+                copies[unit, number] = self.load(unit, number)
+        for unit in work:
+            for number in range(len(self.units[unit])):
+                self.add(unit, number, copies[unit, number])
+            self.stage[unit] += 1
+            self.when[unit] = self.now
+            if self.stage[unit] == 4:
+                del self.stage[unit]
+        self.now += 1
+
+    def close(self):
+        while self.stage:
+            self.tick((1, 1, 1, 1))
+        for copy, waiting in self.started:
+            if waiting:
+                copy.wait_send()
+
+
+def backward_kernel(grid, length, units, of_array, groups, *refs):
+    it = iter(refs)
+
+    def take(count):
+        return [next(it) for _ in range(count)]
+
+    (table_ref, prev_ref, begin_ref) = take(3)
+    (
+        x_hbm, up_hbm, mixed_hbm, r_hbm, k_hbm, v_hbm, gate_hbm, wkv_hbm, attended_hbm, middle_hbm, mixed2_hbm,
+        hidden_hbm, d_carried_hbm, d_recv_hbm,
+    ) = take(14)
+    w_k, w_v, w_r, w_g, w_o, f_r, f_k, f_v = take(8)
+    (d_input_ref,) = take(1)
+    outs = take(len(of_array))
+    landings = {group: take(4) for group in groups}
+    keeps = {(u, n): next(it) for u, unit in enumerate(units) for n in range(len(unit))}
+    gives = {group: next(it) for group in groups}
+    loads = {group: take(4) for group in groups}
+    (
+        hid, dc, dr, m2, dkey, wide, tall, dn, db, mid, nrm, up, dmid, rr, kk, vv, wk, dgate,
+        own_ref, got_ref, out_ref, end_ref, fade_ref, acc, edge_ref, arrive_ref,
+        send_sem, recv_sem, load_sem, in_sem, wide_sem, edge_send, edge_recv, send_a, recv_a, send_b, recv_b,
+    ) = it
+    index, digit = grid.place()
     me = index["seq"]
-    greet([(lax.rem(me + j, grid.seq), index["batch"]) for j in range(1, grid.seq)])
-    width = r_ref.shape[1]
+    tokens, width = dc.shape
+    segments = tokens // length
     pairs, rows = width // LANES, width // grid.seq
+    n0 = grid.shape[0]
+    c_at = grid.order.index("c") - 1
+    scatter = Scatter(grid, index, digit, units, keeps, gives, landings, loads, outs, send_sem, recv_sem, load_sem)
+    batch_roles = [n for n in grid.order if grid.axis[n] == "batch"]
+    peers = [
+        grid.peer(index, digit, n, lax.rem(digit[n] + j, grid.size[n])) for n in batch_roles for j in range(1, grid.size[n])
+    ]
+    peers += [(lax.rem(me + j, grid.seq), index["batch"]) for j in range(1, grid.seq)]
+
+    fetched = {}
+
+    def fetch(name, source, target, slot):
+        copy = pltpu.make_async_copy(source, target, in_sem.at[slot])
+        copy.start()
+        fetched[name] = copy
+
+    def have(*names):
+        for name in names:
+            fetched.pop(name).wait()
+
+    fetch("hid", hidden_hbm, hid, 0)
+    fetch("dc", d_carried_hbm, dc, 1)
+    fetch("tall", f_v.at[0], tall, 2)
+    fetch("m2", mixed2_hbm, m2, 3)
+    fetch("dr", d_recv_hbm, dr, 4)
+    fetch("mid", middle_hbm, mid, 5)
+    fetch("up", up_hbm, up, 6)
+    fetch("att", attended_hbm, dgate, 7)
+    fetch("rr", r_hbm, rr, 8)
+    fetch("kk", k_hbm, kk, 9)
+    fetch("vv", v_hbm, vv, 10)
+    fetch("wk", wkv_hbm, wk, 11)
+    acc[...] = jnp.zeros_like(acc)
+    greet(peers)
+
+    everything = (slice(None),) * 5
+
+    def weight_load(array, column, columns, slot):
+        copy = pltpu.make_async_copy(
+            array.at[everything + (pl.ds(column, columns),)],
+            wide.at[(slot,) + everything + (pl.ds(0, columns),)],
+            wide_sem.at[slot],
+        )
+        copy.start()
+        return copy
+
+    def weight(slot, columns):
+        return wide[(slot,) + everything + (pl.ds(0, columns),)].reshape((-1, columns))
+
+    def tile(n, step):
+        return pl.ds(pl.multiple_of(n * step, step), step)
+
+    def gradient(unit, left_ref, right_ref):
+        parts = units[unit]
+        targets = [scatter.open(unit, number) for number in range(len(parts))]
+        span, narrow = left_ref.shape[1] // n0, parts[0].columns < 256
+        for batch in [list(range(len(parts)))] if narrow else [[number] for number in range(len(parts))]:
+            first = parts[batch[0]]
+            width_all = sum(parts[number].columns for number in batch)
+
+            def run(y, carry, batch=batch, first=first, width_all=width_all):
+                total = dot(left_ref[:, tile(y, span)], right_ref[:, first.column : first.column + width_all], 0, 0)
+                is_zero = digit["c"] == 0
+                for number in batch:
+                    keep, give = targets[number]
+                    at = parts[number].column - first.column
+                    value = total[:, at : at + parts[number].columns].reshape(grid.shape[1:] + parts[number].tile)
+                    zero = value[(slice(None),) * c_at + (0,)]
+                    one = value[(slice(None),) * c_at + (1,)]
+                    keep[y] = jnp.where(is_zero, zero, one).astype(keep.dtype)
+                    give[y] = jnp.where(is_zero, one, zero).astype(give.dtype)
+                return carry
+
+            lax.fori_loop(0, n0, run, 0)
+        scatter.give(unit)
+
+    U = dict(zip(("fv", "fr", "fk", "o", "g", "r", "k", "v", "small"), of_array))
+
+    have("hid", "dc")
+    for unit in U["fv"]:
+        gradient(unit, hid, dc)
+        scatter.tick()
+    span = hid.shape[1] // n0
+    loading = weight_load(f_r, 0, width, 0)
+    for y in range(n0):
+        have("tall")
+
+        def key(m, carry, y=y):
+            at = tile(m, 128)
+            window = slice(y * span, (y + 1) * span)
+            d_hidden = dot(dc[at, :], tall[...].reshape((span, width)), 1, 1)
+            dkey[at, window] = (2.0 * jnp.sqrt(hid[at, window].astype(F32)) * d_hidden).astype(BF16)
+            return carry
+
+        lax.fori_loop(0, tokens // 128, key, 0)
+        if y + 1 < n0:
+            fetch("tall", f_v.at[y + 1], tall, 2)
+    have("m2", "dr")
+    gradient(U["fr"][0], m2.at[1], dr)
+    fetch("mx0", mixed_hbm.at[0], hid.at[:, pl.ds(0, width)], 0)
+    fetch("mx1", mixed_hbm.at[1], hid.at[:, pl.ds(width, width)], 1)
+    fetch("mx2", mixed_hbm.at[2], hid.at[:, pl.ds(2 * width, width)], 2)
+    scatter.tick()
+    loading.wait()
+    chunks = pieces(hid.shape[1], CHUNK)
+    loading = weight_load(f_k, *chunks[0], 1)
+
+    def through_recv(m, carry):
+        at = tile(m, 256)
+        db[at, :] = dot(dr[at, :], weight(0, width), 1, 1)
+        return carry
+
+    lax.fori_loop(0, tokens // 256, through_recv, 0)
+    for number, unit in enumerate(U["fk"]):
+        gradient(unit, m2.at[0], dkey)
+        column, columns = chunks[number]
+        slot = (number + 1) % 2
+        loading.wait()
+        if number + 1 < len(chunks):
+            loading = weight_load(f_k, *chunks[number + 1], 1 - slot)
+
+        def through_key(m, carry, number=number, column=column, columns=columns, slot=slot):
+            at = tile(m, 256)
+            value = dot(dkey[at, column : column + columns], weight(slot, columns), 1, 1)
+            dn[at, :] = value if number == 0 else dn[at, :] + value
+            return carry
+
+        lax.fori_loop(0, tokens // 256, through_key, 0)
+        scatter.tick()
+    fetch("mx3", mixed_hbm.at[3], m2.at[0], 3)
+    loading = weight_load(w_o, 0, width, 0)
+
+    step = 64
+
+    def fold_rows(value):
+        return jnp.sum(value.reshape((step // 8, 8, width)), axis=0)
+
+    def norm(source_ref, gain, bias):
+        def run(i, carry):
+            at = tile(i, step)
+            value = source_ref[at, :].astype(F32)
+            center = value - jnp.mean(value, axis=-1, keepdims=True)
+            spread = jnp.mean(center * center, axis=-1, keepdims=True)
+            nrm[at, :] = center * lax.rsqrt(spread + 1e-05) * table_ref[gain : gain + 1, :] + table_ref[bias : bias + 1, :]
+            return carry
+
+        lax.fori_loop(0, tokens // step, run, 0)
+
+    def swap_edges(slot):
+        edge_ref[...] = jnp.zeros_like(edge_ref)
+        for q in range(segments):
+            edge_ref[q : q + 1, :] = db[q * length : q * length + 8, :][0:1, :]
+        copy = pltpu.make_async_remote_copy(
+            src_ref=edge_ref,
+            dst_ref=arrive_ref.at[slot],
+            send_sem=edge_send.at[slot],
+            recv_sem=edge_recv.at[slot],
+            device_id=(lax.rem(me + grid.seq - 1, grid.seq), index["batch"]),
+            device_id_type=MESH,
+        )
+        copy.start()
+        return copy
+
+    def norm_back(source_ref, gain, bias, slot, base_ref, put):
+        keep_next = jnp.where(me == grid.seq - 1, 0.0, 1.0)
+        for q in range(segments):
+            count = length // step
+
+            def run(i, carry, q=q):
+                at = tile(q * count + count - 1 - i, step)
+                value = source_ref[at, :].astype(F32)
+                center = value - jnp.mean(value, axis=-1, keepdims=True)
+                spread = jnp.mean(center * center, axis=-1, keepdims=True)
+                scale = lax.rsqrt(spread + 1e-05)
+                z = center * scale
+                before = db[at, :]
+                row = lax.broadcasted_iota(jnp.int32, (step, 1), 0)
+                d_normed = dn[at, :] + jnp.where(row == step - 1, carry, pltpu.roll(before, step - 1, 0))
+                acc[gain] += fold_rows(z * d_normed)
+                acc[bias] += fold_rows(d_normed)
+                e = d_normed * table_ref[gain : gain + 1, :]
+                back = (e - jnp.mean(e, axis=-1, keepdims=True) - z * jnp.mean(e * z, axis=-1, keepdims=True)) * scale
+                put(at, base_ref[at, :].astype(F32) + back)
+                return before[0:1, :]
+
+            lax.fori_loop(0, count, run, arrive_ref[slot, q : q + 1, :] * keep_next)
+
+    have("mid")
+    norm(mid, 10, 11)
+    for q in range(segments):
+
+        def blend_two(i, carry, q=q):
+            at = tile(q * (length // step) + i, step)
+            current = nrm[at, :]
+            row = lax.broadcasted_iota(jnp.int32, (step, 1), 0)
+            difference = current - jnp.where(row == 0, carry, pltpu.roll(current, 1, 0))
+            first, second = dn[at, :], db[at, :]
+            acc[12] += fold_rows(difference * first)
+            acc[13] += fold_rows(difference * second)
+            a, b = table_ref[12:13, :], table_ref[13:14, :]
+            dn[at, :] = first * a + second * b
+            db[at, :] = first * (1.0 - a) + second * (1.0 - b)
+            return current[step - 1 : step, :]
+
+        lax.fori_loop(0, length // step, blend_two, prev_ref[1, q : q + 1, :])
+    moving = swap_edges(0)
+    scatter.tick()
+    have("up")
+    moving.wait()
+
+    def put_middle(at, value):
+        dmid[at, :] = value
+        dr[at, :] = value.astype(BF16)
+
+    norm_back(mid, 10, 11, 0, up, put_middle)
+    fetch("mid", gate_hbm, mid, 5)
+    fetch("up", x_hbm, up, 6)
+    have("att")
+    gradient(U["o"][0], dgate, dr)
+    loading.wait()
+
+    def through_out(m, carry):
+        at = tile(m, 256)
+        nrm[at, :] = dot(dr[at, :], weight(0, width), 1, 1)
+        return carry
+
+    lax.fori_loop(0, tokens // 256, through_out, 0)
+    scatter.tick()
+
     ones, ones16 = block_ones(F32), block_ones(BF16)
     share = 1.0 / SUBSPACE_EXTENT
 
-    def columns(p):
-        return pl.ds(pl.multiple_of(p * LANES, LANES), LANES)
+    def columns(p, base=0):
+        return pl.ds(pl.multiple_of(base + p * LANES, LANES), LANES)
+
+    def rate_of(p):
+        return jnp.exp(table_ref[6:7, columns(p)])
+
+    group = lax.div(me * rows, LANES)
+    own_log = table_ref[6:7, pl.ds(pl.multiple_of(group * LANES, LANES), LANES)]
+    fade_ref[...] = column_of(jnp.exp(-length * jnp.exp(own_log)), length)
+    have("wk", "mid", "rr")
 
     def own_states(p, carry):
-        down, _, _ = decays(rate_ref[:, columns(p)], length)
+        down, _, _ = decays(rate_of(p), length)
         both = []
         gain_sum, bias_sum = jnp.zeros((1, LANES), F32), jnp.zeros((1, LANES), F32)
-        for q in range(2):
+        for q in range(segments):
             token = pl.ds(q * length, length)
-            y = wkv_ref[token, columns(p)]
+            y = wk[token, columns(p)]
             center = y.astype(F32) - dot(y, ones16, 1, 0) * share
             spread = head_sum(center * center, ones16) * share
             scale = lax.rsqrt(spread + 0.00064)
             z = center * scale
-            gain = gain_ref[:, columns(p)]
-            normalized = z * gain + bias_ref[:, columns(p)]
-            g = gate_ref[token, columns(p)]
+            gain = table_ref[8:9, columns(p)]
+            normalized = z * gain + table_ref[9:10, columns(p)]
+            g = mid[token, columns(p)]
             s = 1.0 / (1.0 + jnp.exp(-g))
-            d_att = d_att_ref[token, columns(p)]
-            d_gate_ref[token, columns(p)] = (d_att * normalized * s * (1.0 + g * (1.0 - s))).astype(BF16)
+            d_att = nrm[token, columns(p)]
+            dgate[token, columns(p)] = (d_att * normalized * s * (1.0 + g * (1.0 - s))).astype(BF16)
             d_norm = d_att * g * s
             gain_sum = gain_sum + jnp.sum(d_norm * z, axis=0, keepdims=True)
             bias_sum = bias_sum + jnp.sum(d_norm, axis=0, keepdims=True)
             e = d_norm * gain
             dy = ((e - head_sum(e, ones16) * share - z * (head_sum(e * z, ones16) * share)) * scale).astype(BF16)
-            dy_ref[token, columns(p)] = dy
-            r_down = r_ref[token, columns(p)].astype(F32) * down
-            both.append(dot2(r_down, dy, 0, 0, "own"))
-        sums_ref[0:1, columns(p)] = gain_sum
-        sums_ref[1:2, columns(p)] = bias_sum
+            dc[token, columns(p)] = dy
+            both.append(dot2(rr[token, columns(p)].astype(F32) * down, dy, 0, 0, "own"))
+        acc[8, 0:1, columns(p)] = gain_sum
+        acc[9, 0:1, columns(p)] = bias_sum
         own_ref[columns(p), :] = fold(both[0], both[1], ones).astype(BF16)
         return carry
 
     lax.fori_loop(0, pairs, own_states, 0)
     first = exchange(grid, index, own_ref, got_ref, rows, send_a, recv_a)
+    have("mx3")
+    gradient(U["g"][0], m2.at[0], dgate)
+    scatter.tick()
     for copy in first:
         copy.wait_recv()
-    fade = fade_ref[...]
+    fade = fade_ref[pl.ds(pl.multiple_of(lax.rem(me * rows, LANES), rows), rows), :]
     state = jnp.zeros_like(fade)
     for block in reversed(range(grid.seq)):
         at = pl.ds(block * rows, rows)
         out_ref[at, :] = state.astype(BF16)
         state = fade * state + got_ref[at, :].astype(F32)
     second = exchange(grid, index, out_ref, end_ref, rows, send_b, recv_b)
+    have("up")
+    norm(up, 0, 1)
+    have("kk", "vv")
     for copy in second:
         copy.wait_recv()
-
     later = lax.broadcasted_iota(jnp.int32, (length, length), 0) > lax.broadcasted_iota(
         jnp.int32, (length, length), 1
     )
-    step = lax.broadcasted_iota(jnp.int32, (length, LANES), 0).astype(F32)
+    time = lax.broadcasted_iota(jnp.int32, (length, LANES), 0).astype(F32)
 
     def inside(p, carry):
-        rate = rate_ref[:, columns(p)]
-        reward = reward_ref[:, columns(p)]
-        down, up, end = decays(rate, length)
+        rate = rate_of(p)
+        reward = table_ref[7:8, columns(p)]
+        down, up_, end = decays(rate, length)
         pick = half_masks(length)
         begins, ends = begin_ref[columns(p), :].astype(F32), end_ref[columns(p), :].astype(F32)
         reward_sum, rate_sum = jnp.zeros((1, LANES), F32), jnp.zeros((1, LANES), F32)
-        for q in range(2):
+        for q in range(segments):
             token = pl.ds(q * length, length)
-            r = r_ref[token, columns(p)].astype(F32)
-            k = k_ref[token, columns(p)].astype(F32)
-            v = v_ref[token, columns(p)]
-            dy = dy_ref[token, columns(p)]
+            r = rr[token, columns(p)].astype(F32)
+            k = kk[token, columns(p)].astype(F32)
+            v = vv[token, columns(p)]
+            dy = dc[token, columns(p)]
             begin, finish = unfold(begins, q, ones), unfold(ends, q, ones)
             begin16, finish16 = begin.astype(BF16), finish.astype(BF16)
-            r_down = r * down
-            k_up = k * up
+            r_down = (r * down).astype(BF16)
+            k_up = (k * up_).astype(BF16)
             k_end = k * end
-            if not PRECISE["back"]:
-                r_down = r_down.astype(BF16).astype(F32)
-                k_up = k_up.astype(BF16).astype(F32)
-                k_end = k_end.astype(BF16).astype(F32)
+            zero = jnp.zeros_like(r_down)
             d_r, d_k, d_v = [], [], []
             for h in range(2):
-                r_head = jnp.where(pick == (h == 0), r_down, 0.0)
-                dy_head = jnp.where(pick == (h == 0), dy.astype(F32), 0.0).astype(BF16)
-                scores = jnp.where(later, dot3(r_head, k_up, 1, 1, "score"), 0.0)
-                d_scores = jnp.where(later, dot(dy_head, v, 1, 1), 0.0)
-                d_r.append(dot3(d_scores, k_up, 1, 0, "back"))
-                d_k.append(dot3(d_scores, r_down, 0, 0, "back"))
+                here = pick == (h == 0)
+                scores = jnp.where(later, dot(jnp.where(here, r_down, zero), k_up, 1, 1), 0.0)
+                d_scores = jnp.where(later, dot(jnp.where(here, dy, zero), v, 1, 1), 0.0).astype(BF16)
+                d_r.append(dot(d_scores, k_up, 1, 0))
+                d_k.append(dot(d_scores, r_down, 0, 0))
                 d_v.append(dot2(scores, dy, 0, 0, "inner"))
             from_r = jnp.where(pick, d_r[0], d_r[1]) + dot(dy, begin16, 1, 1)
             from_k = jnp.where(pick, d_k[0], d_k[1])
@@ -838,77 +1105,170 @@
             v32, dy32 = v.astype(F32), dy.astype(F32)
             v_dy = head_sum(v32 * dy32, ones16)
             self_part = head_sum(r * reward * k, ones16)
-            dr_ref[token, columns(p)] = (from_r * down + reward * k * v_dy).astype(BF16)
-            dk_ref[token, columns(p)] = (from_k * up + from_end * end + reward * r * v_dy).astype(BF16)
-            dv_ref[token, columns(p)] = (
+            dkey[token, columns(p)] = (from_r * down + reward * k * v_dy).astype(BF16)
+            dkey[token, columns(p, width)] = (from_k * up_ + from_end * end + reward * r * v_dy).astype(BF16)
+            dkey[token, columns(p, 2 * width)] = (
                 jnp.where(pick, d_v[0], d_v[1]) + dot2(k_end, finish16, 1, 0, "cross") + self_part * dy32
             ).astype(BF16)
             reward_sum = reward_sum + jnp.sum(r * k * v_dy, axis=0, keepdims=True)
             terms = (
-                (step + 1.0) * k_up * from_k
-                - step * r_down * from_r
-                - (length - 1.0 - step) * k_end * from_end
+                (time + 1.0) * k_up.astype(F32) * from_k
+                - time * r_down.astype(F32) * from_r
+                - (length - 1.0 - time) * k_end * from_end
             )
             through = lax.dot_general(
                 jnp.ones((8, LANES), F32), begin * finish, (((1,), (1,)), ((), ())),
                 precision=lax.Precision.HIGHEST, preferred_element_type=F32,
             )[0:1, :]
             rate_sum = rate_sum + jnp.sum(terms, axis=0, keepdims=True) - length * jnp.exp(-rate * length) * through
-        sums_ref[2:3, columns(p)] = reward_sum
-        sums_ref[3:4, columns(p)] = rate_sum * rate
+        acc[7, 0:1, columns(p)] = reward_sum
+        acc[6, 0:1, columns(p)] = rate_sum * rate
         return carry
 
-    lax.fori_loop(0, pairs, inside, 0)
-    sums_ref[4:8, :] = jnp.zeros((4, width), F32)
+    for quarter in range(4):
+        lax.fori_loop(quarter * pairs // 4, (quarter + 1) * pairs // 4, inside, 0)
+        scatter.tick()
+    have("mx0", "mx1", "mx2")
+    weights = (w_r, w_k, w_v, w_g)
+    grads = [dkey.at[:, pl.ds(c * width, width)] for c in range(3)] + [dgate]
+
+    def load_rows(y):
+        copies = []
+        for c in range(4):
+            copy = pltpu.make_async_copy(weights[c].at[y], wide.at[c // n0, c % n0], in_sem.at[8 + c])
+            copy.start()
+            copies.append(copy)
+        return copies
+
+    loading = load_rows(0)
+    for c, name in enumerate("rkv"):
+        gradient(U[name][0], hid.at[:, pl.ds(c * width, width)], grads[c])
+    scatter.tick()
+    span = width // n0
+    for y in range(n0):
+        for copy in loading:
+            copy.wait()
+        window = slice(y * span, (y + 1) * span)
+
+        def through_mix(m, carry, y=y, window=window):
+            at = tile(m, 128)
+            current = nrm[at, window]
+            above = nrm[pl.ds(pl.multiple_of(jnp.maximum(m * 128 - 8, 0), 8), 8), window][7:8, :]
+            segment = lax.div(m, length // 128)
+            given = prev_ref[0, 0:1, window]
+            for q in range(1, segments):
+                given = jnp.where(segment == q, prev_ref[0, q : q + 1, window], given)
+            carried = jnp.where(lax.rem(m, length // 128) == 0, given, above)
+            row = lax.broadcasted_iota(jnp.int32, (128, 1), 0)
+            difference = current - jnp.where(row == 0, carried, pltpu.roll(current, 1, 0))
+            here, before = None, None
+            for c in range(4):
+                value = dot(grads[c][at, :], wide[c // n0, c % n0].reshape((span, width)), 1, 1)
+                acc[2 + c, :, window] += jnp.sum((difference * value).reshape((16, 8, span)), axis=0)
+                blend = table_ref[2 + c : 3 + c, window]
+                here = blend * value if c == 0 else here + blend * value
+                before = (1.0 - blend) * value if c == 0 else before + (1.0 - blend) * value
+            dn[at, window] = here
+            db[at, window] = before
+            return carry
+
+        lax.fori_loop(0, tokens // 128, through_mix, 0)
+        if y + 1 < n0:
+            loading = load_rows(y + 1)
+        scatter.tick()
+    moving = swap_edges(1)
+    scatter.tick()
+    moving.wait()
+
+    def put_input(at, value):
+        d_input_ref[at, :] = value.astype(BF16)
+
+    norm_back(up, 0, 1, 1, dmid, put_input)
+
+    sums = [jnp.sum(acc[i], axis=0, keepdims=True) for i in range(14)]
+    for i in range(14):
+        edge_ref[0:1, :] = sums[i]
+        nrm[i : i + 1, :] = edge_ref[0:1, :]
+    nrm[14:16, :] = jnp.zeros((2, width), F32)
+    keep, give = scatter.open(U["small"][0], 0)
+    per = grid.seq * grid.batch // pairs
+    names = [n for n in grid.order if n != "c"]
+
+    def spread(i, carry):
+        at, rest = {}, i
+        for n in reversed(names):
+            at[n] = lax.rem(rest, grid.size[n])
+            rest = lax.div(rest, grid.size[n])
+        for target, core in ((keep, digit["c"]), (give, 1 - digit["c"])):
+            spot = dict(at, c=core)
+            rank = 0
+            for n in grid.order:
+                rank = rank * grid.size[n] + spot[n]
+            target[tuple(at[n] for n in names)] = nrm[0:16, columns(lax.div(rank, per))]
+        return carry
+
+    steps = 1
+    for n in names:
+        steps *= grid.size[n]
+    lax.fori_loop(0, steps, spread, 0)
+    scatter.give(U["small"][0])
     for copy in first + second:
         copy.wait_send()
-
-
-def wkv_backward(grid, r, k, v, gate_pre, wkv, d_att, rate, reward, gain, bias, fade, begin):
-    tokens, width = r.shape
+    scatter.close()
+
+
+def backward(grid, length, table, prev, begin, stored, weights):
+    tokens, width = stored[0].shape
+    hidden = stored[11].shape[1]
+    blk, tall = weights[0].shape[4], weights[7].shape[4]
+    arrays = [
+        (tall, width, LANES, BF16), (blk, width, 512, BF16), (blk, hidden, 512, BF16), (blk, width, 512, BF16),
+        (blk, width, 512, BF16), (blk, width, 512, BF16), (blk, width, 512, BF16), (blk, width, 512, BF16),
+        (16, LANES, LANES, F32),
+    ]
+    units, of_array, counts = scatter_plan(arrays)
+    groups = list(counts)
+    kinds = {group: jnp.dtype(group[3]) for group in groups}
+    shapes = {group: stage_shapes(grid, group) for group in groups}
+    vmem = pl.BlockSpec(memory_space=pltpu.VMEM)
+    anywhere = pl.BlockSpec(memory_space=pl.ANY)
+    flat16, flat32 = pltpu.VMEM((tokens, width), BF16), pltpu.VMEM((tokens, width), F32)
     state = pltpu.VMEM((width, LANES), BF16)
     sems = pltpu.SemaphoreType.DMA((grid.seq - 1,))
-    vmem = pl.BlockSpec(memory_space=pltpu.VMEM)
-    flat = jax.ShapeDtypeStruct((tokens, width), BF16)
-    return pl.pallas_call(
-        functools.partial(wkv_backward_kernel, grid, tokens // 2),
-        out_shape=[flat, flat, flat, flat, jax.ShapeDtypeStruct((8, width), F32)],
-        in_specs=[vmem] * 12,
-        out_specs=[vmem] * 5,
-        scratch_shapes=[pltpu.VMEM((tokens, width), BF16), state, state, state, state, sems, sems, sems, sems],
+    dma = pltpu.SemaphoreType.DMA
+    count = sum(len(unit) for unit in units) * sum(size - 1 for size in grid.shape)
+    landing = [
+        jax.ShapeDtypeStruct((counts[group],) + shape, kinds[group]) for group in groups for shape in shapes[group]
+    ]
+    outs = pl.pallas_call(
+        functools.partial(backward_kernel, grid, length, units, of_array, groups),
+        out_shape=[jax.ShapeDtypeStruct((tokens, width), BF16)]
+        + [jax.ShapeDtypeStruct((a[0], a[1]), F32) for a in arrays]
+        + landing,
+        in_specs=[vmem] * 3 + [anywhere] * 22,
+        out_specs=[vmem] * (1 + len(arrays)) + [anywhere] * len(landing),
+        scratch_shapes=[pltpu.VMEM(grid.sizes("c") + p.tile, p.kind) for unit in units for p in unit]
+        + [pltpu.VMEM(shapes[group][0], kinds[group]) for group in groups]
+        + [pltpu.VMEM(shape, kinds[group]) for group in groups for shape in shapes[group]]
+        + [
+            pltpu.VMEM((tokens, hidden), BF16), flat16, flat16, pltpu.VMEM((2, tokens, width), BF16),
+            pltpu.VMEM((tokens, hidden), BF16),
+            pltpu.VMEM((2,) + grid.shape + (blk, CHUNK), BF16),
+            pltpu.VMEM(grid.shape[1:] + (tall, width), BF16),
+            flat32, flat32, flat32, flat32, flat16, flat32, flat16, flat16, flat16, flat16, flat16,
+            state, state, state, state,
+            pltpu.VMEM((LANES, LANES), F32),
+            pltpu.VMEM((14, 8, width), F32),
+            pltpu.VMEM((8, width), F32),
+            pltpu.VMEM((2, 8, width), F32),
+            dma((count,)), dma((count,)), dma((8,)), dma((12,)), dma((2,)), dma((2,)), dma((2,)),
+            sems, sems, sems, sems,
+        ],
         compiler_params=pltpu.CompilerParams(
-            collective_id=3, has_side_effects=True, vmem_limit_bytes=VMEM_LIMIT
+            collective_id=1, has_side_effects=True, vmem_limit_bytes=VMEM_LIMIT
         ),
-    )(r, k, v, gate_pre, wkv, d_att, rate, reward, gain, bias, fade, begin)
-
-
-def shifted(block, axis, distance):
-    devices = range(lax.axis_size(axis))
-    route = [(i - distance, i) for i in devices if i - distance in devices]
-    return lax.ppermute(block, axis, route)
-
-
-def standardize(rows, epsilon):
-    center = rows - jnp.mean(rows, axis=-1, keepdims=True)
-    spread = jnp.mean(center * center, axis=-1, keepdims=True)
-    scale = lax.rsqrt(spread + epsilon)
-    return center * scale, scale
-
-
-def back_standardize(e, z, scale):
-    return (e - jnp.mean(e, axis=-1, keepdims=True) - z * jnp.mean(e * z, axis=-1, keepdims=True)) * scale
-
-
-def project(rows, weights):
-    return dot(rows, weights, 1, 0)
-
-
-def outer(left_side, right_side):
-    return dot(left_side, right_side, 0, 0).astype(BF16)
-
-
-def back_through(grads, weights):
-    return dot(grads, weights, 1, 1)
+    )(table, prev, begin, *stored, *weights)
+    return outs[0], outs[1 : 1 + len(arrays)]
 
 
 def local(grid, *args):
@@ -921,7 +1281,6 @@
     tokens = segments * length
     ranks = grid.seq * grid.batch
     share = width // ranks
-    is_first = lax.axis_index("seq") == 0
 
     per = LANES // share
     rank = lax.axis_index(("seq", "batch"))
@@ -940,80 +1299,17 @@
     outs = forward(
         grid, incoming.reshape(tokens, width), upstream.reshape(tokens, width), att_entry, ffn_entry, start, shards, length
     )
-    W_k, W_v, W_r, W_g, W_o, F_r, F_k, F_v = [w.reshape((ranks * w.shape[4], w.shape[5])) for w in outs[1:9]]
     (
-        result, table, mixed, r, k, v, gate_pre, wkv, attended, begin, middle, mixed2, hidden, d_carried, d_recv, prev2,
+        result, table, mixed, r, k, v, gate_pre, wkv, attended, begin, middle, mixed2, hidden, d_carried, d_recv, prev,
     ) = outs[9:]
-    g1, b1 = table[0], table[1]
-    mix1 = table[2:6]
-    rate = jnp.exp(table[6])[None, :]
-    bonus = table[7][None, :]
-    gg, gb = table[8][None, :], table[9][None, :]
-    g2, b2 = table[10], table[11]
-    mix2 = table[12:14]
-    own_rate = lax.dynamic_slice_in_dim(rate[0], row, rows, 0)
-    fade = jnp.broadcast_to(jnp.exp(-own_rate * length)[:, None], (rows, LANES))
-    x = incoming.astype(F32)
-    z1, s1 = standardize(x, 1e-05)
-    normed = z1 * g1 + b1
-    arrived = shifted(normed[:, -1:], "seq", 1)
-    previous = jnp.where(is_first, att_entry[:, None, :].astype(F32), arrived)
-    before = jnp.concatenate([previous, normed[:, :-1]], axis=1)
-    middle = middle.reshape(segments, length, width)
-    z2, s2 = standardize(middle, 1e-05)
-    normed2 = z2 * g2 + b2
-    before2 = jnp.concatenate([prev2[:segments][:, None], normed2[:, :-1]], axis=1)
-    key_pos = jnp.sqrt(hidden.astype(F32))
-
-    d_out = upstream.astype(F32).reshape(tokens, width)
-    grad_f_value = outer(hidden, d_carried)
-    grad_f_recept = outer(mixed2[1], d_recv)
-    d_key = (2.0 * key_pos * back_through(d_carried, F_v)).astype(BF16)
-    grad_f_key = outer(mixed2[0], d_key)
-    d_mixed2 = [
-        back_through(d_key, F_k).reshape(segments, length, width),
-        back_through(d_recv, F_r).reshape(segments, length, width),
+    stored = [
+        incoming.reshape(tokens, width), upstream.reshape(tokens, width), mixed, r, k, v, gate_pre, wkv, attended, middle,
+        mixed2, hidden, d_carried, d_recv,
     ]
-    difference2 = normed2 - before2
-    d_mix2 = [jnp.sum(difference2 * d, axis=(0, 1)) for d in d_mixed2]
-    d_before2 = sum((1.0 - mix2[c]) * d_mixed2[c] for c in range(2))
-    from_next2 = shifted(d_before2[:, :1], "seq", -1)
-    d_normed2 = sum(mix2[c] * d_mixed2[c] for c in range(2)) + jnp.concatenate([d_before2[:, 1:], from_next2], axis=1)
-    d_g2 = jnp.sum(z2 * d_normed2, axis=(0, 1))
-    d_b2 = jnp.sum(d_normed2, axis=(0, 1))
-    d_middle = d_out.reshape(segments, length, width) + back_standardize(d_normed2 * g2, z2, s2)
-    d_branch = d_middle.astype(BF16).reshape(tokens, width)
-    grad_out = outer(attended, d_branch)
-    d_attended = back_through(d_branch, W_o)
-    d_gate, d_r, d_k, d_v, sums = wkv_backward(
-        grid, r, k, v, gate_pre, wkv, d_attended, rate, bonus, gg, gb, fade, begin
+    d_input, (s_fv, s_fr, s_fk, s_o, s_g, s_r, s_k, s_v, s_small) = backward(
+        grid, length, table, prev, begin, stored, outs[1:9]
     )
-    grad_r, grad_k, grad_v, grad_g = [
-        outer(m, d) for m, d in zip(mixed, (d_r, d_k, d_v, d_gate))
-    ]
-    d_mixed = [
-        back_through(d, w).reshape(segments, length, width)
-        for d, w in zip((d_r, d_k, d_v, d_gate), (W_r, W_k, W_v, W_g))
-    ]
-    difference = normed - before
-    d_mix1 = [jnp.sum(difference * d, axis=(0, 1)) for d in d_mixed]
-    d_before = sum((1.0 - mix1[c]) * d_mixed[c] for c in range(4))
-    from_next = shifted(d_before[:, :1], "seq", -1)
-    d_normed = sum(mix1[c] * d_mixed[c] for c in range(4)) + jnp.concatenate([d_before[:, 1:], from_next], axis=1)
-    d_g1 = jnp.sum(z1 * d_normed, axis=(0, 1))
-    d_b1 = jnp.sum(d_normed, axis=(0, 1))
-    d_input = (d_middle + back_standardize(d_normed * g1, z1, s1)).astype(BF16)
-
-    rows_of = [d_g1, d_b1] + d_mix1 + [sums[3], sums[2], sums[0], sums[1], d_g2, d_b2] + d_mix2
-    small_grad = jnp.stack(rows_of).reshape(14, ranks, share).transpose(1, 0, 2)
-    small_grad = jnp.pad(small_grad, ((0, 0), (0, 2), (0, LANES - share))).reshape(grid.shape + (16, LANES))
-    parts = [
-        g.reshape(grid.shape + (g.shape[0] // ranks, g.shape[1]))
-        for g in (grad_f_value, grad_f_key, grad_f_recept, grad_out, grad_g, grad_r, grad_k, grad_v)
-    ] + [small_grad]
-    chunks = [("x", "y"), ("y", "x"), ("x", "y"), ("y", "x"), ("x", "y"), ("y", "x"), ("x", "y"), ("y", "x"), ("x", "y")]
-    s_fv, s_fk, s_fr, s_o, s_g, s_r, s_k, s_v, s_small = scatter_all(grid, parts, chunks)
-    s = s_small[:14, :share]
+    s = lax.dynamic_slice_in_dim(s_small, (rank % per) * share, share, 1)
     shape = incoming.shape
     return (
         result.reshape(shape), d_input.reshape(shape),

time: 524 us -> 413 us (0.79)
  matrix products: 57.8 us -> 0 us
  other arithmetic: 21 us -> 0.61 us
  local copies, waits for them, and re-layouts: 35.3 us -> 16.5 us
  Pallas kernels: 400 us -> 391 us
  starting transfers between devices: 5.6 us -> 0 us
    dot_general x16 -> x0, matrix products: 57.8 us -> none  [dot(): lax.dot_general(a, b, (((da,), (db,)), ((), ())), preferred_element_type=...]
    reduce_sum x6 -> x0, other arithmetic: 14.6 us -> none  [the longest x1 8.04 us: local(): d_g1 = jnp.sum(z1 * d_normed, axis=(0, 1))]
    pallas_call x2 -> x1, Pallas kernels: 222 us -> 213 us  [backward(): pl.pallas_call(functools.partial(backward_kernel, grid, length, units, of...]
    another operation x15 -> x0, local copies, waits for them, and re-layouts: 5.86 us -> none  [local(): small_grad = jnp.stack(rows_of).reshape(14, ranks, share).transpose(1, 0, 2)]
    ppermute x3 -> x0, starting transfers between devices: 5.6 us -> none  [shifted(): return lax.ppermute(block, axis, route)]
    unnamed x109 -> x48, local copies, waits for them, and re-layouts: 13.6 us -> 8.84 us
  transfers between devices with their start and end apart: 3 -> 0, of which waited for: 0 -> 0; matrix products, arithmetic and copies ran while one was open for 9% -> 0% of each run, Pallas kernels for 9% -> 0%
where the time goes in v3:
time: 413 us; the launch traced here: 409 us
  Pallas kernels  391 us (95%)
  local copies, waits for them, and re-layouts  16.5 us (4%)
    pallas_call x1, Pallas kernels, backward(): pl.pallas_call(functools.partial(backward_kernel, grid, length, units, of...  213 us
    pallas_call x1, Pallas kernels, forward(): pl.pallas_call(functools.partial(forward_kernel, grid, length, plan, star...  177 us
    unnamed x48, local copies, waits for them, and re-layouts  8.84 us

profile of v3, /device:TPU:0, one launch (start us, length us, event | category | flops | bytes accessed | tf_op | source)
XLA Modules:
  0.0 409.0 jit_solution(10126017639763668580)
XLA Ops:
  0.8 2.1 copy.43
  2.9 0.6 reshape.63
  3.5 0.6 constant_dynamic-slice_fusion.refs_4_
  4.1 0.0 copy-done.9
  4.1 0.0 copy-done.11
  4.1 0.0 copy-done.12
  4.2 0.1 stack.35
  4.3 0.1 tile.10
  4.4 0.6 fusion.refs_5_
  5.0 177.4 %shard_map.374 = (bf16[2,2,2,4,16,128]{5,4,3,2,1,0:T(8,128)(2,1)}, bf16[2,2,2,4,32,1024]{5,4,3,2,1,0:T(8,128)(2,1)}, bf16[2,2,2,4,32,1024]{5,4,3,2,1,0:T(8,128)(...) custom-call(bf16[512,1024]{1,0:T(8,128)(2,1)} %bitcast.45, ...), custom_call_target="tpu_custom_call" | custom-call | tf_op jit(solution)/shard_map/pallas_call | solution.py:553
  182.4 213.5 %shard_map.375 = (bf16[512,1024]{1,0:T(8,128)(2,1)}, f32[112,1024]{1,0:T(8,128)}, f32[32,1024]{1,0:T(8,128)}, f32[32,3584]{1,0:T(8,128)}, f32[32,1024]{1,0:T(8,1...) custom-call(f32[16,1024]{1,0:T(8,128)} %get-tuple-element.55.refs_0_, ...), custom_call_target="tpu_custom_call" | custom-call | tf_op jit(solution)/shard_map/pallas_call | solution.py:1243
  395.9 1.5 dynamic-slice_bitcast_fusion.2
  397.3 1.3 dynamic-slice_bitcast_fusion
  398.7 1.3 dynamic-slice_bitcast_fusion.1
  400.0 2.3 copy.54
  402.3 1.0 copy.55
  403.3 0.7 copy.56
  404.0 0.7 copy.57
  404.6 0.7 copy.58
  405.3 0.7 copy.59
  405.9 0.7 copy.60
  406.6 0.8 copy.61
  407.4 0.8 copy.62
  408.1 0.7 copy.63
  (40 shorter events, 0.1 us)
Async XLA Ops:
  0.7 3.5 copy-start.11
  0.7 3.5 copy-start.12
  0.7 3.4 copy-start.10
  0.7 3.4 copy-start.9
  0.7 3.5 copy-start.13
  0.7 3.5 copy-start.14
  0.7 3.5 copy-start.15
  0.7 3.5 copy-start.16
  0.7 3.5 copy-start.17
  0.8 3.5 copy-start.18
  395.9 6.5 %copy-start = (bf16[512,1024]{1,0:T(8,128)(2,1)S(1)}, bf16[512,1024]{1,0:T(8,128)(2,1)}, u32[]{:S(2)}) copy-start(bf16[512,1024]{1,0:T(8,128)(2,1)} %get-tuple-element.78) | copy-start | bytes 3145732
  400.0 3.3 copy-start.8
  400.0 4.0 copy-start.7
  400.0 4.6 %copy-start.6 = (f32[32,1024]{1,0:T(8,128)S(1)}, f32[32,1024]{1,0:T(8,128)}, u32[]{:S(2)}) copy-start(f32[32,1024]{1,0:T(8,128)} %get-tuple-element.135) | copy-start | bytes 393220
  400.0 5.3 %copy-start.5 = (f32[32,1024]{1,0:T(8,128)S(1)}, f32[32,1024]{1,0:T(8,128)}, u32[]{:S(2)}) copy-start(f32[32,1024]{1,0:T(8,128)} %get-tuple-element.136) | copy-start | bytes 393220
  402.3 3.6 copy-start.4
  402.3 4.3 %copy-start.2 = (f32[32,3584]{1,0:T(8,128)S(1)}, f32[32,3584]{1,0:T(8,128)}, u32[]{:S(2)}) copy-start(f32[32,3584]{1,0:T(8,128)} %get-tuple-element.145) | copy-start | bytes 1376260
  402.3 5.0 %copy-start.1 = (f32[112,1024]{1,0:T(8,128)S(1)}, f32[112,1024]{1,0:T(8,128)}, u32[]{:S(2)}) copy-start(f32[112,1024]{1,0:T(8,128)} %get-tuple-element.146) | copy-start | bytes 1376260
  403.3 4.8 %copy-start.3 = (f32[32,1024]{1,0:T(8,128)S(1)}, f32[32,1024]{1,0:T(8,128)}, u32[]{:S(2)}) copy-start(f32[32,1024]{1,0:T(8,128)} %get-tuple-element.147) | copy-start | bytes 393220

commit v4 on v3

--- a/solution.py
+++ b/solution.py
@@ -141,7 +141,13 @@
 
 
 CHUNK = 1024
-TALL = 512
+TALL = 256
+LAGS = (0, 1, 3)
+AHEAD = 4
+PUMPS = (
+    1, 1, 1, 0, 0, 2, 0, 0, 0, 1, 0, 1, 0, 0, 0, 1, 0, 0, 0, 1, 0, 1, 0, 0, 0, 0, 1, 0, 0, 1, 0, 0, 0, 0, 0, 0, 1, 1, 0, 0, 0,
+    1, 0, 1, 0, 0, 1, 0, 0, 0,
+)
 
 
 def pieces(columns, step):
@@ -154,7 +160,7 @@
         self.shards, self.fulls, self.plan = shards, fulls, plan
         self.own_sem, self.send_sem, self.recv_sem = own_sem, send_sem, recv_sem
         self.started, self.pending, self.own = [], {}, {}
-        self.tick, self.done = 0, 0
+        self.tick, self.done, self.places = 0, 0, 0
 
     def others(self, name):
         size = self.grid.size[name]
@@ -228,11 +234,16 @@
             tick = self.tick
             self.tick += 1
             for number in (1, 2, 3):
-                self.stage(tick - (number - 1), number)
+                self.stage(tick - LAGS[number - 1], number)
             self.stage(tick + self.ahead, 0)
 
+    def point(self):
+        count = PUMPS[self.places]
+        self.places += 1
+        self.pump(count if self.tick < len(self.plan) + LAGS[2] + 1 else 0)
+
     def ready(self, piece):
-        while self.tick < piece + 3:
+        while self.tick < piece + LAGS[2] + 1:
             self.pump()
         while self.done <= piece:
             self.stage(self.done, 4)
@@ -272,15 +283,26 @@
         x_ref, up_ref, att_entry_ref, ffn_entry_ref, start_ref, *shards
     ) = refs[:14]
     fulls = refs[14:23]
+    result_ref, table_ref, begin_ref, prev_ref = refs[23:27]
+    kept = refs[27:39]
     (
-        result_ref, table_ref, mixed_ref, r_ref, k_ref, v_ref, gate_ref, wkv_ref, attended_ref, begin_ref,
-        middle_ref, mixed2_ref, hidden_ref, d_carried_ref, d_recv_ref, prev_ref,
-    ) = refs[23:39]
+        mixed_ref, r_ref, k_ref, v_ref, gate_ref, wkv_ref, attended_ref, middle_ref, mixed2_ref, hidden_ref,
+        d_carried_ref, d_recv_ref,
+    ) = places = refs[39:51]
     (
         normed_ref, wide_ref, tall_ref, small_ref, edge_ref, arrive_ref, recv_ref,
         own_ref, got_ref, out_ref, fade_ref,
-        own_sem, send_sem, recv_sem, load_sem, edge_send, edge_recv, send_a, recv_a, send_b, recv_b,
-    ) = refs[39:]
+        own_sem, send_sem, recv_sem, load_sem, save_sem, edge_send, edge_recv, send_a, recv_a, send_b, recv_b,
+    ) = refs[51:]
+    saved = []
+
+    def save(*names):
+        for name in names:
+            at = [place is name for place in places].index(True)
+            copy = pltpu.make_async_copy(name, kept[at], save_sem.at[at])
+            copy.start()
+            saved.append(copy)
+
     index, digit = grid.place()
     me = index["seq"]
     tokens, width = x_ref.shape
@@ -291,19 +313,22 @@
     peers = [grid.peer(index, digit, n, t) for n in batch_roles for t in gather.others(n)]
     peers += [(lax.rem(me + j, grid.seq), index["batch"]) for j in range(1, grid.seq)]
     greet(peers)
-    gather.open(3)
+    gather.open(AHEAD)
+    gather.point()
 
     def first_piece(array):
         return starts[array]
 
-    def load(array, piece, buffer, slot):
+    def load(piece, buffer, slot):
         gather.ready(piece)
+        array = plan[piece][0]
         column, columns = span(plan[piece])
         source = fulls[array].at[(slice(None),) * 5 + (pl.ds(column, columns),)]
         target = buffer.at[(slot,) + (slice(None),) * 5 + (pl.ds(0, columns),)]
         copy = pltpu.make_async_copy(source, target, load_sem.at[slot])
         copy.start()
-        return copy
+        gather.point()
+        copy.wait()
 
     def weight(buffer, slot, window):
         value = buffer[(slot,) + (slice(None),) * 5 + (window,)]
@@ -311,6 +336,22 @@
 
     def tile(n, step=256):
         return pl.ds(pl.multiple_of(n * step, step), step)
+
+    def norm(source_ref):
+        step = 64
+
+        def run(i, carry):
+            at = pl.ds(pl.multiple_of(i * step, step), step)
+            value = source_ref[at, :].astype(F32)
+            center = value - jnp.mean(value, axis=-1, keepdims=True)
+            spread = jnp.mean(center * center, axis=-1, keepdims=True)
+            normed_ref[at, :] = center * lax.rsqrt(spread + 1e-05)
+            return carry
+
+        lax.fori_loop(0, tokens // step, run, 0)
+
+    norm(x_ref)
+    gather.point()
 
     gather.ready(0)
     copy = pltpu.make_async_copy(fulls[0], small_ref, load_sem.at[0])
@@ -324,14 +365,14 @@
         for j in range(1, per):
             total = total + small[p * per + j]
         table_ref[:, p * LANES : (p + 1) * LANES] = total
-    gather.pump()
-
-    def shift_rows(segment, source_ref, slot, body):
+    gather.point()
+
+    def shift_rows(segment, gain, bias, slot, body):
         step = 64
 
         def run(i, carry):
             at = pl.ds(pl.multiple_of(segment * length + i * step, step), step)
-            current = source_ref[at, :]
+            current = normed_ref[at, :] * table_ref[gain : gain + 1, :] + table_ref[bias : bias + 1, :]
             row = lax.broadcasted_iota(jnp.int32, (step, 1), 0)
             previous = jnp.where(row == 0, carry, pltpu.roll(current, 1, 0))
             body(at, current, previous)
@@ -339,11 +380,12 @@
 
         lax.fori_loop(0, length // step, run, prev_ref[slot, segment : segment + 1, :])
 
-    def swap_edges(entry_ref, slot):
+    def swap_edges(entry_ref, gain, bias, slot):
         edge_ref[...] = jnp.zeros_like(edge_ref)
         for q in range(segments):
             last = (q + 1) * length
-            edge_ref[q : q + 1, :] = normed_ref[last - 8 : last, :][7:8, :]
+            row = normed_ref[last - 8 : last, :][7:8, :]
+            edge_ref[q : q + 1, :] = row * table_ref[gain : gain + 1, :] + table_ref[bias : bias + 1, :]
         copy = pltpu.make_async_remote_copy(
             src_ref=edge_ref,
             dst_ref=arrive_ref.at[slot],
@@ -353,26 +395,13 @@
             device_id_type=MESH,
         )
         copy.start()
+        gather.point()
         copy.wait()
         first = jnp.where(me == 0, 1.0, 0.0)
         prev_ref[slot] = arrive_ref[slot] * (1.0 - first)
         prev_ref[slot, 0:segments, :] += entry_ref[...].astype(F32) * first
 
-    def norm(source_ref, gain, bias):
-        step = 64
-
-        def run(i, carry):
-            at = pl.ds(pl.multiple_of(i * step, step), step)
-            value = source_ref[at, :].astype(F32)
-            center = value - jnp.mean(value, axis=-1, keepdims=True)
-            spread = jnp.mean(center * center, axis=-1, keepdims=True)
-            normed_ref[at, :] = center * lax.rsqrt(spread + 1e-05) * table_ref[gain : gain + 1, :] + table_ref[bias : bias + 1, :]
-            return carry
-
-        lax.fori_loop(0, tokens // step, run, 0)
-
-    norm(x_ref, 0, 1)
-    swap_edges(att_entry_ref, 0)
+    swap_edges(att_entry_ref, 0, 1, 0)
 
     def mix_one(at, current, previous):
         for c in range(4):
@@ -380,21 +409,27 @@
             mixed_ref[c, at, :] = (current * blend + previous * (1.0 - blend)).astype(BF16)
 
     for q in range(segments):
-        shift_rows(q, normed_ref, 0, mix_one)
+        shift_rows(q, 0, 1, 0, mix_one)
+        gather.point()
+    save(mixed_ref)
 
     def project_to(array, slot, left, target_ref):
-        copy = load(array, first_piece(array), wide_ref, slot)
-        copy.wait()
-
-        def run(n, carry):
-            value = dot(left[...], weight(wide_ref, slot, tile(n)), 1, 0)
-            target_ref[:, tile(n)] = value.astype(target_ref.dtype)
-            return carry
-
-        lax.fori_loop(0, width // 256, run, 0)
+        for number, piece in enumerate(range(starts[array], starts[array + 1])):
+            column, size = span(plan[piece])
+            here = (slot + number) % 2
+            load(piece, wide_ref, here)
+
+            def run(n, carry, column=column, here=here):
+                value = dot(left[...], weight(wide_ref, here, tile(n)), 1, 0)
+                target_ref[:, pl.ds(pl.multiple_of(column + n * 256, 256), 256)] = value.astype(target_ref.dtype)
+                return carry
+
+            lax.fori_loop(0, size // 256, run, 0)
+            gather.point()
 
     project_to(1, 0, mixed_ref.at[1], k_ref)
     project_to(2, 1, mixed_ref.at[2], v_ref)
+    save(k_ref, v_ref)
     ones, ones16 = block_ones(F32), block_ones(BF16)
     group = lax.div(me * rows, LANES)
     own_log = table_ref[6:7, pl.ds(pl.multiple_of(group * LANES, LANES), LANES)]
@@ -418,8 +453,10 @@
 
     lax.fori_loop(0, pairs, own_states, 0)
     first = exchange(grid, index, own_ref, got_ref, rows, send_a, recv_a)
+    gather.point()
     project_to(3, 0, mixed_ref.at[0], r_ref)
     project_to(4, 1, mixed_ref.at[3], gate_ref)
+    save(r_ref, gate_ref)
     for copy in first:
         copy.wait_recv()
     state = start_ref[...]
@@ -429,7 +466,7 @@
         out_ref[at, :] = state.astype(BF16)
         state = fade * state + got_ref[at, :].astype(F32)
     second = exchange(grid, index, out_ref, begin_ref, rows, send_b, recv_b)
-    gather.pump()
+    gather.point()
 
     later = lax.broadcasted_iota(jnp.int32, (length, length), 0) > lax.broadcasted_iota(
         jnp.int32, (length, length), 1
@@ -467,12 +504,12 @@
             attended_ref[token, columns(p)] = (normalized * g / (1.0 + jnp.exp(-g))).astype(BF16)
         return carry
 
-    for quarter in range(4):
-        lax.fori_loop(quarter * pairs // 4, (quarter + 1) * pairs // 4, inside, 0)
-        gather.pump()
-
-    copy = load(5, first_piece(5), wide_ref, 0)
-    copy.wait()
+    for p in range(pairs):
+        lax.fori_loop(p, p + 1, inside, 0)
+        gather.point()
+    save(wkv_ref, attended_ref)
+
+    load(first_piece(5), wide_ref, 0)
 
     def out_project(n, carry):
         value = dot(attended_ref[...], weight(wide_ref, 0, tile(n)), 1, 0)
@@ -480,8 +517,11 @@
         return carry
 
     lax.fori_loop(0, width // 256, out_project, 0)
-    norm(middle_ref, 10, 11)
-    swap_edges(ffn_entry_ref, 1)
+    save(middle_ref)
+    gather.point()
+    norm(middle_ref)
+    gather.point()
+    swap_edges(ffn_entry_ref, 10, 11, 1)
 
     def mix_two(at, current, previous):
         for c in range(2):
@@ -489,9 +529,10 @@
             mixed2_ref[c, at, :] = (current * blend + previous * (1.0 - blend)).astype(BF16)
 
     for q in range(segments):
-        shift_rows(q, normed_ref, 1, mix_two)
-    copy = load(6, first_piece(6), wide_ref, 1)
-    copy.wait()
+        shift_rows(q, 10, 11, 1, mix_two)
+        gather.point()
+    save(mixed2_ref)
+    load(first_piece(6), wide_ref, 1)
 
     def receive(n, carry):
         value = dot(mixed2_ref[1], weight(wide_ref, 1, tile(n)), 1, 0)
@@ -501,12 +542,13 @@
         return carry
 
     lax.fori_loop(0, width // 256, receive, 0)
+    save(d_carried_ref)
+    gather.point()
 
     for piece in range(starts[7], starts[8]):
         slot = (piece - starts[7]) % 2
         column, size = span(plan[piece])
-        copy = load(7, piece, wide_ref, slot)
-        copy.wait()
+        load(piece, wide_ref, slot)
 
         def key(n, carry):
             value = jnp.maximum(dot(mixed2_ref[0], weight(wide_ref, slot, tile(n)), 1, 0), 0.0)
@@ -514,11 +556,12 @@
             return carry
 
         lax.fori_loop(0, size // 256, key, 0)
+        gather.point()
+    save(hidden_ref)
     for piece in range(starts[8], len(plan)):
         slot = (piece - starts[8]) % 2
         column, size = span(plan[piece])
-        copy = load(8, piece, tall_ref, slot)
-        copy.wait()
+        load(piece, tall_ref, slot)
         window = pl.ds(column, size)
 
         def carry_out(m, carry):
@@ -531,37 +574,44 @@
             return carry
 
         lax.fori_loop(0, tokens // 256, carry_out, 0)
-
+        gather.point()
+
+    save(d_recv_ref)
     for copy in first + second:
         copy.wait_send()
     gather.close()
+    for copy in saved:
+        copy.wait()
 
 
 def forward(grid, x, upstream, att_entry, ffn_entry, start, shards, length):
     tokens, width = x.shape
-    steps = [LANES] + [CHUNK] * 7 + [TALL]
+    steps = [LANES, CHUNK // 2] + [CHUNK] * 6 + [TALL]
     plan, starts = gather_plan([(s.shape[1], step) for s, step in zip(shards, steps)])
     total = sum(len(unit[1]) for unit in plan)
     hidden = shards[7].shape[1]
     vmem = pl.BlockSpec(memory_space=pltpu.VMEM)
     anywhere = pl.BlockSpec(memory_space=pl.ANY)
     flat = jax.ShapeDtypeStruct((tokens, width), BF16)
-    flat32 = jax.ShapeDtypeStruct((tokens, width), F32)
     state = pltpu.VMEM((width, LANES), BF16)
     sems = pltpu.SemaphoreType.DMA((grid.seq - 1,))
     count = total * sum(size - 1 for size in grid.shape)
+    kept = [
+        ((4, tokens, width), BF16), ((tokens, width), BF16), ((tokens, width), BF16), ((tokens, width), BF16),
+        ((tokens, width), F32), ((tokens, width), BF16), ((tokens, width), BF16), ((tokens, width), F32),
+        ((2, tokens, width), BF16), ((tokens, hidden), BF16), ((tokens, width), BF16), ((tokens, width), BF16),
+    ]
     return pl.pallas_call(
         functools.partial(forward_kernel, grid, length, plan, starts),
         out_shape=[jax.ShapeDtypeStruct(grid.shape + s.shape, s.dtype) for s in shards]
         + [
-            flat, jax.ShapeDtypeStruct((16, width), F32), jax.ShapeDtypeStruct((4, tokens, width), BF16),
-            flat, flat, flat, flat32, flat, flat, jax.ShapeDtypeStruct((width, LANES), BF16),
-            flat32, jax.ShapeDtypeStruct((2, tokens, width), BF16), jax.ShapeDtypeStruct((tokens, hidden), BF16),
-            flat, flat, jax.ShapeDtypeStruct((2, 8, width), F32),
-        ],
+            flat, jax.ShapeDtypeStruct((16, width), F32), jax.ShapeDtypeStruct((width, LANES), BF16),
+            jax.ShapeDtypeStruct((2, 8, width), F32),
+        ]
+        + [jax.ShapeDtypeStruct(*entry) for entry in kept],
         in_specs=[vmem] * 5 + [anywhere] * 9,
-        out_specs=[anywhere] * 9 + [vmem] * 16,
-        scratch_shapes=[
+        out_specs=[anywhere] * 9 + [vmem] * 4 + [anywhere] * len(kept),
+        scratch_shapes=[pltpu.VMEM(*entry) for entry in kept] + [
             pltpu.VMEM((tokens, width), F32),
             pltpu.VMEM((2,) + grid.shape + (shards[1].shape[0], CHUNK), BF16),
             pltpu.VMEM((2,) + grid.shape + (shards[8].shape[0], TALL), BF16),
@@ -575,6 +625,7 @@
             pltpu.SemaphoreType.DMA((count,)),
             pltpu.SemaphoreType.DMA((count,)),
             pltpu.SemaphoreType.DMA((2,)),
+            pltpu.SemaphoreType.DMA((len(kept),)),
             pltpu.SemaphoreType.DMA((2,)),
             pltpu.SemaphoreType.DMA((2,)),
             sems, sems, sems, sems,
@@ -587,6 +638,8 @@
 
 STAGES = ("c", "first", "second", "z")
 GAPS = (1, 2, 2, 2)
+SLOTS = (1, 1, 1, 1)
+TICKS = (0, 0, 1, 1, 1, 1, 0, 0, 1, 1, 0, 0, 0, 1, 0, 0, 0, 0, 0, 1, 0, 0, 1, 0, 0, 0, 0, 0, 1, 1, 0, 0, 0, 1, 0, 0, 1, 1, 0, 0, 1, 1, 2, 0, 1, 1, 1, 2)
 
 
 class Piece:
@@ -635,7 +688,7 @@
         self.keeps, self.gives, self.landings, self.loads, self.outs = keeps, gives, landings, loads, outs
         self.send_sem, self.recv_sem, self.load_sem = send_sem, recv_sem, load_sem
         self.started, self.pending, self.giving = [], {}, {}
-        self.stage, self.when, self.now = {}, {}, 0
+        self.stage, self.when, self.now, self.reading, self.places = {}, {}, 0, [], 0
 
     def copy(self, source, target, name, digit):
         slot = len(self.started)
@@ -667,21 +720,21 @@
             self.pending[unit, number] = [copy]
         self.stage[unit], self.when[unit] = 0, self.now
 
-    def load(self, unit, number):
+    def load(self, unit, number, slot):
         piece, stage = self.units[unit][number], self.stage[unit]
         for copy in self.pending[unit, number]:
             copy.wait_recv()
         copy = pltpu.make_async_copy(
             self.landings[piece.group][stage].at[piece.place],
-            self.loads[piece.group][stage],
-            self.load_sem.at[2 * stage + number],
+            self.loads[piece.group][stage].at[slot],
+            self.load_sem.at[2 * (sum(SLOTS[:stage]) + slot) + number],
         )
         copy.start()
         return copy
 
-    def add(self, unit, number, copy):
+    def add(self, unit, number, slot, copy):
         piece, stage = self.units[unit][number], self.stage[unit]
-        keep, got = self.keeps[unit, number], self.loads[piece.group][stage]
+        keep, got = self.keeps[unit, number], self.loads[piece.group][stage].at[slot]
         names = [n for n in self.grid.order if n != "c"]
         fixed = ((), (piece.first,), (piece.first, piece.second), ("x", "y", "z"))[stage]
         free = [n for n in names if n not in fixed]
@@ -721,28 +774,35 @@
             copies.append(self.copy(source, self.landings[piece.group][stage + 1].at[piece.place, j - 1], name, target))
         self.pending[unit, number] = copies
 
-    def tick(self, gaps=GAPS):
-        work = []
-        for stage in (3, 2, 1, 0):
-            waiting = [u for u in sorted(self.stage) if self.stage[u] == stage]
-            if waiting and self.now - self.when[waiting[0]] >= gaps[stage]:
-                work.append(waiting[0])
-        copies = {}
-        for unit in work:
-            for number in range(len(self.units[unit])):
-                copies[unit, number] = self.load(unit, number)
-        for unit in work:
-            for number in range(len(self.units[unit])):
-                self.add(unit, number, copies[unit, number])
+    def finish(self):
+        for unit, slot, copies in self.reading:
+            for number, copy in enumerate(copies):
+                self.add(unit, number, slot, copy)
             self.stage[unit] += 1
             self.when[unit] = self.now
             if self.stage[unit] == 4:
                 del self.stage[unit]
+        self.reading = []
+
+    def tick(self, stages=(3, 2, 1, 0), gaps=GAPS):
         self.now += 1
+        self.finish()
+        for stage in stages:
+            waiting = [u for u in sorted(self.stage) if self.stage[u] == stage and self.now - self.when[u] >= gaps[stage]]
+            for slot, unit in enumerate(waiting[: SLOTS[stage]]):
+                copies = [self.load(unit, number, slot) for number in range(len(self.units[unit]))]
+                self.reading.append((unit, slot, copies))
+
+    def point(self):
+        count = TICKS[self.places]
+        self.places += 1
+        for _ in range(count):
+            self.tick()
 
     def close(self):
         while self.stage:
-            self.tick((1, 1, 1, 1))
+            self.tick(gaps=(1, 1, 1, 1))
+            self.finish()
         for copy, waiting in self.started:
             if waiting:
                 copy.wait_send()
@@ -857,7 +917,7 @@
     have("hid", "dc")
     for unit in U["fv"]:
         gradient(unit, hid, dc)
-        scatter.tick()
+        scatter.point()
     span = hid.shape[1] // n0
     loading = weight_load(f_r, 0, width, 0)
     for y in range(n0):
@@ -873,12 +933,14 @@
         lax.fori_loop(0, tokens // 128, key, 0)
         if y + 1 < n0:
             fetch("tall", f_v.at[y + 1], tall, 2)
+        if y < 2:
+            scatter.point()
     have("m2", "dr")
     gradient(U["fr"][0], m2.at[1], dr)
     fetch("mx0", mixed_hbm.at[0], hid.at[:, pl.ds(0, width)], 0)
     fetch("mx1", mixed_hbm.at[1], hid.at[:, pl.ds(width, width)], 1)
     fetch("mx2", mixed_hbm.at[2], hid.at[:, pl.ds(2 * width, width)], 2)
-    scatter.tick()
+    scatter.point()
     loading.wait()
     chunks = pieces(hid.shape[1], CHUNK)
     loading = weight_load(f_k, *chunks[0], 1)
@@ -889,8 +951,10 @@
         return carry
 
     lax.fori_loop(0, tokens // 256, through_recv, 0)
+    scatter.point()
     for number, unit in enumerate(U["fk"]):
         gradient(unit, m2.at[0], dkey)
+        scatter.point()
         column, columns = chunks[number]
         slot = (number + 1) % 2
         loading.wait()
@@ -904,7 +968,7 @@
             return carry
 
         lax.fori_loop(0, tokens // 256, through_key, 0)
-        scatter.tick()
+        scatter.point()
     fetch("mx3", mixed_hbm.at[3], m2.at[0], 3)
     loading = weight_load(w_o, 0, width, 0)
 
@@ -962,9 +1026,11 @@
                 return before[0:1, :]
 
             lax.fori_loop(0, count, run, arrive_ref[slot, q : q + 1, :] * keep_next)
+            scatter.point()
 
     have("mid")
     norm(mid, 10, 11)
+    scatter.point()
     for q in range(segments):
 
         def blend_two(i, carry, q=q):
@@ -981,8 +1047,9 @@
             return current[step - 1 : step, :]
 
         lax.fori_loop(0, length // step, blend_two, prev_ref[1, q : q + 1, :])
+        scatter.point()
     moving = swap_edges(0)
-    scatter.tick()
+    scatter.point()
     have("up")
     moving.wait()
 
@@ -995,6 +1062,7 @@
     fetch("up", x_hbm, up, 6)
     have("att")
     gradient(U["o"][0], dgate, dr)
+    scatter.point()
     loading.wait()
 
     def through_out(m, carry):
@@ -1003,7 +1071,7 @@
         return carry
 
     lax.fori_loop(0, tokens // 256, through_out, 0)
-    scatter.tick()
+    scatter.point()
 
     ones, ones16 = block_ones(F32), block_ones(BF16)
     share = 1.0 / SUBSPACE_EXTENT
@@ -1048,11 +1116,13 @@
         own_ref[columns(p), :] = fold(both[0], both[1], ones).astype(BF16)
         return carry
 
-    lax.fori_loop(0, pairs, own_states, 0)
+    for quarter in range(4):
+        lax.fori_loop(quarter * pairs // 4, (quarter + 1) * pairs // 4, own_states, 0)
+        scatter.point()
     first = exchange(grid, index, own_ref, got_ref, rows, send_a, recv_a)
     have("mx3")
     gradient(U["g"][0], m2.at[0], dgate)
-    scatter.tick()
+    scatter.point()
     for copy in first:
         copy.wait_recv()
     fade = fade_ref[pl.ds(pl.multiple_of(lax.rem(me * rows, LANES), rows), rows), :]
@@ -1062,8 +1132,10 @@
         out_ref[at, :] = state.astype(BF16)
         state = fade * state + got_ref[at, :].astype(F32)
     second = exchange(grid, index, out_ref, end_ref, rows, send_b, recv_b)
+    scatter.point()
     have("up")
     norm(up, 0, 1)
+    scatter.point()
     have("kk", "vv")
     for copy in second:
         copy.wait_recv()
@@ -1125,9 +1197,9 @@
         acc[6, 0:1, columns(p)] = rate_sum * rate
         return carry
 
-    for quarter in range(4):
-        lax.fori_loop(quarter * pairs // 4, (quarter + 1) * pairs // 4, inside, 0)
-        scatter.tick()
+    for p in range(pairs):
+        lax.fori_loop(p, p + 1, inside, 0)
+        scatter.point()
     have("mx0", "mx1", "mx2")
     weights = (w_r, w_k, w_v, w_g)
     grads = [dkey.at[:, pl.ds(c * width, width)] for c in range(3)] + [dgate]
@@ -1143,7 +1215,7 @@
     loading = load_rows(0)
     for c, name in enumerate("rkv"):
         gradient(U[name][0], hid.at[:, pl.ds(c * width, width)], grads[c])
-    scatter.tick()
+        scatter.point()
     span = width // n0
     for y in range(n0):
         for copy in loading:
@@ -1175,15 +1247,17 @@
         lax.fori_loop(0, tokens // 128, through_mix, 0)
         if y + 1 < n0:
             loading = load_rows(y + 1)
-        scatter.tick()
+        if y < 2:
+            scatter.point()
     moving = swap_edges(1)
-    scatter.tick()
+    scatter.point()
     moving.wait()
 
     def put_input(at, value):
-        d_input_ref[at, :] = value.astype(BF16)
+        dr[at, :] = value.astype(BF16)
 
     norm_back(up, 0, 1, 1, dmid, put_input)
+    fetch("result", dr, d_input_ref, 4)
 
     sums = [jnp.sum(acc[i], axis=0, keepdims=True) for i in range(14)]
     for i in range(14):
@@ -1212,9 +1286,11 @@
         steps *= grid.size[n]
     lax.fori_loop(0, steps, spread, 0)
     scatter.give(U["small"][0])
+    scatter.point()
     for copy in first + second:
         copy.wait_send()
     scatter.close()
+    have("result")
 
 
 def backward(grid, length, table, prev, begin, stored, weights):
@@ -1246,10 +1322,10 @@
         + [jax.ShapeDtypeStruct((a[0], a[1]), F32) for a in arrays]
         + landing,
         in_specs=[vmem] * 3 + [anywhere] * 22,
-        out_specs=[vmem] * (1 + len(arrays)) + [anywhere] * len(landing),
+        out_specs=[anywhere] + [vmem] * len(arrays) + [anywhere] * len(landing),
         scratch_shapes=[pltpu.VMEM(grid.sizes("c") + p.tile, p.kind) for unit in units for p in unit]
         + [pltpu.VMEM(shapes[group][0], kinds[group]) for group in groups]
-        + [pltpu.VMEM(shape, kinds[group]) for group in groups for shape in shapes[group]]
+        + [pltpu.VMEM((slots,) + shape, kinds[group]) for group in groups for slots, shape in zip(SLOTS, shapes[group])]
         + [
             pltpu.VMEM((tokens, hidden), BF16), flat16, flat16, pltpu.VMEM((2, tokens, width), BF16),
             pltpu.VMEM((tokens, hidden), BF16),
@@ -1261,7 +1337,7 @@
             pltpu.VMEM((14, 8, width), F32),
             pltpu.VMEM((8, width), F32),
             pltpu.VMEM((2, 8, width), F32),
-            dma((count,)), dma((count,)), dma((8,)), dma((12,)), dma((2,)), dma((2,)), dma((2,)),
+            dma((count,)), dma((count,)), dma((2 * sum(SLOTS),)), dma((12,)), dma((2,)), dma((2,)), dma((2,)),
             sems, sems, sems, sems,
         ],
         compiler_params=pltpu.CompilerParams(
@@ -1300,7 +1376,7 @@
         grid, incoming.reshape(tokens, width), upstream.reshape(tokens, width), att_entry, ffn_entry, start, shards, length
     )
     (
-        result, table, mixed, r, k, v, gate_pre, wkv, attended, begin, middle, mixed2, hidden, d_carried, d_recv, prev,
+        result, table, begin, prev, mixed, r, k, v, gate_pre, wkv, attended, middle, mixed2, hidden, d_carried, d_recv,
     ) = outs[9:]
     stored = [
         incoming.reshape(tokens, width), upstream.reshape(tokens, width), mixed, r, k, v, gate_pre, wkv, attended, middle,

time: 413 us -> 360 us (0.87)
  Pallas kernels: 391 us -> 336 us
    pallas_call x1, Pallas kernels: 213 us -> 180 us  [backward(): pl.pallas_call(functools.partial(backward_kernel, grid, length, units, of...]
    pallas_call x1, Pallas kernels: 177 us -> 156 us  [forward(): pl.pallas_call(functools.partial(forward_kernel, grid, length, plan, star...]
where the time goes in v4:
time: 360 us; the launch traced here: 354 us
  Pallas kernels  336 us (93%)
  local copies, waits for them, and re-layouts  16.5 us (5%)
    pallas_call x1, Pallas kernels, backward(): pl.pallas_call(functools.partial(backward_kernel, grid, length, units, of...  180 us
    pallas_call x1, Pallas kernels, forward(): pl.pallas_call(functools.partial(forward_kernel, grid, length, plan, star...  156 us
    unnamed x48, local copies, waits for them, and re-layouts  8.84 us

profile of v4, /device:TPU:0, one launch (start us, length us, event | category | flops | bytes accessed | tf_op | source)
XLA Modules:
  0.0 354.4 jit_solution(15366336229908949437)
XLA Ops:
  0.8 2.1 copy.43
  2.9 0.6 reshape.63
  3.5 0.6 constant_dynamic-slice_fusion.refs_4_
  4.1 0.0 copy-done.10
  4.2 0.1 stack.35
  4.3 0.1 tile.10
  4.4 0.6 fusion.refs_5_
  5.0 156.3 %shard_map.374 = (bf16[2,2,2,4,16,128]{5,4,3,2,1,0:T(8,128)(2,1)}, bf16[2,2,2,4,32,1024]{5,4,3,2,1,0:T(8,128)(2,1)}, bf16[2,2,2,4,32,1024]{5,4,3,2,1,0:T(8,128)(...) custom-call(bf16[512,1024]{1,0:T(8,128)(2,1)} %bitcast.45, ...), custom_call_target="tpu_custom_call" | custom-call | tf_op jit(solution)/shard_map/pallas_call | solution.py:604
  161.3 179.7 %shard_map.375 = (bf16[512,1024]{1,0:T(8,128)(2,1)}, f32[112,1024]{1,0:T(8,128)}, f32[32,1024]{1,0:T(8,128)}, f32[32,3584]{1,0:T(8,128)}, f32[32,1024]{1,0:T(8,1...) custom-call(f32[16,1024]{1,0:T(8,128)} %get-tuple-element.55.refs_0_, ...), custom_call_target="tpu_custom_call" | custom-call | tf_op jit(solution)/shard_map/pallas_call | solution.py:1319
  341.1 1.5 dynamic-slice_bitcast_fusion.2
  342.5 1.3 dynamic-slice_bitcast_fusion
  343.9 1.3 dynamic-slice_bitcast_fusion.1
  345.2 2.3 copy.54
  347.5 1.0 copy.55
  348.5 0.7 copy.56
  349.2 0.0 copy-done.7
  349.2 0.7 copy.57
  349.8 0.0 copy-done.6
  349.8 0.7 copy.58
  350.5 0.7 copy.59
  351.1 0.7 copy.60
  351.8 0.8 copy.61
  352.6 0.8 copy.62
  353.3 0.7 copy.63
  (40 shorter events, 0.1 us)
Async XLA Ops:
  0.7 3.5 copy-start.11
  0.7 3.5 copy-start.12
  0.7 3.4 copy-start.10
  0.7 3.4 copy-start.9
  0.7 3.5 copy-start.13
  0.7 3.5 copy-start.14
  0.7 3.5 copy-start.15
  0.7 3.5 copy-start.16
  0.7 3.5 copy-start.17
  0.8 3.5 copy-start.18
  341.1 6.5 %copy-start = (bf16[512,1024]{1,0:T(8,128)(2,1)S(1)}, bf16[512,1024]{1,0:T(8,128)(2,1)}, u32[]{:S(2)}) copy-start(bf16[512,1024]{1,0:T(8,128)(2,1)} %get-tuple-element.78) | copy-start | bytes 3145732
  345.2 3.3 copy-start.8
  345.2 4.0 %copy-start.7 = (f32[32,1024]{1,0:T(8,128)S(1)}, f32[32,1024]{1,0:T(8,128)}, u32[]{:S(2)}) copy-start(f32[32,1024]{1,0:T(8,128)} %get-tuple-element.134) | copy-start | bytes 393220
  345.2 4.6 %copy-start.6 = (f32[32,1024]{1,0:T(8,128)S(1)}, f32[32,1024]{1,0:T(8,128)}, u32[]{:S(2)}) copy-start(f32[32,1024]{1,0:T(8,128)} %get-tuple-element.135) | copy-start | bytes 393220
  345.2 5.3 %copy-start.5 = (f32[32,1024]{1,0:T(8,128)S(1)}, f32[32,1024]{1,0:T(8,128)}, u32[]{:S(2)}) copy-start(f32[32,1024]{1,0:T(8,128)} %get-tuple-element.136) | copy-start | bytes 393220
  347.5 3.6 %copy-start.4 = (f32[32,1024]{1,0:T(8,128)S(1)}, f32[32,1024]{1,0:T(8,128)}, u32[]{:S(2)}) copy-start(f32[32,1024]{1,0:T(8,128)} %get-tuple-element.141) | copy-start | bytes 393220
  347.5 4.3 %copy-start.2 = (f32[32,3584]{1,0:T(8,128)S(1)}, f32[32,3584]{1,0:T(8,128)}, u32[]{:S(2)}) copy-start(f32[32,3584]{1,0:T(8,128)} %get-tuple-element.145) | copy-start | bytes 1376260
  347.5 5.0 %copy-start.1 = (f32[112,1024]{1,0:T(8,128)S(1)}, f32[112,1024]{1,0:T(8,128)}, u32[]{:S(2)}) copy-start(f32[112,1024]{1,0:T(8,128)} %get-tuple-element.146) | copy-start | bytes 1376260
  348.5 4.8 %copy-start.3 = (f32[32,1024]{1,0:T(8,128)S(1)}, f32[32,1024]{1,0:T(8,128)}, u32[]{:S(2)}) copy-start(f32[32,1024]{1,0:T(8,128)} %get-tuple-element.147) | copy-start | bytes 393220

commit v5 on v4

--- a/solution.py
+++ b/solution.py
@@ -145,8 +145,8 @@
 LAGS = (0, 1, 3)
 AHEAD = 4
 PUMPS = (
-    1, 1, 1, 0, 0, 2, 0, 0, 0, 1, 0, 1, 0, 0, 0, 1, 0, 0, 0, 1, 0, 1, 0, 0, 0, 0, 1, 0, 0, 1, 0, 0, 0, 0, 0, 0, 1, 1, 0, 0, 0,
-    1, 0, 1, 0, 0, 1, 0, 0, 0,
+    0, 0, 1, 0, 0, 0, 2, 0, 0, 0, 0, 0, 1, 0, 0, 0, 0, 1, 0, 1, 0, 0, 1, 0, 0, 0, 0, 1, 1, 0, 0, 0, 1, 0, 1, 1, 0, 0, 0, 0,
+    1, 0, 0, 0, 1, 0, 0, 0, 0, 0,
 )
 
 
@@ -282,7 +282,7 @@
     (
         x_ref, up_ref, att_entry_ref, ffn_entry_ref, start_ref, *shards
     ) = refs[:14]
-    fulls = refs[14:23]
+    stored = refs[14:23]
     result_ref, table_ref, begin_ref, prev_ref = refs[23:27]
     kept = refs[27:39]
     (
@@ -290,10 +290,11 @@
         d_carried_ref, d_recv_ref,
     ) = places = refs[39:51]
     (
-        normed_ref, wide_ref, tall_ref, small_ref, edge_ref, arrive_ref, recv_ref,
+        normed_ref, edge_ref, arrive_ref, recv_ref,
         own_ref, got_ref, out_ref, fade_ref,
-        own_sem, send_sem, recv_sem, load_sem, save_sem, edge_send, edge_recv, send_a, recv_a, send_b, recv_b,
-    ) = refs[51:]
+        own_sem, send_sem, recv_sem, store_sem, save_sem, edge_send, edge_recv, send_a, recv_a, send_b, recv_b,
+    ) = refs[60:]
+    fulls = refs[51:60]
     saved = []
 
     def save(*names):
@@ -319,19 +320,18 @@
     def first_piece(array):
         return starts[array]
 
-    def load(piece, buffer, slot):
-        gather.ready(piece)
-        array = plan[piece][0]
-        column, columns = span(plan[piece])
-        source = fulls[array].at[(slice(None),) * 5 + (pl.ds(column, columns),)]
-        target = buffer.at[(slot,) + (slice(None),) * 5 + (pl.ds(0, columns),)]
-        copy = pltpu.make_async_copy(source, target, load_sem.at[slot])
+    def await_unit(unit):
+        gather.ready(unit)
+        array = plan[unit][0]
+        column, columns = span(plan[unit])
+        window = (slice(None),) * 5 + (pl.ds(column, columns),)
+        copy = pltpu.make_async_copy(fulls[array].at[window], stored[array].at[window], store_sem.at[unit])
         copy.start()
+        saved.append(copy)
         gather.point()
-        copy.wait()
-
-    def weight(buffer, slot, window):
-        value = buffer[(slot,) + (slice(None),) * 5 + (window,)]
+
+    def weight(array, window):
+        value = fulls[array][(slice(None),) * 5 + (window,)]
         return value.reshape((-1, value.shape[-1]))
 
     def tile(n, step=256):
@@ -354,11 +354,8 @@
     gather.point()
 
     gather.ready(0)
-    copy = pltpu.make_async_copy(fulls[0], small_ref, load_sem.at[0])
-    copy.start()
-    copy.wait()
     ranks = grid.seq * grid.batch
-    small = small_ref[...].astype(F32).reshape((ranks, 16, LANES))
+    small = fulls[0][...].astype(F32).reshape((ranks, 16, LANES))
     per = ranks // pairs
     for p in range(pairs):
         total = small[p * per]
@@ -413,22 +410,24 @@
         gather.point()
     save(mixed_ref)
 
-    def project_to(array, slot, left, target_ref):
-        for number, piece in enumerate(range(starts[array], starts[array + 1])):
-            column, size = span(plan[piece])
-            here = (slot + number) % 2
-            load(piece, wide_ref, here)
-
-            def run(n, carry, column=column, here=here):
-                value = dot(left[...], weight(wide_ref, here, tile(n)), 1, 0)
-                target_ref[:, pl.ds(pl.multiple_of(column + n * 256, 256), 256)] = value.astype(target_ref.dtype)
+    def shifted_tile(column, n):
+        return pl.ds(pl.multiple_of(column + n * 256, 256), 256)
+
+    def project_to(array, left, target_ref):
+        for unit in range(starts[array], starts[array + 1]):
+            await_unit(unit)
+            column, size = span(plan[unit])
+
+            def run(n, carry, column=column):
+                window = shifted_tile(column, n)
+                target_ref[:, window] = dot(left[...], weight(array, window), 1, 0).astype(target_ref.dtype)
                 return carry
 
             lax.fori_loop(0, size // 256, run, 0)
             gather.point()
 
-    project_to(1, 0, mixed_ref.at[1], k_ref)
-    project_to(2, 1, mixed_ref.at[2], v_ref)
+    project_to(1, mixed_ref.at[1], k_ref)
+    project_to(2, mixed_ref.at[2], v_ref)
     save(k_ref, v_ref)
     ones, ones16 = block_ones(F32), block_ones(BF16)
     group = lax.div(me * rows, LANES)
@@ -454,8 +453,8 @@
     lax.fori_loop(0, pairs, own_states, 0)
     first = exchange(grid, index, own_ref, got_ref, rows, send_a, recv_a)
     gather.point()
-    project_to(3, 0, mixed_ref.at[0], r_ref)
-    project_to(4, 1, mixed_ref.at[3], gate_ref)
+    project_to(3, mixed_ref.at[0], r_ref)
+    project_to(4, mixed_ref.at[3], gate_ref)
     save(r_ref, gate_ref)
     for copy in first:
         copy.wait_recv()
@@ -509,10 +508,10 @@
         gather.point()
     save(wkv_ref, attended_ref)
 
-    load(first_piece(5), wide_ref, 0)
+    await_unit(first_piece(5))
 
     def out_project(n, carry):
-        value = dot(attended_ref[...], weight(wide_ref, 0, tile(n)), 1, 0)
+        value = dot(attended_ref[...], weight(5, tile(n)), 1, 0)
         middle_ref[:, tile(n)] = x_ref[:, tile(n)].astype(F32) + value
         return carry
 
@@ -532,10 +531,10 @@
         shift_rows(q, 10, 11, 1, mix_two)
         gather.point()
     save(mixed2_ref)
-    load(first_piece(6), wide_ref, 1)
+    await_unit(first_piece(6))
 
     def receive(n, carry):
-        value = dot(mixed2_ref[1], weight(wide_ref, 1, tile(n)), 1, 0)
+        value = dot(mixed2_ref[1], weight(6, tile(n)), 1, 0)
         recv = 1.0 / (1.0 + jnp.exp(-value))
         recv_ref[:, tile(n)] = recv
         d_carried_ref[:, tile(n)] = (recv * up_ref[:, tile(n)].astype(F32)).astype(BF16)
@@ -546,27 +545,26 @@
     gather.point()
 
     for piece in range(starts[7], starts[8]):
-        slot = (piece - starts[7]) % 2
         column, size = span(plan[piece])
-        load(piece, wide_ref, slot)
-
-        def key(n, carry):
-            value = jnp.maximum(dot(mixed2_ref[0], weight(wide_ref, slot, tile(n)), 1, 0), 0.0)
-            hidden_ref[:, pl.ds(pl.multiple_of(column + n * 256, 256), 256)] = (value * value).astype(BF16)
+        await_unit(piece)
+
+        def key(n, carry, column=column):
+            window = shifted_tile(column, n)
+            value = jnp.maximum(dot(mixed2_ref[0], weight(7, window), 1, 0), 0.0)
+            hidden_ref[:, window] = (value * value).astype(BF16)
             return carry
 
         lax.fori_loop(0, size // 256, key, 0)
         gather.point()
     save(hidden_ref)
     for piece in range(starts[8], len(plan)):
-        slot = (piece - starts[8]) % 2
         column, size = span(plan[piece])
-        load(piece, tall_ref, slot)
+        await_unit(piece)
         window = pl.ds(column, size)
 
         def carry_out(m, carry):
             at = tile(m, 256)
-            carried = dot(hidden_ref[at, :], weight(tall_ref, slot, pl.ds(0, size)), 1, 0)
+            carried = dot(hidden_ref[at, :], weight(8, window), 1, 0)
             recv = recv_ref[at, window]
             result_ref[at, window] = (middle_ref[at, window] + recv * carried).astype(BF16)
             upstream = up_ref[at, window].astype(F32)
@@ -611,11 +609,10 @@
         + [jax.ShapeDtypeStruct(*entry) for entry in kept],
         in_specs=[vmem] * 5 + [anywhere] * 9,
         out_specs=[anywhere] * 9 + [vmem] * 4 + [anywhere] * len(kept),
-        scratch_shapes=[pltpu.VMEM(*entry) for entry in kept] + [
+        scratch_shapes=[pltpu.VMEM(*entry) for entry in kept]
+        + [pltpu.VMEM(grid.shape + s.shape, s.dtype) for s in shards]
+        + [
             pltpu.VMEM((tokens, width), F32),
-            pltpu.VMEM((2,) + grid.shape + (shards[1].shape[0], CHUNK), BF16),
-            pltpu.VMEM((2,) + grid.shape + (shards[8].shape[0], TALL), BF16),
-            pltpu.VMEM(grid.shape + shards[0].shape, BF16),
             pltpu.VMEM((8, width), F32),
             pltpu.VMEM((2, 8, width), F32),
             pltpu.VMEM((tokens, width), F32),
@@ -624,7 +621,7 @@
             pltpu.SemaphoreType.DMA((total,)),
             pltpu.SemaphoreType.DMA((count,)),
             pltpu.SemaphoreType.DMA((count,)),
-            pltpu.SemaphoreType.DMA((2,)),
+            pltpu.SemaphoreType.DMA((len(plan),)),
             pltpu.SemaphoreType.DMA((len(kept),)),
             pltpu.SemaphoreType.DMA((2,)),
             pltpu.SemaphoreType.DMA((2,)),
@@ -638,8 +635,12 @@
 
 STAGES = ("c", "first", "second", "z")
 GAPS = (1, 2, 2, 2)
+ALL = (3, 2, 1, 0)
 SLOTS = (1, 1, 1, 1)
-TICKS = (0, 0, 1, 1, 1, 1, 0, 0, 1, 1, 0, 0, 0, 1, 0, 0, 0, 0, 0, 1, 0, 0, 1, 0, 0, 0, 0, 0, 1, 1, 0, 0, 0, 1, 0, 0, 1, 1, 0, 0, 1, 1, 2, 0, 1, 1, 1, 2)
+TICKS = (
+    0, 0, 1, 4, 3, 1, 3, 0, 0, 0, 1, 0, 0, 0, 0, 0, 1, 0, 0, 1, 0, 0, 0, 0, 1, 0, 0, 0, 1, 4, 3, 0, 4, 4, 0, 3, 0, 1, 0, 0,
+    2, 4, 4, 3, 2, 0, 0, 0,
+)
 
 
 class Piece:
@@ -784,7 +785,7 @@
                 del self.stage[unit]
         self.reading = []
 
-    def tick(self, stages=(3, 2, 1, 0), gaps=GAPS):
+    def tick(self, stages, gaps=GAPS):
         self.now += 1
         self.finish()
         for stage in stages:
@@ -794,14 +795,14 @@
                 self.reading.append((unit, slot, copies))
 
     def point(self):
-        count = TICKS[self.places]
+        kind = TICKS[self.places]
         self.places += 1
-        for _ in range(count):
-            self.tick()
+        for stages in ((), (ALL,), (ALL, ALL), ((0,),), (ALL[:3],))[kind]:
+            self.tick(stages)
 
     def close(self):
         while self.stage:
-            self.tick(gaps=(1, 1, 1, 1))
+            self.tick((0, 1, 2, 3), gaps=(1, 1, 1, 1))
             self.finish()
         for copy, waiting in self.started:
             if waiting:

time: 360 us -> 349 us (0.969)
  Pallas kernels: 336 us -> 326 us
    pallas_call x1, Pallas kernels: 156 us -> 146 us  [forward(): pl.pallas_call(functools.partial(forward_kernel, grid, length, plan, star...]
where the time goes in v5:
time: 349 us; the launch traced here: 344 us
  Pallas kernels  326 us (93%)
  local copies, waits for them, and re-layouts  16.5 us (5%)
    pallas_call x1, Pallas kernels, backward(): pl.pallas_call(functools.partial(backward_kernel, grid, length, units, of...  180 us
    pallas_call x1, Pallas kernels, forward(): pl.pallas_call(functools.partial(forward_kernel, grid, length, plan, star...  146 us
    unnamed x48, local copies, waits for them, and re-layouts  8.84 us

profile of v5, /device:TPU:0, one launch (start us, length us, event | category | flops | bytes accessed | tf_op | source)
XLA Modules:
  0.0 344.2 jit_solution(12823081044529105544)
XLA Ops:
  0.7 0.0 copy-start.11
  0.8 2.1 copy.43
  2.9 0.6 reshape.63
  3.5 0.6 constant_dynamic-slice_fusion.refs_4_
  4.1 0.0 copy-done.9
  4.2 0.1 stack.35
  4.3 0.1 tile.10
  4.4 0.6 fusion.refs_5_
  5.0 146.3 %shard_map.374 = (bf16[2,2,2,4,16,128]{5,4,3,2,1,0:T(8,128)(2,1)}, bf16[2,2,2,4,32,1024]{5,4,3,2,1,0:T(8,128)(2,1)}, bf16[2,2,2,4,32,1024]{5,4,3,2,1,0:T(8,128)(...) custom-call(bf16[512,1024]{1,0:T(8,128)(2,1)} %bitcast.45, ...), custom_call_target="tpu_custom_call" | custom-call | tf_op jit(solution)/shard_map/pallas_call | solution.py:602
  151.3 179.5 %shard_map.375 = (bf16[512,1024]{1,0:T(8,128)(2,1)}, f32[112,1024]{1,0:T(8,128)}, f32[32,1024]{1,0:T(8,128)}, f32[32,3584]{1,0:T(8,128)}, f32[32,1024]{1,0:T(8,1...) custom-call(f32[16,1024]{1,0:T(8,128)} %get-tuple-element.55.refs_0_, ...), custom_call_target="tpu_custom_call" | custom-call | tf_op jit(solution)/shard_map/pallas_call | solution.py:1320
  330.9 1.5 dynamic-slice_bitcast_fusion.2
  332.3 1.3 dynamic-slice_bitcast_fusion
  333.7 1.3 dynamic-slice_bitcast_fusion.1
  335.0 2.3 copy.54
  337.3 1.0 copy.55
  338.3 0.7 copy.56
  339.0 0.7 copy.57
  339.6 0.7 copy.58
  340.3 0.7 copy.59
  340.9 0.7 copy.60
  341.6 0.8 copy.61
  342.4 0.8 copy.62
  343.1 0.0 copy-done.3
  343.1 0.7 copy.63
  (40 shorter events, 0.1 us)
Async XLA Ops:
  0.7 3.5 %copy-start.11 = (bf16[32]{0:T(256)(128)(2,1)S(1)}, bf16[32]{0:T(256)(128)(2,1)}, u32[]{:S(2)}) copy-start(bf16[32]{0:T(256)(128)(2,1)} %param.28) | copy-start | bytes 196
  0.7 3.5 %copy-start.12 = (bf16[32]{0:T(256)(128)(2,1)S(1)}, bf16[32]{0:T(256)(128)(2,1)}, u32[]{:S(2)}) copy-start(bf16[32]{0:T(256)(128)(2,1)} %param.29) | copy-start | bytes 196
  0.7 3.4 copy-start.10
  0.7 3.4 copy-start.9
  0.7 3.5 %copy-start.13 = (bf16[32]{0:T(256)(128)(2,1)S(1)}, bf16[32]{0:T(256)(128)(2,1)}, u32[]{:S(2)}) copy-start(bf16[32]{0:T(256)(128)(2,1)} %param.35) | copy-start | bytes 196
  0.7 3.5 %copy-start.14 = (bf16[32]{0:T(256)(128)(2,1)S(1)}, bf16[32]{0:T(256)(128)(2,1)}, u32[]{:S(2)}) copy-start(bf16[32]{0:T(256)(128)(2,1)} %param.36) | copy-start | bytes 196
  0.7 3.5 %copy-start.15 = (bf16[32]{0:T(256)(128)(2,1)S(1)}, bf16[32]{0:T(256)(128)(2,1)}, u32[]{:S(2)}) copy-start(bf16[32]{0:T(256)(128)(2,1)} %param.37) | copy-start | bytes 196
  0.7 3.5 %copy-start.16 = (bf16[32]{0:T(256)(128)(2,1)S(1)}, bf16[32]{0:T(256)(128)(2,1)}, u32[]{:S(2)}) copy-start(bf16[32]{0:T(256)(128)(2,1)} %param.38) | copy-start | bytes 196
  0.7 3.5 %copy-start.17 = (bf16[32]{0:T(256)(128)(2,1)S(1)}, bf16[32]{0:T(256)(128)(2,1)}, u32[]{:S(2)}) copy-start(bf16[32]{0:T(256)(128)(2,1)} %param.40) | copy-start | bytes 196
  0.8 3.5 %copy-start.18 = (bf16[32]{0:T(256)(128)(2,1)S(1)}, bf16[32]{0:T(256)(128)(2,1)}, u32[]{:S(2)}) copy-start(bf16[32]{0:T(256)(128)(2,1)} %param.41) | copy-start | bytes 196
  330.9 6.5 %copy-start = (bf16[512,1024]{1,0:T(8,128)(2,1)S(1)}, bf16[512,1024]{1,0:T(8,128)(2,1)}, u32[]{:S(2)}) copy-start(bf16[512,1024]{1,0:T(8,128)(2,1)} %get-tuple-element.78) | copy-start | bytes 3145732
  335.0 3.3 copy-start.8
  335.0 4.0 %copy-start.7 = (f32[32,1024]{1,0:T(8,128)S(1)}, f32[32,1024]{1,0:T(8,128)}, u32[]{:S(2)}) copy-start(f32[32,1024]{1,0:T(8,128)} %get-tuple-element.134) | copy-start | bytes 393220
  335.0 4.6 %copy-start.6 = (f32[32,1024]{1,0:T(8,128)S(1)}, f32[32,1024]{1,0:T(8,128)}, u32[]{:S(2)}) copy-start(f32[32,1024]{1,0:T(8,128)} %get-tuple-element.135) | copy-start | bytes 393220
  335.0 5.3 %copy-start.5 = (f32[32,1024]{1,0:T(8,128)S(1)}, f32[32,1024]{1,0:T(8,128)}, u32[]{:S(2)}) copy-start(f32[32,1024]{1,0:T(8,128)} %get-tuple-element.136) | copy-start | bytes 393220
  337.3 3.6 %copy-start.4 = (f32[32,1024]{1,0:T(8,128)S(1)}, f32[32,1024]{1,0:T(8,128)}, u32[]{:S(2)}) copy-start(f32[32,1024]{1,0:T(8,128)} %get-tuple-element.141) | copy-start | bytes 393220
  337.3 4.3 %copy-start.2 = (f32[32,3584]{1,0:T(8,128)S(1)}, f32[32,3584]{1,0:T(8,128)}, u32[]{:S(2)}) copy-start(f32[32,3584]{1,0:T(8,128)} %get-tuple-element.145) | copy-start | bytes 1376260
  337.3 5.0 %copy-start.1 = (f32[112,1024]{1,0:T(8,128)S(1)}, f32[112,1024]{1,0:T(8,128)}, u32[]{:S(2)}) copy-start(f32[112,1024]{1,0:T(8,128)} %get-tuple-element.146) | copy-start | bytes 1376260
  338.3 4.8 %copy-start.3 = (f32[32,1024]{1,0:T(8,128)S(1)}, f32[32,1024]{1,0:T(8,128)}, u32[]{:S(2)}) copy-start(f32[32,1024]{1,0:T(8,128)} %get-tuple-element.147) | copy-start | bytes 393220

commit v6 on v5

--- a/solution.py
+++ b/solution.py
@@ -635,11 +635,11 @@
 
 STAGES = ("c", "first", "second", "z")
 GAPS = (1, 2, 2, 2)
-ALL = (3, 2, 1, 0)
+ALL = (0, 1, 2, 3)
 SLOTS = (1, 1, 1, 1)
 TICKS = (
-    0, 0, 1, 4, 3, 1, 3, 0, 0, 0, 1, 0, 0, 0, 0, 0, 1, 0, 0, 1, 0, 0, 0, 0, 1, 0, 0, 0, 1, 4, 3, 0, 4, 4, 0, 3, 0, 1, 0, 0,
-    2, 4, 4, 3, 2, 0, 0, 0,
+    4, 0, 1, 1, 4, 0, 1, 1, 0, 0, 0, 4, 0, 0, 0, 0, 1, 1, 0, 0, 0, 0, 3, 1, 0, 0, 0, 0, 1, 1, 3, 3, 0, 1, 4, 3, 0, 0, 1, 0,
+    2, 4, 4, 3, 2, 0, 0, 3,
 )
 
 
@@ -797,7 +797,7 @@
     def point(self):
         kind = TICKS[self.places]
         self.places += 1
-        for stages in ((), (ALL,), (ALL, ALL), ((0,),), (ALL[:3],))[kind]:
+        for stages in ((), (ALL,), (ALL, ALL), ((0,),), (tuple(n for n in ALL if n),))[kind]:
             self.tick(stages)
 
     def close(self):
@@ -921,38 +921,38 @@
         scatter.point()
     span = hid.shape[1] // n0
     loading = weight_load(f_r, 0, width, 0)
+    chunks = pieces(hid.shape[1], CHUNK)
     for y in range(n0):
         have("tall")
 
         def key(m, carry, y=y):
-            at = tile(m, 128)
+            at = tile(m, 256)
             window = slice(y * span, (y + 1) * span)
             d_hidden = dot(dc[at, :], tall[...].reshape((span, width)), 1, 1)
             dkey[at, window] = (2.0 * jnp.sqrt(hid[at, window].astype(F32)) * d_hidden).astype(BF16)
             return carry
 
-        lax.fori_loop(0, tokens // 128, key, 0)
+        lax.fori_loop(0, tokens // 256, key, 0)
         if y + 1 < n0:
             fetch("tall", f_v.at[y + 1], tall, 2)
         if y < 2:
             scatter.point()
-    have("m2", "dr")
-    gradient(U["fr"][0], m2.at[1], dr)
-    fetch("mx0", mixed_hbm.at[0], hid.at[:, pl.ds(0, width)], 0)
-    fetch("mx1", mixed_hbm.at[1], hid.at[:, pl.ds(width, width)], 1)
-    fetch("mx2", mixed_hbm.at[2], hid.at[:, pl.ds(2 * width, width)], 2)
-    scatter.point()
-    loading.wait()
-    chunks = pieces(hid.shape[1], CHUNK)
-    loading = weight_load(f_k, *chunks[0], 1)
-
-    def through_recv(m, carry):
-        at = tile(m, 256)
-        db[at, :] = dot(dr[at, :], weight(0, width), 1, 1)
-        return carry
-
-    lax.fori_loop(0, tokens // 256, through_recv, 0)
-    scatter.point()
+        if y == 0:
+            have("m2", "dr")
+            gradient(U["fr"][0], m2.at[1], dr)
+            scatter.point()
+            loading.wait()
+            loading = weight_load(f_k, *chunks[0], 1)
+
+            def through_recv(m, carry):
+                at = tile(m, 256)
+                db[at, :] = dot(dr[at, :], weight(0, width), 1, 1)
+                return carry
+
+            lax.fori_loop(0, tokens // 256, through_recv, 0)
+            scatter.point()
+    for c in range(3):
+        fetch("mx%d" % c, mixed_hbm.at[c], hid.at[:, pl.ds(c * width, width)], c)
     for number, unit in enumerate(U["fk"]):
         gradient(unit, m2.at[0], dkey)
         scatter.point()
@@ -1032,25 +1032,29 @@
     have("mid")
     norm(mid, 10, 11)
     scatter.point()
-    for q in range(segments):
-
-        def blend_two(i, carry, q=q):
+
+    def blend_two(q, first, last, carry):
+        def run(i, carry):
             at = tile(q * (length // step) + i, step)
             current = nrm[at, :]
             row = lax.broadcasted_iota(jnp.int32, (step, 1), 0)
             difference = current - jnp.where(row == 0, carry, pltpu.roll(current, 1, 0))
-            first, second = dn[at, :], db[at, :]
-            acc[12] += fold_rows(difference * first)
-            acc[13] += fold_rows(difference * second)
+            here, before = dn[at, :], db[at, :]
+            acc[12] += fold_rows(difference * here)
+            acc[13] += fold_rows(difference * before)
             a, b = table_ref[12:13, :], table_ref[13:14, :]
-            dn[at, :] = first * a + second * b
-            db[at, :] = first * (1.0 - a) + second * (1.0 - b)
+            dn[at, :] = here * a + before * b
+            db[at, :] = here * (1.0 - a) + before * (1.0 - b)
             return current[step - 1 : step, :]
 
-        lax.fori_loop(0, length // step, blend_two, prev_ref[1, q : q + 1, :])
-        scatter.point()
+        return lax.fori_loop(first, last, run, carry)
+
+    above = [blend_two(q, 0, 1, prev_ref[1, q : q + 1, :]) for q in range(segments)]
     moving = swap_edges(0)
     scatter.point()
+    for q in range(segments):
+        blend_two(q, 1, length // step, above[q])
+        scatter.point()
     have("up")
     moving.wait()
 
@@ -1224,20 +1228,17 @@
         window = slice(y * span, (y + 1) * span)
 
         def through_mix(m, carry, y=y, window=window):
-            at = tile(m, 128)
+            at = tile(m, length)
             current = nrm[at, window]
-            above = nrm[pl.ds(pl.multiple_of(jnp.maximum(m * 128 - 8, 0), 8), 8), window][7:8, :]
-            segment = lax.div(m, length // 128)
             given = prev_ref[0, 0:1, window]
             for q in range(1, segments):
-                given = jnp.where(segment == q, prev_ref[0, q : q + 1, window], given)
-            carried = jnp.where(lax.rem(m, length // 128) == 0, given, above)
-            row = lax.broadcasted_iota(jnp.int32, (128, 1), 0)
-            difference = current - jnp.where(row == 0, carried, pltpu.roll(current, 1, 0))
+                given = jnp.where(m == q, prev_ref[0, q : q + 1, window], given)
+            row = lax.broadcasted_iota(jnp.int32, (length, 1), 0)
+            difference = current - jnp.where(row == 0, given, pltpu.roll(current, 1, 0))
             here, before = None, None
             for c in range(4):
                 value = dot(grads[c][at, :], wide[c // n0, c % n0].reshape((span, width)), 1, 1)
-                acc[2 + c, :, window] += jnp.sum((difference * value).reshape((16, 8, span)), axis=0)
+                acc[2 + c, :, window] += jnp.sum((difference * value).reshape((length // 8, 8, span)), axis=0)
                 blend = table_ref[2 + c : 3 + c, window]
                 here = blend * value if c == 0 else here + blend * value
                 before = (1.0 - blend) * value if c == 0 else before + (1.0 - blend) * value
@@ -1245,7 +1246,7 @@
             db[at, window] = before
             return carry
 
-        lax.fori_loop(0, tokens // 128, through_mix, 0)
+        lax.fori_loop(0, segments, through_mix, 0)
         if y + 1 < n0:
             loading = load_rows(y + 1)
         if y < 2:

time: 349 us -> 337 us (0.966)
  Pallas kernels: 326 us -> 313 us
    pallas_call x1, Pallas kernels: 180 us -> 167 us  [backward(): pl.pallas_call(functools.partial(backward_kernel, grid, length, units, of...]
where the time goes in v6:
time: 337 us; the launch traced here: 332 us
  Pallas kernels  313 us (93%)
  local copies, waits for them, and re-layouts  16.5 us (5%)
    pallas_call x1, Pallas kernels, backward(): pl.pallas_call(functools.partial(backward_kernel, grid, length, units, of...  167 us
    pallas_call x1, Pallas kernels, forward(): pl.pallas_call(functools.partial(forward_kernel, grid, length, plan, star...  146 us
    unnamed x48, local copies, waits for them, and re-layouts  8.84 us

profile of v6, /device:TPU:0, one launch (start us, length us, event | category | flops | bytes accessed | tf_op | source)
XLA Modules:
  0.0 331.6 jit_solution(3476710921374083323)
XLA Ops:
  0.7 0.0 copy-start.11
  0.7 0.0 copy-start.12
  0.7 0.0 copy-start.10
  0.8 2.1 copy.43
  2.9 0.6 reshape.63
  3.5 0.6 constant_dynamic-slice_fusion.refs_4_
  4.2 0.1 stack.35
  4.3 0.1 tile.10
  4.4 0.6 fusion.refs_5_
  5.0 146.3 %shard_map.374 = (bf16[2,2,2,4,16,128]{5,4,3,2,1,0:T(8,128)(2,1)}, bf16[2,2,2,4,32,1024]{5,4,3,2,1,0:T(8,128)(2,1)}, bf16[2,2,2,4,32,1024]{5,4,3,2,1,0:T(8,128)(...) custom-call(bf16[512,1024]{1,0:T(8,128)(2,1)} %bitcast.45, ...), custom_call_target="tpu_custom_call" | custom-call | tf_op jit(solution)/shard_map/pallas_call | solution.py:602
  151.3 167.0 %shard_map.375 = (bf16[512,1024]{1,0:T(8,128)(2,1)}, f32[112,1024]{1,0:T(8,128)}, f32[32,1024]{1,0:T(8,128)}, f32[32,3584]{1,0:T(8,128)}, f32[32,1024]{1,0:T(8,1...) custom-call(f32[16,1024]{1,0:T(8,128)} %get-tuple-element.55.refs_0_, ...), custom_call_target="tpu_custom_call" | custom-call | tf_op jit(solution)/shard_map/pallas_call | solution.py:1321
  318.3 1.5 dynamic-slice_bitcast_fusion.2
  319.8 1.3 dynamic-slice_bitcast_fusion
  321.1 1.3 dynamic-slice_bitcast_fusion.1
  322.4 2.3 copy.54
  324.7 1.0 copy.55
  325.7 0.7 copy.56
  326.4 0.7 copy.57
  327.0 0.7 copy.58
  327.7 0.7 copy.59
  328.4 0.7 copy.60
  329.0 0.8 copy.61
  329.8 0.8 copy.62
  330.6 0.7 copy.63
  (40 shorter events, 0.1 us)
Async XLA Ops:
  0.7 3.5 %copy-start.11 = (bf16[32]{0:T(256)(128)(2,1)S(1)}, bf16[32]{0:T(256)(128)(2,1)}, u32[]{:S(2)}) copy-start(bf16[32]{0:T(256)(128)(2,1)} %param.28) | copy-start | bytes 196
  0.7 3.5 %copy-start.12 = (bf16[32]{0:T(256)(128)(2,1)S(1)}, bf16[32]{0:T(256)(128)(2,1)}, u32[]{:S(2)}) copy-start(bf16[32]{0:T(256)(128)(2,1)} %param.29) | copy-start | bytes 196
  0.7 3.4 %copy-start.10 = (bf16[32,2]{0,1:T(2,128)(2,1)S(1)}, bf16[32,2]{0,1:T(2,128)(2,1)}, u32[]{:S(2)}) copy-start(bf16[32,2]{0,1:T(2,128)(2,1)} %param.42) | copy-start | bytes 388
  0.7 3.4 %copy-start.9 = (bf16[32,4]{0,1:T(4,128)(2,1)S(1)}, bf16[32,4]{0,1:T(4,128)(2,1)}, u32[]{:S(2)}) copy-start(bf16[32,4]{0,1:T(4,128)(2,1)} %param.30) | copy-start | bytes 772
  0.7 3.5 %copy-start.13 = (bf16[32]{0:T(256)(128)(2,1)S(1)}, bf16[32]{0:T(256)(128)(2,1)}, u32[]{:S(2)}) copy-start(bf16[32]{0:T(256)(128)(2,1)} %param.35) | copy-start | bytes 196
  0.7 3.5 %copy-start.14 = (bf16[32]{0:T(256)(128)(2,1)S(1)}, bf16[32]{0:T(256)(128)(2,1)}, u32[]{:S(2)}) copy-start(bf16[32]{0:T(256)(128)(2,1)} %param.36) | copy-start | bytes 196
  0.7 3.5 %copy-start.15 = (bf16[32]{0:T(256)(128)(2,1)S(1)}, bf16[32]{0:T(256)(128)(2,1)}, u32[]{:S(2)}) copy-start(bf16[32]{0:T(256)(128)(2,1)} %param.37) | copy-start | bytes 196
  0.7 3.5 %copy-start.16 = (bf16[32]{0:T(256)(128)(2,1)S(1)}, bf16[32]{0:T(256)(128)(2,1)}, u32[]{:S(2)}) copy-start(bf16[32]{0:T(256)(128)(2,1)} %param.38) | copy-start | bytes 196
  0.7 3.5 %copy-start.17 = (bf16[32]{0:T(256)(128)(2,1)S(1)}, bf16[32]{0:T(256)(128)(2,1)}, u32[]{:S(2)}) copy-start(bf16[32]{0:T(256)(128)(2,1)} %param.40) | copy-start | bytes 196
  0.8 3.5 %copy-start.18 = (bf16[32]{0:T(256)(128)(2,1)S(1)}, bf16[32]{0:T(256)(128)(2,1)}, u32[]{:S(2)}) copy-start(bf16[32]{0:T(256)(128)(2,1)} %param.41) | copy-start | bytes 196
  318.3 6.5 %copy-start = (bf16[512,1024]{1,0:T(8,128)(2,1)S(1)}, bf16[512,1024]{1,0:T(8,128)(2,1)}, u32[]{:S(2)}) copy-start(bf16[512,1024]{1,0:T(8,128)(2,1)} %get-tuple-element.78) | copy-start | bytes 3145732
  322.4 3.3 %copy-start.8 = (f32[32,1024]{1,0:T(8,128)S(1)}, f32[32,1024]{1,0:T(8,128)}, u32[]{:S(2)}) copy-start(f32[32,1024]{1,0:T(8,128)} %get-tuple-element.133) | copy-start | bytes 393220
  322.4 4.0 %copy-start.7 = (f32[32,1024]{1,0:T(8,128)S(1)}, f32[32,1024]{1,0:T(8,128)}, u32[]{:S(2)}) copy-start(f32[32,1024]{1,0:T(8,128)} %get-tuple-element.134) | copy-start | bytes 393220
  322.4 4.6 %copy-start.6 = (f32[32,1024]{1,0:T(8,128)S(1)}, f32[32,1024]{1,0:T(8,128)}, u32[]{:S(2)}) copy-start(f32[32,1024]{1,0:T(8,128)} %get-tuple-element.135) | copy-start | bytes 393220
  322.4 5.3 %copy-start.5 = (f32[32,1024]{1,0:T(8,128)S(1)}, f32[32,1024]{1,0:T(8,128)}, u32[]{:S(2)}) copy-start(f32[32,1024]{1,0:T(8,128)} %get-tuple-element.136) | copy-start | bytes 393220
  324.7 3.6 %copy-start.4 = (f32[32,1024]{1,0:T(8,128)S(1)}, f32[32,1024]{1,0:T(8,128)}, u32[]{:S(2)}) copy-start(f32[32,1024]{1,0:T(8,128)} %get-tuple-element.141) | copy-start | bytes 393220
  324.7 4.3 %copy-start.2 = (f32[32,3584]{1,0:T(8,128)S(1)}, f32[32,3584]{1,0:T(8,128)}, u32[]{:S(2)}) copy-start(f32[32,3584]{1,0:T(8,128)} %get-tuple-element.145) | copy-start | bytes 1376260
  324.7 5.0 %copy-start.1 = (f32[112,1024]{1,0:T(8,128)S(1)}, f32[112,1024]{1,0:T(8,128)}, u32[]{:S(2)}) copy-start(f32[112,1024]{1,0:T(8,128)} %get-tuple-element.146) | copy-start | bytes 1376260
  325.7 4.8 %copy-start.3 = (f32[32,1024]{1,0:T(8,128)S(1)}, f32[32,1024]{1,0:T(8,128)}, u32[]{:S(2)}) copy-start(f32[32,1024]{1,0:T(8,128)} %get-tuple-element.147) | copy-start | bytes 393220

commit v7 on v6

--- a/solution.py
+++ b/solution.py
@@ -892,8 +892,8 @@
     def gradient(unit, left_ref, right_ref):
         parts = units[unit]
         targets = [scatter.open(unit, number) for number in range(len(parts))]
-        span, narrow = left_ref.shape[1] // n0, parts[0].columns < 256
-        for batch in [list(range(len(parts)))] if narrow else [[number] for number in range(len(parts))]:
+        span = left_ref.shape[1] // n0
+        for batch in [list(range(len(parts)))]:
             first = parts[batch[0]]
             width_all = sum(parts[number].columns for number in batch)
 

time: 337 us -> 334 us (level)
  no operation moved by 1% of the time
where the time goes in v7:
time: 334 us; the launch traced here: 329 us
  Pallas kernels  311 us (93%)
  local copies, waits for them, and re-layouts  16.5 us (5%)
    pallas_call x1, Pallas kernels, backward(): pl.pallas_call(functools.partial(backward_kernel, grid, length, units, of...  164 us
    pallas_call x1, Pallas kernels, forward(): pl.pallas_call(functools.partial(forward_kernel, grid, length, plan, star...  146 us
    unnamed x48, local copies, waits for them, and re-layouts  8.84 us

profile of v7, /device:TPU:0, one launch (start us, length us, event | category | flops | bytes accessed | tf_op | source)
XLA Modules:
  0.0 329.1 jit_solution(14836286554486350447)
XLA Ops:
  0.7 0.0 copy-start.11
  0.7 0.0 copy-start.12
  0.7 0.0 copy-start.10
  0.8 2.1 copy.43
  2.9 0.6 reshape.63
  3.5 0.6 constant_dynamic-slice_fusion.refs_4_
  4.2 0.1 stack.35
  4.3 0.1 tile.10
  4.4 0.6 fusion.refs_5_
  5.0 146.3 %shard_map.374 = (bf16[2,2,2,4,16,128]{5,4,3,2,1,0:T(8,128)(2,1)}, bf16[2,2,2,4,32,1024]{5,4,3,2,1,0:T(8,128)(2,1)}, bf16[2,2,2,4,32,1024]{5,4,3,2,1,0:T(8,128)(...) custom-call(bf16[512,1024]{1,0:T(8,128)(2,1)} %bitcast.45, ...), custom_call_target="tpu_custom_call" | custom-call | tf_op jit(solution)/shard_map/pallas_call | solution.py:602
  151.3 164.4 %shard_map.375 = (bf16[512,1024]{1,0:T(8,128)(2,1)}, f32[112,1024]{1,0:T(8,128)}, f32[32,1024]{1,0:T(8,128)}, f32[32,3584]{1,0:T(8,128)}, f32[32,1024]{1,0:T(8,1...) custom-call(f32[16,1024]{1,0:T(8,128)} %get-tuple-element.55.refs_0_, ...), custom_call_target="tpu_custom_call" | custom-call | tf_op jit(solution)/shard_map/pallas_call | solution.py:1321
  315.7 1.5 dynamic-slice_bitcast_fusion.2
  317.2 1.3 dynamic-slice_bitcast_fusion
  318.5 1.3 dynamic-slice_bitcast_fusion.1
  319.9 2.3 copy.54
  322.2 1.0 copy.55
  323.2 0.7 copy.56
  323.8 0.7 copy.57
  324.5 0.7 copy.58
  325.2 0.7 copy.59
  325.8 0.7 copy.60
  326.5 0.8 copy.61
  327.2 0.8 copy.62
  328.0 0.7 copy.63
  (40 shorter events, 0.1 us)
Async XLA Ops:
  0.7 3.5 %copy-start.11 = (bf16[32]{0:T(256)(128)(2,1)S(1)}, bf16[32]{0:T(256)(128)(2,1)}, u32[]{:S(2)}) copy-start(bf16[32]{0:T(256)(128)(2,1)} %param.28) | copy-start | bytes 196
  0.7 3.5 %copy-start.12 = (bf16[32]{0:T(256)(128)(2,1)S(1)}, bf16[32]{0:T(256)(128)(2,1)}, u32[]{:S(2)}) copy-start(bf16[32]{0:T(256)(128)(2,1)} %param.29) | copy-start | bytes 196
  0.7 3.4 %copy-start.10 = (bf16[32,2]{0,1:T(2,128)(2,1)S(1)}, bf16[32,2]{0,1:T(2,128)(2,1)}, u32[]{:S(2)}) copy-start(bf16[32,2]{0,1:T(2,128)(2,1)} %param.42) | copy-start | bytes 388
  0.7 3.4 %copy-start.9 = (bf16[32,4]{0,1:T(4,128)(2,1)S(1)}, bf16[32,4]{0,1:T(4,128)(2,1)}, u32[]{:S(2)}) copy-start(bf16[32,4]{0,1:T(4,128)(2,1)} %param.30) | copy-start | bytes 772
  0.7 3.5 %copy-start.13 = (bf16[32]{0:T(256)(128)(2,1)S(1)}, bf16[32]{0:T(256)(128)(2,1)}, u32[]{:S(2)}) copy-start(bf16[32]{0:T(256)(128)(2,1)} %param.35) | copy-start | bytes 196
  0.7 3.5 %copy-start.14 = (bf16[32]{0:T(256)(128)(2,1)S(1)}, bf16[32]{0:T(256)(128)(2,1)}, u32[]{:S(2)}) copy-start(bf16[32]{0:T(256)(128)(2,1)} %param.36) | copy-start | bytes 196
  0.7 3.5 %copy-start.15 = (bf16[32]{0:T(256)(128)(2,1)S(1)}, bf16[32]{0:T(256)(128)(2,1)}, u32[]{:S(2)}) copy-start(bf16[32]{0:T(256)(128)(2,1)} %param.37) | copy-start | bytes 196
  0.7 3.5 %copy-start.16 = (bf16[32]{0:T(256)(128)(2,1)S(1)}, bf16[32]{0:T(256)(128)(2,1)}, u32[]{:S(2)}) copy-start(bf16[32]{0:T(256)(128)(2,1)} %param.38) | copy-start | bytes 196
  0.7 3.5 %copy-start.17 = (bf16[32]{0:T(256)(128)(2,1)S(1)}, bf16[32]{0:T(256)(128)(2,1)}, u32[]{:S(2)}) copy-start(bf16[32]{0:T(256)(128)(2,1)} %param.40) | copy-start | bytes 196
  0.8 3.5 %copy-start.18 = (bf16[32]{0:T(256)(128)(2,1)S(1)}, bf16[32]{0:T(256)(128)(2,1)}, u32[]{:S(2)}) copy-start(bf16[32]{0:T(256)(128)(2,1)} %param.41) | copy-start | bytes 196
  315.7 6.5 %copy-start = (bf16[512,1024]{1,0:T(8,128)(2,1)S(1)}, bf16[512,1024]{1,0:T(8,128)(2,1)}, u32[]{:S(2)}) copy-start(bf16[512,1024]{1,0:T(8,128)(2,1)} %get-tuple-element.78) | copy-start | bytes 3145732
  319.9 3.3 %copy-start.8 = (f32[32,1024]{1,0:T(8,128)S(1)}, f32[32,1024]{1,0:T(8,128)}, u32[]{:S(2)}) copy-start(f32[32,1024]{1,0:T(8,128)} %get-tuple-element.133) | copy-start | bytes 393220
  319.9 4.0 %copy-start.7 = (f32[32,1024]{1,0:T(8,128)S(1)}, f32[32,1024]{1,0:T(8,128)}, u32[]{:S(2)}) copy-start(f32[32,1024]{1,0:T(8,128)} %get-tuple-element.134) | copy-start | bytes 393220
  319.9 4.6 %copy-start.6 = (f32[32,1024]{1,0:T(8,128)S(1)}, f32[32,1024]{1,0:T(8,128)}, u32[]{:S(2)}) copy-start(f32[32,1024]{1,0:T(8,128)} %get-tuple-element.135) | copy-start | bytes 393220
  319.9 5.3 %copy-start.5 = (f32[32,1024]{1,0:T(8,128)S(1)}, f32[32,1024]{1,0:T(8,128)}, u32[]{:S(2)}) copy-start(f32[32,1024]{1,0:T(8,128)} %get-tuple-element.136) | copy-start | bytes 393220
  322.2 3.6 %copy-start.4 = (f32[32,1024]{1,0:T(8,128)S(1)}, f32[32,1024]{1,0:T(8,128)}, u32[]{:S(2)}) copy-start(f32[32,1024]{1,0:T(8,128)} %get-tuple-element.141) | copy-start | bytes 393220
  322.2 4.3 %copy-start.2 = (f32[32,3584]{1,0:T(8,128)S(1)}, f32[32,3584]{1,0:T(8,128)}, u32[]{:S(2)}) copy-start(f32[32,3584]{1,0:T(8,128)} %get-tuple-element.145) | copy-start | bytes 1376260
  322.2 5.0 %copy-start.1 = (f32[112,1024]{1,0:T(8,128)S(1)}, f32[112,1024]{1,0:T(8,128)}, u32[]{:S(2)}) copy-start(f32[112,1024]{1,0:T(8,128)} %get-tuple-element.146) | copy-start | bytes 1376260
  323.2 4.8 %copy-start.3 = (f32[32,1024]{1,0:T(8,128)S(1)}, f32[32,1024]{1,0:T(8,128)}, u32[]{:S(2)}) copy-start(f32[32,1024]{1,0:T(8,128)} %get-tuple-element.147) | copy-start | bytes 393220
